TPU v7x, 32 devices: a whole 2x2x4 slice. The times are simulated.
32 devices in a mesh: lat: 4 (over y, x), lon: 8 (over z, core).
Axes of the slice: x: 2, y: 2, z: 4, core: 2. Of those that a mesh axis runs over, the one named last changes fastest.
Arguments:
- q_state: bfloat16 [128, 256, 1024], P(('lat', 'lon')), may hold values from -5 to 5
- scales: float32 [128, 256], P(('lat', 'lon')), may hold values from 0.1 to 2
- land_mask: int32 [256, 1024], P('lat', 'lon'), may hold values 0 or 1
- stem_weight: bfloat16 [128, 192], replicated, may hold values from -0.5 to 0.5
- stem_bias: float32 [192], replicated, may hold values from -3 to 3
- dw_weight: float32 [2, 192, 7, 7], replicated, may hold values from -0.875 to 0.875
- dw_bias: float32 [2, 192], replicated, may hold values from -3 to 3
- ln_gain: float32 [2, 192], replicated, may hold values from 0.5 to 2
- ln_bias: float32 [2, 192], replicated, may hold values from -3 to 3
- w_in: bfloat16 [2, 192, 768], replicated, may hold values from -0.4375 to 0.4375
- b_in: float32 [2, 768], replicated, may hold values from -3 to 3
- w_out: bfloat16 [2, 768, 192], replicated, may hold values from -0.21875 to 0.21875
- b_out: float32 [2, 192], replicated, may hold values from -3 to 3
- layer_scale: float32 [2, 192], replicated, may hold values from 0.3 to 1
- head_weight: bfloat16 [192, 128], replicated, may hold values from -0.4375 to 0.4375
Outputs:
- tendency: float32 [128, 256, 1024], P(None, 'lat', 'lon')
Inputs may be any that keep to these rules, and one draw needn't show every extreme that they name: `land_mask`: 1 marks an ocean point, 0 a land point.
All inputs are finite; a program needn't handle non-finite values. No bound on the sum of `land_mask` on one device may be relied on, other than what follows from the above.
Results may differ from a plain program's by a relative error of at most 0.0057.
Values may be sent and summed in bfloat16 or wider, within the bound.
No kernel may reach another device: no remote copies, remote signals or barrier semaphores. Data moves between devices by JAX's collectives and lax.ppermute only.
A program may use at most 192 MiB of HBM per device.

v0:
```python
import jax
import jax.numpy as jnp
from jax import lax
from jax.sharding import PartitionSpec as P

ln_eps = 1e-06


def with_halo(cells, sides, width, closed):
    for axis, dim in sides:
        count = lax.axis_size(axis)
        ends = count if closed else count - 1
        head = lax.slice_in_dim(cells, 0, width, axis=dim)
        tail = lax.slice_in_dim(cells, cells.shape[dim] - width, cells.shape[dim], axis=dim)
        cells = jnp.concatenate(
            [
                lax.ppermute(tail, axis, [(i, (i + 1) % count) for i in range(ends)]),
                cells,
                lax.ppermute(head, axis, [((i + 1) % count, i) for i in range(ends)]),
            ],
            axis=dim,
        )
    return cells


def depthwise(padded, kernel, shift_bias, row_count, col_count):
    summed = (
        jnp.zeros((padded.shape[0], row_count, col_count), jnp.float32) + shift_bias[:, None, None]
    )
    for i in range(7):
        for j in range(7):
            summed = (
                summed
                + padded[:, i : i + row_count, j : j + col_count] * kernel[:, i, j][:, None, None]
            )
    return summed


def mix_cells(
    convolved,
    residual_in,
    ocean,
    gain_one,
    lnbias_one,
    expand,
    expand_bias,
    contract,
    contract_bias,
    branch_scale,
):
    average = jnp.mean(convolved, axis=0, keepdims=True)
    centered = convolved - average
    variance = jnp.mean(centered * centered, axis=0, keepdims=True)
    normed = (
        centered * lax.rsqrt(variance + ln_eps) * gain_one[:, None] + lnbias_one[:, None]
    ).astype(jnp.bfloat16)
    hidden = jax.nn.gelu(
        jnp.dot(expand.T, normed, preferred_element_type=jnp.float32) + expand_bias[:, None],
        approximate=False,
    ).astype(jnp.bfloat16)
    projected = (
        jnp.dot(contract.T, hidden, preferred_element_type=jnp.float32) + contract_bias[:, None]
    )
    updated = (residual_in.astype(jnp.float32) + branch_scale[:, None] * projected) * ocean[None, :]
    return updated.astype(jnp.bfloat16)


def mix_region(convolved, residual_in, ocean, params):
    channels, row_count, col_count = convolved.shape
    cells = row_count * col_count
    flat_conv = convolved.reshape(channels, cells)
    flat_resid = residual_in.reshape(channels, cells)
    flat_ocean = ocean.reshape(cells)
    part_size = max((d for d in range(1, min(cells, 4096) + 1) if cells % d == 0))
    turns = cells // part_size

    def one_part(turn_index, result):
        offset = turn_index * part_size
        conv_part = lax.dynamic_slice_in_dim(flat_conv, offset, part_size, 1)
        resid_part = lax.dynamic_slice_in_dim(flat_resid, offset, part_size, 1)
        ocean_part = lax.dynamic_slice_in_dim(flat_ocean, offset, part_size, 0)
        mixed = mix_cells(conv_part, resid_part, ocean_part, *params)
        return lax.dynamic_update_slice_in_dim(result, mixed, offset, 1)

    result = lax.fori_loop(0, turns, one_part, jnp.zeros((channels, cells), jnp.bfloat16))
    return result.reshape(channels, row_count, col_count)


def body(
    q_state,
    scales,
    land_mask,
    stem_weight,
    stem_bias,
    dw_weight,
    dw_bias,
    ln_gain,
    ln_bias,
    w_in,
    b_in,
    w_out,
    b_out,
    layer_scale,
    head_weight,
):
    n_lat = lax.axis_size("lat")
    n_lon = lax.axis_size("lon")
    per_device = q_state.shape[0]
    lat_rows = land_mask.shape[0]
    lon_cols = land_mask.shape[1]
    dequant = (q_state * scales[:, :, None]).astype(jnp.bfloat16)
    tiles = dequant.reshape(per_device, n_lat, lat_rows, n_lon, lon_cols).transpose(1, 3, 0, 2, 4)
    tiles = tiles.reshape(n_lat * n_lon, per_device, lat_rows, lon_cols)
    gathered = lax.all_to_all(tiles, ("lat", "lon"), split_axis=0, concat_axis=1, tiled=True)
    state_tile = gathered.reshape(n_lat * n_lon * per_device, lat_rows, lon_cols)
    channels_in = state_tile.shape[0]
    ocean = land_mask.astype(jnp.float32)
    stem_out = (
        jnp.dot(
            stem_weight.T, state_tile.reshape(channels_in, -1), preferred_element_type=jnp.float32
        )
        + stem_bias[:, None]
    )
    features = (stem_out.reshape(-1, lat_rows, lon_cols) * ocean[None]).astype(jnp.bfloat16)
    layer_count = dw_weight.shape[0]
    for layer_index in range(layer_count):
        padded = with_halo(features, (("lat", 1),), 3, False)
        padded = with_halo(padded, (("lon", 2),), 3, True)
        convolved = depthwise(
            padded, dw_weight[layer_index], dw_bias[layer_index], lat_rows, lon_cols
        )
        features = mix_region(
            convolved,
            features,
            ocean,
            (
                ln_gain[layer_index],
                ln_bias[layer_index],
                w_in[layer_index],
                b_in[layer_index],
                w_out[layer_index],
                b_out[layer_index],
                layer_scale[layer_index],
            ),
        )
    tendency = jnp.dot(
        head_weight.T, features.reshape(features.shape[0], -1), preferred_element_type=jnp.float32
    )
    return tendency.reshape(-1, lat_rows, lon_cols)


def solution(mesh):
    placed = (
        P(("lat", "lon"), None, None),
        P(("lat", "lon"), None),
        P("lat", "lon"),
        P(),
        P(),
        P(),
        P(),
        P(),
        P(),
        P(),
        P(),
        P(),
        P(),
        P(),
        P(),
    )
    return jax.shard_map(
        body, mesh=mesh, in_specs=placed, out_specs=P(None, "lat", "lon"), check_vma=False
    )
```

profile of v0, /device:TPU:0, one launch (start us, length us, event | category | flops | bytes accessed | tf_op | source)
XLA Modules:
  0.0 520.4 jit_solution(6855256512787086528)
XLA Ops:
  4.6 7.3 %all-to-all-start = ((bf16[32,4,64,128]{3,2,1,0:T(8,128)(2,1)}), bf16[32,4,64,128]{3,2,1,0:T(8,128)(2,1)S(1)}, u32[]{:S(2)}, u32[]{:S(2)}) async-start(bf16[32,4,64,128]{3,2,1,0:T(8,128)(2,1)} %bitcast.15), calls=%async_computation | async-start | bytes 4194304 | tf_op jit(solution)/shard_map/all_to_all | solution.py:114
  18.0 44.0 %all-to-all-done = bf16[32,4,64,128]{3,2,1,0:T(8,128)(2,1)S(1)} async-done(((bf16[32,4,64,128]{3,2,1,0:T(8,128)(2,1)}), bf16[32,4,64,128]{3,2,1,0:T(8,128)(2,1)S(1)}, u32[]{:S(2)}, u32[]{:S(2)}) %all-to-all-start) | async-done | bytes 2097184 | tf_op jit(solution)/shard_map/all_to_all | solution.py:114
  62.0 4.3 fusion.128
  66.3 3.8 copy.57
  70.1 9.0 %copy.40 = f32[192,64,128]{0,1,2:T(8,128)} copy(f32[192,64,128]{2,1,0:T(8,128)} %bitcast.359) | data formatting | bytes 12582912 | tf_op jit(solution)/shard_map/reshape | solution.py:124
  79.1 4.1 multiply_convert_fusion
  87.0 4.6 collective-permute-done
  91.6 7.9 %collective-permute-done.1 = bf16[192,3,128]{0,1,2:T(4,128)(2,1)S(1)} collective-permute-done((bf16[192,3,128]{0,1,2:T(4,128)(2,1)S(1)}, bf16[192,3,128]{0,1,2:T(4,128)(2,1)S(1)}, u32[]{:S(2)}, u32[]{:S(2)}) %collective-permute-start.1) | collective-permute-done | bytes 147488 | tf_op jit(solution)/shard_map/ppermute | solution.py:19
  99.7 3.8 collective-permute-start.3
  106.1 10.7 %maximum_maximum_fusion.1 = (bf16[192,70,131]{0,1,2:T(8,128)(2,1)S(1)}, bf16[192,70,131]{0,1,2:T(8,128)(2,1)S(1)}) fusion(bf16[192,3,128]{0,1,2:T(4,128)(2,1)S(1)} %collective-permute-done.1, bf16[192,64,128]{0,1,2:T(8,128)(2,1)} %copy-done.3, bf16[192,3,128]{0,1,2:T(4,128)(2,1)S(1)} %collective-permute-done, ...), kind=kLoop, calls=%fused_computation.156 | loop fusion | flops 28170240 | bytes 10644480 | tf_op jit(solution)/shard_map/concatenate | solution.py:15
  116.9 65.6 %multiply_add_fusion = f32[192,64,128]{0,1,2:T(8,128)} fusion(bf16[192,64,128]{0,1,2:T(8,128)(2,1)S(1)} %copy-done.4, bf16[192,3,128]{0,1,2:T(4,128)(2,1)S(1)} %collective-permute-done.1, bf16[192,3,128]{0,1,2:T(4,128)(2,1)S(1)} %collective-permute-done, bf16[192,70,131]{0,1,2:T(8,128)(2,1)S(1)} %get-tuple-element.454, ...), kind=kLoop, calls=%fused_computation.143 | loop fusion | flops 259522560 | bytes 141891072 | tf_op jit(solution)/shard_map/add | solution.py:33
  182.6 8.3 %copy.42 = f32[192,64,128]{2,1,0:T(8,128)} copy(f32[192,64,128]{0,1,2:T(8,128)} %multiply_add_fusion) | data formatting | bytes 12582912 | tf_op jit(solution)/shard_map/add | solution.py:33
  190.9 10.9 %copy.72 = f32[24,8,64,128]{3,1,2,0:T(8,128)} copy(f32[24,8,64,128]{3,2,1,0:T(8,128)} %bitcast.360) | data formatting | bytes 12582912
  202.2 85.0 %while.26 = (s32[]{:T(128)}, bf16[192,8192]{1,0:T(8,128)(2,1)S(1)}, bf16[192,8192]{1,0:T(8,128)(2,1)}, f32[1,192]{1,0:T(1,128)S(1)}, f32[192,8192]{1,0:T(8,128)}...) while((s32[]{:T(128)}, bf16[192,8192]{1,0:T(8,128)(2,1)S(1)}, ...), condition=%wide.region_3.0_spmd, body=%wide.region_0.0_spmd.sunk | while | flops 2635337728 | bytes 13483227 | solution.py:85
  218.1 32.1 %fusion.171 = bf16[192,8192]{1,0:T(8,128)(2,1)S(1)} fusion(bf16[192,8192]{1,0:T(8,128)(2,1)S(1)} %get-tuple-element.755, s32[]{:T(128)S(6)} %select_n.22, bf16[768,192]{1,0:T(8,128)(2,1)} %get-tuple-element.780, bf16[192,768]{1,0:T(8,128)(2,1)} %get-tuple-element.778, f32[768]{0:T(1024)S(1)} %reduce.4, f32[192,8192]{1,0:T(8,128)} %get-tuple-element.775, ...), kind=kOutput, calls=%fused_computation.30.clone.1 | convolution fusion | flops 2632187904 | bytes 7037952 | tf_op jit(solution)/shard_map/while/body/eval_jaxpr/dot_general | solution.py:62
  254.6 32.1 %fusion.171 = bf16[192,8192]{1,0:T(8,128)(2,1)S(1)} fusion(bf16[192,8192]{1,0:T(8,128)(2,1)S(1)} %get-tuple-element.755, s32[]{:T(128)S(6)} %select_n.22, bf16[768,192]{1,0:T(8,128)(2,1)} %get-tuple-element.780, bf16[192,768]{1,0:T(8,128)(2,1)} %get-tuple-element.778, f32[768]{0:T(1024)S(1)} %reduce.4, f32[192,8192]{1,0:T(8,128)} %get-tuple-element.775, ...), kind=kOutput, calls=%fused_computation.30.clone.1 | convolution fusion | flops 2632187904 | bytes 7037952 | tf_op jit(solution)/shard_map/while/body/eval_jaxpr/dot_general | solution.py:62
  289.5 4.6 collective-permute-start.4
  294.1 2.4 constant_dynamic-update-slice_fusion.1
  299.7 4.5 fusion.138
  304.2 4.6 copy.44
  308.9 4.5 copy.47
  313.4 3.6 collective-permute-start.7
  317.7 3.2 copy.45
  321.0 3.4 copy.48
  324.8 12.4 %maximum_maximum_fusion = (bf16[192,70,131]{2,1,0:T(8,128)(2,1)S(1)}, bf16[192,70,131]{2,1,0:T(8,128)(2,1)S(1)}) fusion(bf16[192,3,128]{2,1,0:T(4,128)(2,1)S(1)} %copy-done.7, bf16[192,64,128]{2,1,0:T(8,128)(2,1)} %bitcast.355, bf16[192,3,128]{2,1,0:T(4,128)(2,1)S(1)} %collective-permute-done.4, bf16[192,70,3]{2,1,0:T(8,128)(2,1)} %copy.45, ...), kind=kLoop, calls=%fused_computation.145 | loop fusion | flops 28170240 | bytes 10644480 | tf_op jit(solution)/shard_map/concatenate | solution.py:15
  337.6 89.3 %multiply_add_fusion.1 = f32[192,64,128]{2,1,0:T(8,128)} fusion(bf16[192,64,128]{2,1,0:T(8,128)(2,1)} %bitcast.356, bf16[192,3,128]{2,1,0:T(4,128)(2,1)S(1)} %collective-permute-done.4, bf16[192,70,131]{2,1,0:T(8,128)(2,1)S(1)} %get-tuple-element.460, bf16[192,67,128]{2,1,0:T(8,128)(2,1)} %constant_dynamic-update-slice_fusion, ...), kind=kLoop, calls=%fused_computation.155 | loop fusion | flops 245366784 | bytes 151180800 | tf_op jit(solution)/shard_map/add | solution.py:33
  426.9 10.9 %copy.71 = f32[24,8,64,128]{3,1,2,0:T(8,128)} copy(f32[24,8,64,128]{3,2,1,0:T(8,128)} %bitcast.357) | data formatting | bytes 12582912
  438.2 73.3 %while.27 = (s32[]{:T(128)}, bf16[192,8192]{1,0:T(8,128)(2,1)S(1)}, bf16[192,8192]{1,0:T(8,128)(2,1)}, f32[1,192]{1,0:T(1,128)S(1)}, f32[192,8192]{1,0:T(8,128)}...) while((s32[]{:T(128)}, bf16[192,8192]{1,0:T(8,128)(2,1)S(1)}, ...), condition=%wide.region_7.0_spmd, body=%wide.region_4.0_spmd.sunk | while | flops 2635337728 | bytes 13483227 | solution.py:85
  442.8 32.2 %fusion.174 = bf16[192,8192]{1,0:T(8,128)(2,1)S(1)} fusion(bf16[192,8192]{1,0:T(8,128)(2,1)S(1)} %get-tuple-element.806, s32[]{:T(128)S(6)} %select_n.23, bf16[768,192]{1,0:T(8,128)(2,1)} %get-tuple-element.831, bf16[192,768]{1,0:T(8,128)(2,1)} %get-tuple-element.829, f32[768]{0:T(1024)S(1)} %reduce.5, f32[192,8192]{1,0:T(8,128)} %get-tuple-element.826, ...), kind=kOutput, calls=%fused_computation.101.clone.1 | convolution fusion | flops 2632187904 | bytes 7037952 | tf_op jit(solution)/shard_map/while/body/eval_jaxpr/dot_general | solution.py:62
  479.3 32.2 %fusion.174 = bf16[192,8192]{1,0:T(8,128)(2,1)S(1)} fusion(bf16[192,8192]{1,0:T(8,128)(2,1)S(1)} %get-tuple-element.806, s32[]{:T(128)S(6)} %select_n.23, bf16[768,192]{1,0:T(8,128)(2,1)} %get-tuple-element.831, bf16[192,768]{1,0:T(8,128)(2,1)} %get-tuple-element.829, f32[768]{0:T(1024)S(1)} %reduce.5, f32[192,8192]{1,0:T(8,128)} %get-tuple-element.826, ...), kind=kOutput, calls=%fused_computation.101.clone.1 | convolution fusion | flops 2632187904 | bytes 7037952 | tf_op jit(solution)/shard_map/while/body/eval_jaxpr/dot_general | solution.py:62
  511.5 3.4 fusion.155
  514.9 5.3 %copy.50 = f32[128,64,128]{2,1,0:T(8,128)} copy(f32[128,64,128]{0,2,1:T(8,128)} %bitcast.361) | data formatting | bytes 8388608 | tf_op jit(solution)/shard_map/reshape | solution.py:149
  (230 shorter events, 41.4 us)
Async XLA Ops:
  0.0 62.0 %copy-start = (bf16[128,192]{0,1:T(8,128)(2,1)S(1)}, bf16[128,192]{0,1:T(8,128)(2,1)}, u32[]{:S(2)}) copy-start(bf16[128,192]{0,1:T(8,128)(2,1)} %param.22) | copy-start | bytes 147460
  2.1 13.9 %copy-start.8 = (bf16[2,768,192]{1,2,0:T(8,128)(2,1)S(1)}, bf16[2,768,192]{1,2,0:T(8,128)(2,1)}, u32[]{:S(2)}) copy-start(bf16[2,768,192]{1,2,0:T(8,128)(2,1)} %param.30) | copy-start | bytes 1769476
  4.6 57.4 %all-to-all-start = ((bf16[32,4,64,128]{3,2,1,0:T(8,128)(2,1)}), bf16[32,4,64,128]{3,2,1,0:T(8,128)(2,1)S(1)}, u32[]{:S(2)}, u32[]{:S(2)}) async-start(bf16[32,4,64,128]{3,2,1,0:T(8,128)(2,1)} %bitcast.15), calls=%async_computation | async-start | bytes 4194304 | tf_op jit(solution)/shard_map/all_to_all | solution.py:114
  79.1 24.4 %copy-start.72 = (f32[2,192]{1,0:T(2,128)S(1)}, f32[2,192]{1,0:T(2,128)}, u32[]{:S(2)}) copy-start(f32[2,192]{1,0:T(2,128)} %param.25) | copy-start | bytes 4612
  83.3 16.2 %copy-start.3 = (bf16[192,64,128]{0,1,2:T(8,128)(2,1)}, bf16[192,64,128]{0,1,2:T(8,128)(2,1)S(1)}, u32[]{:S(2)}) copy-start(bf16[192,64,128]{0,1,2:T(8,128)(2,1)S(1)} %multiply_convert_fusion) | copy-start | bytes 9437188
  83.5 8.1 %collective-permute-start = (bf16[192,3,128]{0,1,2:T(4,128)(2,1)S(1)}, bf16[192,3,128]{0,1,2:T(4,128)(2,1)S(1)}, u32[]{:S(2)}, u32[]{:S(2)}) collective-permute-start(bf16[192,3,128]{0,1,2:T(4,128)(2,1)S(1)} %get-tuple-element.457), channel_id=1, source_target_pairs={{0,8},{8,16},{16,24},{1,9},{9,17},{17,25},{2,10},{10,18},{18,26},{... | collective-permute-start | bytes 442376 | tf_op jit(solution)/shard_map/ppermute | solution.py:17
  85.1 14.4 %collective-permute-start.1 = (bf16[192,3,128]{0,1,2:T(4,128)(2,1)S(1)}, bf16[192,3,128]{0,1,2:T(4,128)(2,1)S(1)}, u32[]{:S(2)}, u32[]{:S(2)}) collective-permute-start(bf16[192,3,128]{0,1,2:T(4,128)(2,1)S(1)} %get-tuple-element.458), channel_id=1, source_target_pairs={{8,0},{16,8},{24,16},{9,1},{17,9},{25,17},{10,2},{18,10},{26,18},{... | collective-permute-start | bytes 442376 | tf_op jit(solution)/shard_map/ppermute | solution.py:19
  99.6 6.5 %collective-permute-start.2 = (bf16[192,70,3]{0,1,2:T(8,128)(2,1)S(1)}, bf16[192,70,3]{0,1,2:T(8,128)(2,1)S(1)}, u32[]{:S(2)}, u32[]{:S(2)}) collective-permute-start(bf16[192,70,3]{0,1,2:T(8,128)(2,1)S(1)} %get-tuple-element.455), channel_id=1, source_target_pairs={{0,1},{1,2},{2,3},{3,4},{4,5},{5,6},{6,7},{7,0},{8,9},{9,10},{10,1... | collective-permute-start | bytes 241928 | tf_op jit(solution)/shard_map/ppermute | solution.py:17
  99.7 6.4 %collective-permute-start.3 = (bf16[192,70,3]{0,1,2:T(8,128)(2,1)S(1)}, bf16[192,70,3]{0,1,2:T(8,128)(2,1)S(1)}, u32[]{:S(2)}, u32[]{:S(2)}) collective-permute-start(bf16[192,70,3]{0,1,2:T(8,128)(2,1)S(1)} %get-tuple-element.456), channel_id=1, source_target_pairs={{1,0},{2,1},{3,2},{4,3},{5,4},{6,5},{7,6},{0,7},{9,8},{10,9},{11,1... | collective-permute-start | bytes 241928 | tf_op jit(solution)/shard_map/ppermute | solution.py:19
  288.2 9.4 %collective-permute-start.5 = (bf16[192,3,128]{2,1,0:T(4,128)(2,1)S(1)}, bf16[192,3,128]{2,1,0:T(4,128)(2,1)S(1)}, u32[]{:S(2)}, u32[]{:S(2)}) collective-permute-start(bf16[192,3,128]{2,1,0:T(4,128)(2,1)S(1)} %get-tuple-element.463), channel_id=1, source_target_pairs={{8,0},{16,8},{24,16},{9,1},{17,9},{25,17},{10,2},{18,10},{26,18},{... | collective-permute-start | bytes 442376 | tf_op jit(solution)/shard_map/ppermute | solution.py:19
  289.5 8.1 %collective-permute-start.4 = (bf16[192,3,128]{2,1,0:T(4,128)(2,1)S(1)}, bf16[192,3,128]{2,1,0:T(4,128)(2,1)S(1)}, u32[]{:S(2)}, u32[]{:S(2)}) collective-permute-start(bf16[192,3,128]{2,1,0:T(4,128)(2,1)S(1)} %get-tuple-element.464), channel_id=1, source_target_pairs={{0,8},{8,16},{16,24},{1,9},{9,17},{17,25},{2,10},{10,18},{18,26},{... | collective-permute-start | bytes 442376 | tf_op jit(solution)/shard_map/ppermute | solution.py:17
  308.8 9.0 %collective-permute-start.6 = (bf16[192,70,3]{0,1,2:T(8,128)(2,1)S(1)}, bf16[192,70,3]{0,1,2:T(8,128)(2,1)S(1)}, u32[]{:S(2)}, u32[]{:S(2)}) collective-permute-start(bf16[192,70,3]{0,1,2:T(8,128)(2,1)S(1)} %copy.44), channel_id=1, source_target_pairs={{0,1},{1,2},{2,3},{3,4},{4,5},{5,6},{6,7},{7,0},{8,9},{9,10},{10,1... | collective-permute-start | bytes 241928 | tf_op jit(solution)/shard_map/ppermute | solution.py:17
  313.4 7.6 %collective-permute-start.7 = (bf16[192,70,3]{0,1,2:T(8,128)(2,1)S(1)}, bf16[192,70,3]{0,1,2:T(8,128)(2,1)S(1)}, u32[]{:S(2)}, u32[]{:S(2)}) collective-permute-start(bf16[192,70,3]{0,1,2:T(8,128)(2,1)S(1)} %copy.47), channel_id=1, source_target_pairs={{1,0},{2,1},{3,2},{4,3},{5,4},{6,5},{7,6},{0,7},{9,8},{10,9},{11,1... | collective-permute-start | bytes 241928 | tf_op jit(solution)/shard_map/ppermute | solution.py:19
  324.4 12.8 %copy-start.18 = (f32[192,1,1]{0,2,1:T(1,128)S(1)}, f32[192,1,1]{0,2,1:T(1,128)}, u32[]{:S(2)}) copy-start(f32[192,1,1]{0,2,1:T(1,128)} %get-tuple-element.513) | copy-start | bytes 2308
  324.4 12.8 %copy-start.19 = (f32[192,1,1]{0,2,1:T(1,128)S(1)}, f32[192,1,1]{0,2,1:T(1,128)}, u32[]{:S(2)}) copy-start(f32[192,1,1]{0,2,1:T(1,128)} %get-tuple-element.514) | copy-start | bytes 2308
  324.4 12.8 %copy-start.20 = (f32[192,1,1]{0,2,1:T(1,128)S(1)}, f32[192,1,1]{0,2,1:T(1,128)}, u32[]{:S(2)}) copy-start(f32[192,1,1]{0,2,1:T(1,128)} %get-tuple-element.515) | copy-start | bytes 2308
  324.4 12.8 %copy-start.21 = (f32[192,1,1]{0,2,1:T(1,128)S(1)}, f32[192,1,1]{0,2,1:T(1,128)}, u32[]{:S(2)}) copy-start(f32[192,1,1]{0,2,1:T(1,128)} %get-tuple-element.516) | copy-start | bytes 2308
  324.5 12.8 %copy-start.22 = (f32[192,1,1]{0,2,1:T(1,128)S(1)}, f32[192,1,1]{0,2,1:T(1,128)}, u32[]{:S(2)}) copy-start(f32[192,1,1]{0,2,1:T(1,128)} %get-tuple-element.517) | copy-start | bytes 2308
  324.5 12.8 %copy-start.23 = (f32[192,1,1]{0,2,1:T(1,128)S(1)}, f32[192,1,1]{0,2,1:T(1,128)}, u32[]{:S(2)}) copy-start(f32[192,1,1]{0,2,1:T(1,128)} %get-tuple-element.518) | copy-start | bytes 2308
  324.5 12.8 %copy-start.24 = (f32[192,1,1]{0,2,1:T(1,128)S(1)}, f32[192,1,1]{0,2,1:T(1,128)}, u32[]{:S(2)}) copy-start(f32[192,1,1]{0,2,1:T(1,128)} %get-tuple-element.519) | copy-start | bytes 2308
  324.5 12.8 %copy-start.25 = (f32[192,1,1]{0,2,1:T(1,128)S(1)}, f32[192,1,1]{0,2,1:T(1,128)}, u32[]{:S(2)}) copy-start(f32[192,1,1]{0,2,1:T(1,128)} %get-tuple-element.490) | copy-start | bytes 2308
  324.5 12.8 %copy-start.26 = (f32[192,1,1]{0,2,1:T(1,128)S(1)}, f32[192,1,1]{0,2,1:T(1,128)}, u32[]{:S(2)}) copy-start(f32[192,1,1]{0,2,1:T(1,128)} %get-tuple-element.491) | copy-start | bytes 2308
  324.5 12.8 %copy-start.27 = (f32[192,1,1]{0,2,1:T(1,128)S(1)}, f32[192,1,1]{0,2,1:T(1,128)}, u32[]{:S(2)}) copy-start(f32[192,1,1]{0,2,1:T(1,128)} %get-tuple-element.492) | copy-start | bytes 2308
  324.5 12.8 %copy-start.28 = (f32[192,1,1]{0,2,1:T(1,128)S(1)}, f32[192,1,1]{0,2,1:T(1,128)}, u32[]{:S(2)}) copy-start(f32[192,1,1]{0,2,1:T(1,128)} %get-tuple-element.493) | copy-start | bytes 2308
  324.5 12.8 %copy-start.29 = (f32[192,1,1]{0,2,1:T(1,128)S(1)}, f32[192,1,1]{0,2,1:T(1,128)}, u32[]{:S(2)}) copy-start(f32[192,1,1]{0,2,1:T(1,128)} %get-tuple-element.494) | copy-start | bytes 2308
  324.5 12.8 %copy-start.30 = (f32[192,1,1]{0,2,1:T(1,128)S(1)}, f32[192,1,1]{0,2,1:T(1,128)}, u32[]{:S(2)}) copy-start(f32[192,1,1]{0,2,1:T(1,128)} %get-tuple-element.495) | copy-start | bytes 2308
  324.5 12.8 %copy-start.31 = (f32[192,1,1]{0,2,1:T(1,128)S(1)}, f32[192,1,1]{0,2,1:T(1,128)}, u32[]{:S(2)}) copy-start(f32[192,1,1]{0,2,1:T(1,128)} %get-tuple-element.496) | copy-start | bytes 2308
  324.6 12.8 %copy-start.32 = (f32[192,1,1]{0,2,1:T(1,128)S(1)}, f32[192,1,1]{0,2,1:T(1,128)}, u32[]{:S(2)}) copy-start(f32[192,1,1]{0,2,1:T(1,128)} %get-tuple-element.497) | copy-start | bytes 2308
  324.6 12.8 %copy-start.33 = (f32[192,1,1]{0,2,1:T(1,128)S(1)}, f32[192,1,1]{0,2,1:T(1,128)}, u32[]{:S(2)}) copy-start(f32[192,1,1]{0,2,1:T(1,128)} %get-tuple-element.498) | copy-start | bytes 2308
  324.6 12.8 %copy-start.34 = (f32[192,1,1]{0,2,1:T(1,128)S(1)}, f32[192,1,1]{0,2,1:T(1,128)}, u32[]{:S(2)}) copy-start(f32[192,1,1]{0,2,1:T(1,128)} %get-tuple-element.499) | copy-start | bytes 2308
  324.6 12.8 %copy-start.35 = (f32[192,1,1]{0,2,1:T(1,128)S(1)}, f32[192,1,1]{0,2,1:T(1,128)}, u32[]{:S(2)}) copy-start(f32[192,1,1]{0,2,1:T(1,128)} %get-tuple-element.500) | copy-start | bytes 2308
  438.2 73.3 %copy-start.11 = (bf16[192,128]{1,0:T(8,128)(2,1)S(1)}, bf16[192,128]{1,0:T(8,128)(2,1)}, u32[]{:S(2)}) copy-start(bf16[192,128]{1,0:T(8,128)(2,1)} %param.33) | copy-start | bytes 147460
  (60 other events, 681.1 us)
where the time goes:
time: 522 us; the launch traced here: 520 us
  other arithmetic  204 us (39%)
  matrix products  136 us (26%)
  local copies, waits for them, and re-layouts  85.5 us (16%)
  waiting for transfers between devices  57.7 us (11%)
  starting transfers between devices  23.6 us (5%)
  loops' own time  12.3 us (2%)
    add x2, other arithmetic, depthwise(): summed + padded[:, i:i + row_count, j:j + col_count] * kernel[:, i, j][:,...  155 us
    dot_general x4, matrix products, mix_cells(): jnp.dot(contract.T, hidden, preferred_element_type=jnp.float32)  129 us
    all_to_all x1, waiting for transfers between devices, body(): lax.all_to_all(tiles, ('lat', 'lon'), split_axis=0, concat_axis=1, tiled=...  44 us
    unnamed x174, local copies, waits for them, and re-layouts  31.6 us
    concatenate x3, other arithmetic, with_halo(): jnp.concatenate([lax.ppermute(tail, axis, [(i, (i + 1) % count) for i in...  25.1 us
    another operation x2, loops' own time, mix_region(): lax.fori_loop(0, turns, one_part, jnp.zeros((channels, cells), jnp.bfloat...  12.3 us
  transfers between devices with their start and end apart: 9, of which 4 were waited for; matrix products, arithmetic and copies ran while one was open for 4% of the time, Pallas kernels for 0%

commit v1 on v0

v1 whole, which is shorter than its diff:
```python
import functools

import jax
import jax.numpy as jnp
from jax import lax
from jax.experimental import pallas as pl
from jax.experimental.pallas import tpu as pltpu
from jax.sharding import PartitionSpec as P

ln_eps = 1e-06
f32 = jnp.float32
bf16 = jnp.bfloat16
lanes = 128
vmem_bytes = 56 * 2**20

edge_order = [*range(0, 16), *range(48, 64), *range(16, 20), *range(44, 48)]
mid_order = [*range(24, 40), *range(40, 44), *range(20, 24)]


def params_for(flops=0, bytes_accessed=0):
    return dict(
        compiler_params=pltpu.CompilerParams(vmem_limit_bytes=vmem_bytes),
        cost_estimate=pl.CostEstimate(
            flops=int(flops), bytes_accessed=int(bytes_accessed), transcendentals=0
        ),
    )


def lane_index(shape):
    return lax.broadcasted_iota(jnp.int32, shape, len(shape) - 1)


def prep_body(q_ref, s_ref, edge_ref, mid_ref):
    channels, tiles = q_ref.shape[0], q_ref.shape[2] // lanes
    low = lax.broadcasted_iota(jnp.int32, (8, lanes), 0) < 4
    for c in range(channels):
        scale = s_ref[c]
        for b in range(tiles):
            x = q_ref[c, :, b * lanes : (b + 1) * lanes].astype(f32) * scale
            edge_ref[0, b, c, 0:16] = x[0:16].astype(bf16)
            edge_ref[0, b, c, 16:32] = x[48:64].astype(bf16)
            edge_ref[0, b, c, 32:40] = jnp.where(low, x[16:24], x[40:48]).astype(bf16)
            mid_ref[0, b, c, 0:16] = x[24:40].astype(bf16)
            mid_ref[0, b, c, 16:24] = jnp.where(low, x[40:48], x[16:24]).astype(bf16)


def prep(q_state, scales, n_lat, n_lon, rows):
    channels, n_rows, n_cols = q_state.shape
    wide = jnp.broadcast_to(scales[:, :, None], (channels, n_rows, lanes))
    sizes = (len(edge_order), len(mid_order))
    outs = pl.pallas_call(
        prep_body,
        grid=(n_lat,),
        in_specs=[
            pl.BlockSpec((channels, rows, n_cols), lambda a: (0, a, 0)),
            pl.BlockSpec((channels, rows, lanes), lambda a: (0, a, 0)),
        ],
        out_specs=[
            pl.BlockSpec((1, n_lon, channels, n, lanes), lambda a: (a, 0, 0, 0, 0)) for n in sizes
        ],
        out_shape=[
            jax.ShapeDtypeStruct((n_lat, n_lon, channels, n, lanes), bf16) for n in sizes
        ],
        name="dequantize",
        **params_for(0, 2 * q_state.size * 2),
    )(q_state, wide)
    return [o.reshape(n_lat * n_lon, channels, n, lanes) for o, n in zip(outs, sizes)]


def pack_edges(packed, row_value, slot):
    turned = row_value if slot == 0 else pltpu.roll(row_value, 8 * slot, 1)
    if packed is None:
        return turned
    here = ((lane_index(row_value.shape) + 4) >> 3) & 15
    return jnp.where(here == slot, turned, packed)


def stem_body(order, x_ref, w_ref, b_ref, mask_ref, f_ref, e_ref):
    count = len(order)
    bias = b_ref[...]
    done = 0
    while done < count:
        size = min(16, count - done)
        x = x_ref[:, done : done + size, :]
        if size == 16:
            x = jnp.swapaxes(x, 0, 1)
        else:
            x = jnp.swapaxes(x.astype(f32), 0, 1).astype(bf16)
        packed = None
        for half in range(0, size, 8):
            joined = jnp.concatenate([x[half + i] for i in range(8)], axis=1)
            y = jnp.dot(w_ref[...], joined, preferred_element_type=f32)
            for i in range(8):
                at = done + half + i
                ocean = mask_ref[order[at] : order[at] + 1, :].astype(f32)
                value = ((y[:, i * lanes : (i + 1) * lanes] + bias) * ocean).astype(bf16)
                f_ref[at] = value
                packed = pack_edges(packed, value, half + i)
        e_ref[done // 16] = packed
        done += size


def stem(state, weight_t, bias_wide, mask, order):
    d = weight_t.shape[0]
    n = len(order)
    groups = -(-n // 16)
    return pl.pallas_call(
        functools.partial(stem_body, order),
        out_shape=[
            jax.ShapeDtypeStruct((n, d, lanes), bf16),
            jax.ShapeDtypeStruct((groups, d, lanes), bf16),
        ],
        name="stem",
        **params_for(2 * d * state.size, 2 * state.size + 2 * n * d * lanes),
    )(state, weight_t, bias_wide, mask)


def band_body(segments, v_ref, o_ref):
    m, k = o_ref.shape[1:]
    width = v_ref.shape[1]
    row = lax.broadcasted_iota(jnp.int32, (m, width), 0)

    def step(g, _):
        for u in range(8):
            c = g * 8 + u
            spread = jnp.broadcast_to(v_ref[pl.ds(c, 1), :], (m, width))
            band = None
            for first, shift in segments:
                turned = pltpu.roll(spread, shift, 1, stride=1, stride_axis=0)
                band = turned if band is None else jnp.where(row < first, band, turned)
            o_ref[c] = band[:, :k].astype(bf16)
        return 0

    lax.fori_loop(0, v_ref.shape[0] // 8, step, 0)


def band(dw, window, m, segments):
    d = dw.shape[0]
    k = 7 * window
    width = -(-k // lanes) * lanes
    taps = jnp.transpose(dw, (0, 2, 1))
    taps = jnp.pad(taps, ((0, 0), (0, 0), (0, window - 7))).reshape(d, k)
    taps = jnp.pad(taps, ((0, 0), (0, width - k)))
    return pl.pallas_call(
        functools.partial(band_body, segments),
        out_shape=jax.ShapeDtypeStruct((d, m, k), bf16),
        name="bands",
        **params_for(0, 2 * d * m * k),
    )(taps)


def block_body(plan, head, *refs):
    feats = refs[: plan["sources"]]
    refs = refs[plan["sources"] :]
    (band_ref, dwb_ref, gain_ref, lnb_ref, w1_ref, w2_ref, ones_ref, ls_ref, lsb_ref, mask_ref) = refs[:10]
    refs = refs[10:]
    if head:
        head_ref = refs[0]
        refs = refs[1 + plan["carried"] :]
        out_ref, conv_ref, tend_ref, sems = refs
    else:
        f_ref, e_ref, conv_ref = refs
    window, out_rows = plan["window"], plan["out_rows"]
    p, m = len(window), len(out_rows)
    d = band_ref.shape[0]
    lane = lane_index((p, lanes))
    left_part = ((lane_index((16, lanes)) + 4) & 7) < 4

    def conv_step(g, _):
        cs = pl.ds(pl.multiple_of(g * 16, 16), 16)
        halos = {}
        xs, hs = [], []
        zero = jnp.zeros((16, lanes), bf16)
        for start in range(0, p, 16):
            xrow, hrow = [], []
            for entry in window[start : start + 16]:
                if entry is None:
                    xrow.append(zero)
                    hrow.append(zero)
                    continue
                src, at, left, right, slot = entry
                xrow.append(feats[src][at, cs, :])
                if (left, right) not in halos:
                    halos[left, right] = jnp.where(
                        left_part, feats[left[0]][left[1], cs, :], feats[right[0]][right[1], cs, :]
                    )
                both = halos[left, right]
                hrow.append(both if slot == 0 else pltpu.roll(both, lanes - 8 * slot, 1))
            xs.append(jnp.swapaxes(jnp.stack(xrow), 0, 1))
            hs.append(jnp.swapaxes(jnp.stack(hrow), 0, 1))
        for u in range(16):
            x = jnp.concatenate([part[u] for part in xs], axis=0)
            h = jnp.concatenate([part[u] for part in hs], axis=0)
            shifted = []
            for s in range(-3, 4):
                if s == 0:
                    shifted.append(x)
                    continue
                past = (lane < s) if s > 0 else (lane >= lanes + s)
                shifted.append(pltpu.roll(jnp.where(past, h, x), (-s) % lanes, 1))
            taps = jnp.concatenate(shifted, axis=0)
            conv_ref[g * 16 + u] = jnp.dot(band_ref[g * 16 + u], taps, preferred_element_type=f32)
        return 0

    lax.fori_loop(0, d // 16, conv_step, 0)

    packed = None
    for k in range(m // 8):
        y = conv_ref[:, 8 * k : 8 * k + 8, :] + dwb_ref[...]
        average = jnp.sum(y, axis=0, keepdims=True) * (1.0 / d)
        centered = y - average
        variance = jnp.sum(centered * centered, axis=0, keepdims=True) * (1.0 / d)
        normed = centered * lax.rsqrt(variance + ln_eps) * gain_ref[...] + lnb_ref[...]
        normed = jnp.swapaxes(normed, 0, 1).astype(bf16)
        joined = jnp.concatenate([normed[i] for i in range(8)], axis=1)
        joined = jnp.concatenate([joined, ones_ref[...]], axis=0)
        hidden = jnp.dot(w1_ref[...], joined, preferred_element_type=f32)
        hidden = (hidden + hidden * lax.erf(hidden * 0.7071067811865476)).astype(bf16)
        projected = jnp.dot(w2_ref[...], hidden, preferred_element_type=f32)
        updated = []
        for i in range(8):
            row = out_rows[8 * k + i]
            src, at = plan["residual"][8 * k + i]
            ocean = mask_ref[row : row + 1, :].astype(f32)
            branch = projected[:, i * lanes : (i + 1) * lanes] * ls_ref[...] + lsb_ref[...]
            value = ((feats[src][at].astype(f32) + branch) * ocean).astype(bf16)
            updated.append(value)
            if not head:
                f_ref[8 * k + i] = value
                slot = (8 * k + i) % 16
                packed = pack_edges(packed if slot else None, value, slot)
                if slot == 15:
                    e_ref[(8 * k + i) // 16] = packed
        if head:
            joined = jnp.concatenate(updated, axis=1)
            t = jnp.dot(head_ref[...], joined, preferred_element_type=f32)
            t = jnp.stack([t[:, i * lanes : (i + 1) * lanes] for i in range(8)])
            tend_ref[:, 8 * k : 8 * k + 8, :] = jnp.swapaxes(t, 0, 1)
            first = out_rows[8 * k]
            pltpu.make_async_copy(
                tend_ref.at[:, pl.ds(8 * k, 8), :], out_ref.at[:, pl.ds(first, 8), :], sems.at[k]
            ).start()
    if head:
        for k in range(m // 8):
            first = out_rows[8 * k]
            pltpu.make_async_copy(
                tend_ref.at[:, pl.ds(8 * k, 8), :], out_ref.at[:, pl.ds(first, 8), :], sems.at[k]
            ).wait()


def block(plan, feats, bands, layer, mask, head=None, carried=None):
    d = bands.shape[0]
    m = len(plan["out_rows"])
    hid = layer[3].shape[0]
    plan = dict(plan, sources=len(feats), carried=0 if carried is None else 1)
    flops = 2 * m * lanes * (2 * d * hid + d * 7 * len(plan["window"]))
    operands = [*feats, bands, *layer, mask]
    scratch = [pltpu.VMEM((d, m, lanes), f32)]
    if head is None:
        return pl.pallas_call(
            functools.partial(block_body, plan, False),
            out_shape=[
                jax.ShapeDtypeStruct((m, d, lanes), bf16),
                jax.ShapeDtypeStruct((m // 16, d, lanes), bf16),
            ],
            scratch_shapes=scratch,
            name="block",
            **params_for(flops, 20 * m * d * lanes),
        )(*operands)
    vmem = pl.BlockSpec(memory_space=pltpu.VMEM)
    anywhere = pl.BlockSpec(memory_space=pl.ANY)
    c_out = head.shape[0]
    specs = [vmem] * (len(operands) + 1)
    operands.append(head)
    aliases = {}
    if carried is not None:
        aliases = {len(operands): 0}
        operands.append(carried)
        specs.append(anywhere)
    scratch += [pltpu.VMEM((c_out, m, lanes), f32), pltpu.SemaphoreType.DMA((m // 8,))]
    return pl.pallas_call(
        functools.partial(block_body, plan, True),
        out_shape=jax.ShapeDtypeStruct((c_out, mask.shape[0], lanes), f32),
        in_specs=specs,
        out_specs=anywhere,
        scratch_shapes=scratch,
        input_output_aliases=aliases,
        name="block_head",
        **params_for(flops, 20 * m * d * lanes),
    )(*operands)


def filled(window):
    return window + [None] * (-len(window) % 16)


def body(
    q_state,
    scales,
    land_mask,
    stem_weight,
    stem_bias,
    dw_weight,
    dw_bias,
    ln_gain,
    ln_bias,
    w_in,
    b_in,
    w_out,
    b_out,
    layer_scale,
    head_weight,
):
    n_lat = lax.axis_size("lat")
    n_lon = lax.axis_size("lon")
    rows = land_mask.shape[0]
    d = stem_weight.shape[1]
    axes = ("lat", "lon")

    edge_send, mid_send = prep(q_state, scales, n_lat, n_lon, rows)

    def regroup(part):
        got = lax.all_to_all(part, axes, split_axis=0, concat_axis=0, tiled=True)
        return got.reshape(-1, part.shape[2], lanes)

    edge_state = regroup(edge_send)
    mid_state = regroup(mid_send)

    def wide(v):
        return jnp.broadcast_to(v[:, None], (v.shape[0], lanes))

    def wide8(v):
        return jnp.broadcast_to(v[:, None, None], (v.shape[0], 8, lanes))

    ones = jnp.broadcast_to(
        (lax.broadcasted_iota(jnp.int32, (16, 8 * lanes), 0) < 3).astype(bf16), (16, 8 * lanes)
    )

    def layer_of(b):
        high = b_in[b].astype(bf16)
        rest = b_in[b] - high.astype(f32)
        mid = rest.astype(bf16)
        low = (rest - mid.astype(f32)).astype(bf16)
        terms = jnp.stack([high, mid, low], axis=1)
        w1 = jnp.concatenate([w_in[b].T, jnp.pad(terms, ((0, 0), (0, 13)))], axis=1)
        return (
            wide8(dw_bias[b]),
            wide8(ln_gain[b]),
            wide8(ln_bias[b]),
            w1,
            w_out[b].T,
            ones,
            wide(layer_scale[b] * 0.5),
            wide(layer_scale[b] * b_out[b]),
        )

    layers = [layer_of(b) for b in range(2)]
    two = ((0, 0), (16, 6))
    bands_edge1 = band(dw_weight[0], 48, 32, two)
    bands_mid1 = band(dw_weight[0], 48, 32, ((0, 0),))
    bands_edge2 = band(dw_weight[1], 32, 16, ((0, 0), (8, 6)))
    bands_mid2 = band(dw_weight[1], 64, 48, ((0, 0),))

    def lon_exchange(packed):
        return (
            lax.ppermute(packed, "lon", [(i, (i + 1) % n_lon) for i in range(n_lon)]),
            lax.ppermute(packed, "lon", [((i + 1) % n_lon, i) for i in range(n_lon)]),
        )

    def lat_exchange(feat, left, right, first, last):
        def send(at, group):
            return jnp.concatenate(
                [feat[at : at + 3], left[group : group + 1], right[group : group + 1]], axis=0
            )

        north = lax.ppermute(send(*last), "lat", [(i, i + 1) for i in range(n_lat - 1)])
        south = lax.ppermute(send(*first), "lat", [(i + 1, i) for i in range(n_lat - 1)])
        return north, south

    weight_t = stem_weight.T
    stem_wide = wide(stem_bias)

    fe, ee = stem(edge_state, weight_t, stem_wide, land_mask, edge_order)
    el, er = lon_exchange(ee)
    north, south = lat_exchange(fe, el, er, (0, 0), (29, 1))

    def own(order, src, left, right):
        return {
            r: (src, t, (left, t // 16), (right, t // 16), t % 16) for t, r in enumerate(order)
        }

    def lat_halo(src_n, src_s, last_slot):
        got = {}
        for i in range(3):
            got[i - 3] = (src_n, i, (src_n, 3), (src_n, 4), last_slot + i)
            got[rows + i] = (src_s, i, (src_s, 3), (src_s, 4), i)
        return got

    def plan_of(table, groups):
        window, out_rows = [], []
        for first, last in groups:
            window += [table[r] for r in range(first - 3, last + 3)]
            out_rows += list(range(first, last))
        return dict(
            window=filled(window),
            out_rows=out_rows,
            residual=[table[r][:2] for r in out_rows],
        )

    table = {**own(edge_order, 0, 1, 2), **lat_halo(3, 4, 13)}
    edge1_order = [*range(0, 16), *range(48, 64)]
    ge, pe = block(
        plan_of(table, [(0, 16), (48, 64)]),
        (fe, el, er, north, south),
        bands_edge1,
        layers[0],
        land_mask,
    )

    fm, em = stem(mid_state, weight_t, stem_wide, land_mask, mid_order)
    ml, mr = lon_exchange(em)
    table = {**own(edge_order, 0, 1, 2), **own(mid_order, 3, 4, 5)}
    gm, pm = block(
        plan_of(table, [(16, 48)]),
        (fe, el, er, fm, ml, mr),
        bands_mid1,
        layers[0],
        land_mask,
    )

    gel, ger = lon_exchange(pe)
    gnorth, gsouth = lat_exchange(ge, gel, ger, (0, 0), (29, 1))
    gml, gmr = lon_exchange(pm)
    head_t = head_weight.T
    table = {**own(edge1_order, 0, 1, 2), **lat_halo(3, 4, 13)}
    out = block(
        plan_of(table, [(0, 8), (56, 64)]),
        (ge, gel, ger, gnorth, gsouth),
        bands_edge2,
        layers[1],
        land_mask,
        head=head_t,
    )
    table = {**own(edge1_order, 0, 1, 2), **own(range(16, 48), 3, 4, 5)}
    return block(
        plan_of(table, [(8, 56)]),
        (ge, gel, ger, gm, gml, gmr),
        bands_mid2,
        layers[1],
        land_mask,
        head=head_t,
        carried=out,
    )


def solution(mesh):
    placed = (
        P(("lat", "lon"), None, None),
        P(("lat", "lon"), None),
        P("lat", "lon"),
        *([P()] * 12),
    )
    return jax.shard_map(
        body, mesh=mesh, in_specs=placed, out_specs=P(None, "lat", "lon"), check_vma=False
    )
```

time: 522 us -> 217 us (0.42)
  other arithmetic: 204 us -> 1.97 us
  matrix products: 136 us -> 0 us
  Pallas kernels: 0 us -> 115 us
  local copies, waits for them, and re-layouts: 85.5 us -> 23.8 us
  waiting for transfers between devices: 57.7 us -> 44.8 us
  loops' own time: 12.3 us -> 0 us
    add x2 -> x0, other arithmetic: 155 us -> none  [depthwise(): summed + padded[:, i:i + row_count, j:j + col_count] * kernel[:, i, j][:,...]
    dot_general x6 -> x0, matrix products: 136 us -> none  [the longest x4 129 us: mix_cells(): jnp.dot(contract.T, hidden, preferred_element_type=jnp.float32)]
    pallas_call x0 -> x11, Pallas kernels: none -> 115 us  [the longest x2 41.1 us: block(): pl.pallas_call(functools.partial(block_body, plan, True), out_shape=jax.S...]
    unnamed x174 -> x52, local copies, waits for them, and re-layouts: 31.6 us -> 3.36 us
    concatenate x3 -> x6, other arithmetic: 25.1 us -> 1.92 us  [the longest x2 1.79 us: layer_of(): w1 = jnp.concatenate([w_in[b].T, jnp.pad(terms, ((0, 0), (0, 13)))], axis=1)]
    reduce_sum x8 -> x0, other arithmetic: 17.2 us -> none  [the longest x4 8.97 us: mix_cells(): variance = jnp.mean(centered * centered, axis=0, keepdims=True)]
    slice x17 -> x11, local copies, waits for them, and re-layouts: 19.1 us -> 2.16 us  [the longest x2 2 us: send(): feat[at:at + 3]]
    all_to_all x1 -> x2, waiting for transfers between devices: 44 us -> 29.3 us  [regroup(): got = lax.all_to_all(part, axes, split_axis=0, concat_axis=0, tiled=True)]
  transfers between devices with their start and end apart: 9 -> 14, of which waited for: 4 -> 5; matrix products, arithmetic and copies ran while one was open for 4% -> 10% of each run, Pallas kernels for 0% -> 39%
where the time goes in v1:
time: 217 us; the launch traced here: 215 us
  Pallas kernels  115 us (53%)
  waiting for transfers between devices  44.8 us (21%)
  starting transfers between devices  28.3 us (13%)
  local copies, waits for them, and re-layouts  23.8 us (11%)
    pallas_call x2, Pallas kernels, block(): pl.pallas_call(functools.partial(block_body, plan, True), out_shape=jax.S...  41.1 us
    pallas_call x2, Pallas kernels, block(): pl.pallas_call(functools.partial(block_body, plan, False), out_shape=[jax...  38.5 us
    all_to_all x2, waiting for transfers between devices, regroup(): got = lax.all_to_all(part, axes, split_axis=0, concat_axis=0, tiled=True)  29.3 us
    pallas_call x4, Pallas kernels, band(): pl.pallas_call(functools.partial(band_body, segments), out_shape=jax.Shap...  25.3 us
    all_to_all x2, starting transfers between devices, regroup(): got = lax.all_to_all(part, axes, split_axis=0, concat_axis=0, tiled=True)  9.92 us
    ppermute x4, waiting for transfers between devices, lon_exchange(): lax.ppermute(packed, 'lon', [((i + 1) % n_lon, i) for i in range(n_lon)])  9.28 us
    ppermute x2, starting transfers between devices, lat_exchange(): lax.ppermute(send(*last), 'lat', [(i, i + 1) for i in range(n_lat - 1)])  7.85 us
    ppermute x4, starting transfers between devices, lon_exchange(): lax.ppermute(packed, 'lon', [((i + 1) % n_lon, i) for i in range(n_lon)])  7.32 us
  transfers between devices with their start and end apart: 14, of which 5 were waited for; matrix products, arithmetic and copies ran while one was open for 10% of the time, Pallas kernels for 39%

profile of v1, /device:TPU:0, one launch (start us, length us, event | category | flops | bytes accessed | tf_op | source)
XLA Modules:
  0.0 214.9 jit_solution(15984938826999545542)
XLA Ops:
  0.0 1.7 broadcast_in_dim.36.s_ref
  1.7 4.0 %dequantize.1 = (bf16[4,8,4,40,128]{4,3,2,1,0:T(8,128)(2,1)}, bf16[4,8,4,24,128]{4,3,2,1,0:T(8,128)(2,1)}) custom-call(bf16[4,256,1024]{2,1,0:T(8,128)(2,1)} %q_ref.1, f32[4,256,128]{2,1,0:T(8,128)} %broadcast_in_dim.36.s_ref), custom_call_target="tpu_custom_call" | custom-call | bytes 4194304 | tf_op jit(solution)/shard_map/dequantize/pallas_call | solution.py:51
  5.7 7.3 %all-to-all-start = ((bf16[32,4,40,128]{3,2,1,0:T(8,128)(2,1)}), bf16[32,4,40,128]{3,2,1,0:T(8,128)(2,1)S(1)}, u32[]{:S(2)}, u32[]{:S(2)}) async-start(bf16[32,4,40,128]{3,2,1,0:T(8,128)(2,1)} %bitcast.72), calls=%async_computation | async-start | bytes 2621440 | tf_op jit(solution)/shard_map/all_to_all | solution.py:323
  15.0 1.9 slice_bitcast_fusion
  16.9 29.3 %all-to-all-done = bf16[32,4,40,128]{3,2,1,0:T(8,128)(2,1)S(1)} async-done(((bf16[32,4,40,128]{3,2,1,0:T(8,128)(2,1)}), bf16[32,4,40,128]{3,2,1,0:T(8,128)(2,1)S(1)}, u32[]{:S(2)}, u32[]{:S(2)}) %all-to-all-start) | async-done | bytes 1310752 | tf_op jit(solution)/shard_map/all_to_all | solution.py:323
  46.2 2.6 %all-to-all-start.1 = ((bf16[32,4,24,128]{3,2,1,0:T(8,128)(2,1)}), bf16[32,4,24,128]{3,2,1,0:T(8,128)(2,1)S(1)}, u32[]{:S(2)}, u32[]{:S(2)}) async-start(bf16[32,4,24,128]{3,2,1,0:T(8,128)(2,1)} %bitcast.16), calls=%async_computation.1 | async-start | bytes 1572864 | tf_op jit(solution)/shard_map/all_to_all | solution.py:323
  50.5 3.7 %stem.2 = (bf16[40,192,128]{2,1,0:T(8,128)(2,1)}, bf16[3,192,128]{2,1,0:T(8,128)(2,1)}) custom-call(bf16[128,40,128]{2,1,0:T(8,128)(2,1)} %bitcast.66, bf16[192,128]{1,0:T(8,128)(2,1)} %bitcast.76, f32[192,128]{1,0:T(8,128)} %broadcast_in_dim.37.b_ref, s32[64,128]{1,0:T(8,128)} %refs_15_.3), custom_call_target="tpu_custom_call" | custom-call | flops 251658240 | bytes 3276800 | tf_op jit(solution)/shard_map/stem/pallas_call | solution.py:107
  54.1 3.4 %collective-permute-start.1 = (bf16[3,192,128]{2,1,0:T(8,128)(2,1)}, bf16[3,192,128]{2,1,0:T(8,128)(2,1)S(1)}, u32[]{:S(2)}, u32[]{:S(2)}) collective-permute-start(bf16[3,192,128]{2,1,0:T(8,128)(2,1)} %get-tuple-element.17), channel_id=1, source_target_pairs={{1,0},{2,1},{3,2},{4,3},{5,4},{6,5},{7,6},{0,7},{9,8},{10,9},{11,1... | collective-permute-start | bytes 442376 | tf_op jit(solution)/shard_map/ppermute | solution.py:367
  58.5 6.8 %collective-permute-done.1.refs_2_ = bf16[3,192,128]{2,1,0:T(8,128)(2,1)S(1)} collective-permute-done((bf16[3,192,128]{2,1,0:T(8,128)(2,1)}, bf16[3,192,128]{2,1,0:T(8,128)(2,1)S(1)}, u32[]{:S(2)}, u32[]{:S(2)}) %collective-permute-start.1) | collective-permute-done | bytes 147488 | tf_op jit(solution)/shard_map/ppermute | solution.py:367
  65.3 3.5 %collective-permute-done.refs_1_ = bf16[3,192,128]{2,1,0:T(8,128)(2,1)S(1)} collective-permute-done((bf16[3,192,128]{2,1,0:T(8,128)(2,1)}, bf16[3,192,128]{2,1,0:T(8,128)(2,1)S(1)}, u32[]{:S(2)}, u32[]{:S(2)}) %collective-permute-start) | collective-permute-done | bytes 147488 | tf_op jit(solution)/shard_map/ppermute | solution.py:366
  68.9 3.4 %collective-permute-start.2 = (bf16[5,192,128]{2,1,0:T(8,128)(2,1)S(1)}, bf16[5,192,128]{2,1,0:T(8,128)(2,1)S(1)}, u32[]{:S(2)}, u32[]{:S(2)}) collective-permute-start(bf16[5,192,128]{2,1,0:T(8,128)(2,1)S(1)} %pad_maximum_fusion), channel_id=1, source_target_pairs={{0,8},{8,16},{16,24},{1,9},{9,17},{17,25},{2,10},{10,18},{18,26},{... | collective-permute-start | bytes 737288 | tf_op jit(solution)/shard_map/ppermute | solution.py:376
  72.4 1.3 collective-permute-start.3
  74.7 6.2 %bands.5.refs_6_ = bf16[192,32,336]{2,1,0:T(8,128)(2,1)} custom-call(f32[192,384]{1,0:T(8,128)} %pad.34.v_ref), custom_call_target="tpu_custom_call" | custom-call | bytes 4128768 | tf_op jit(solution)/shard_map/bands/pallas_call | solution.py:144
  80.8 6.1 %bands.4.refs_5_ = bf16[192,32,336]{2,1,0:T(8,128)(2,1)} custom-call(f32[192,384]{1,0:T(8,128)} %pad.34.v_ref), custom_call_target="tpu_custom_call" | custom-call | bytes 4128768 | tf_op jit(solution)/shard_map/bands/pallas_call | solution.py:144
  89.5 4.2 %bands.7.refs_5_ = bf16[192,16,224]{2,1,0:T(8,128)(2,1)} custom-call(f32[192,256]{1,0:T(8,128)} %pad.40.v_ref), custom_call_target="tpu_custom_call" | custom-call | bytes 1376256 | tf_op jit(solution)/shard_map/bands/pallas_call | solution.py:144
  93.7 8.9 %bands.6.refs_6_ = bf16[192,48,448]{2,1,0:T(8,128)(2,1)} custom-call(f32[192,512]{1,0:T(8,128)} %pad.37.v_ref), custom_call_target="tpu_custom_call" | custom-call | bytes 8257536 | tf_op jit(solution)/shard_map/bands/pallas_call | solution.py:144
  103.5 2.9 %stem.3 = (bf16[24,192,128]{2,1,0:T(8,128)(2,1)}, bf16[2,192,128]{2,1,0:T(8,128)(2,1)}) custom-call(bf16[128,24,128]{2,1,0:T(8,128)(2,1)} %bitcast.67, bf16[192,128]{1,0:T(8,128)(2,1)} %bitcast.77, f32[192,128]{1,0:T(8,128)} %broadcast_in_dim.37.b_ref, s32[64,128]{1,0:T(8,128)} %refs_15_.3), custom_call_target="tpu_custom_call" | custom-call | flops 150994944 | bytes 1966080 | tf_op jit(solution)/shard_map/stem/pallas_call | solution.py:107
  109.1 1.2 broadcast_in_dim.85.refs_8_.refs_9_
  110.3 1.2 broadcast_in_dim.41.refs_7_.refs_8_
  111.5 1.2 broadcast_in_dim.39.refs_6_.refs_7_
  112.7 19.2 %block.2 = (bf16[32,192,128]{2,1,0:T(8,128)(2,1)}, bf16[2,192,128]{2,1,0:T(8,128)(2,1)}) custom-call(bf16[40,192,128]{2,1,0:T(8,128)(2,1)} %get-tuple-element.16.refs_0_, bf16[3,192,128]{2,1,0:T(8,128)(2,1)} %copy-done.6, bf16[3,192,128]{2,1,0:T(8,128)(2,1)} %copy-done.5, bf16[5,192,128]{2,1,0:T(8,128)(2,1)} %copy-done.22, bf16[5,192,128]{2,1,0:T(8,128)(2,1)} %copy-done.23, ...), custom_call_target="tpu_custom_call" | custom-call | flops 2944401408 | bytes 15728640 | tf_op jit(solution)/shard_map/block/pallas_call | solution.py:260
  131.8 3.2 %collective-permute-start.5 = (bf16[2,192,128]{2,1,0:T(8,128)(2,1)}, bf16[2,192,128]{2,1,0:T(8,128)(2,1)S(1)}, u32[]{:S(2)}, u32[]{:S(2)}) collective-permute-start(bf16[2,192,128]{2,1,0:T(8,128)(2,1)} %get-tuple-element.19), channel_id=1, source_target_pairs={{1,0},{2,1},{3,2},{4,3},{5,4},{6,5},{7,6},{0,7},{9,8},{10,9},{11,1... | collective-permute-start | bytes 294920 | tf_op jit(solution)/shard_map/ppermute | solution.py:367
  136.0 2.5 %collective-permute-done.5.refs_2_ = bf16[2,192,128]{2,1,0:T(8,128)(2,1)S(1)} collective-permute-done((bf16[2,192,128]{2,1,0:T(8,128)(2,1)}, bf16[2,192,128]{2,1,0:T(8,128)(2,1)S(1)}, u32[]{:S(2)}, u32[]{:S(2)}) %collective-permute-start.5) | collective-permute-done | bytes 98336 | tf_op jit(solution)/shard_map/ppermute | solution.py:367
  138.5 2.7 %collective-permute-done.4.refs_1_ = bf16[2,192,128]{2,1,0:T(8,128)(2,1)S(1)} collective-permute-done((bf16[2,192,128]{2,1,0:T(8,128)(2,1)}, bf16[2,192,128]{2,1,0:T(8,128)(2,1)S(1)}, u32[]{:S(2)}, u32[]{:S(2)}) %collective-permute-start.4) | collective-permute-done | bytes 98336 | tf_op jit(solution)/shard_map/ppermute | solution.py:366
  141.2 4.4 %collective-permute-start.10 = (bf16[5,192,128]{2,1,0:T(8,128)(2,1)S(1)}, bf16[5,192,128]{2,1,0:T(8,128)(2,1)S(1)}, u32[]{:S(2)}, u32[]{:S(2)}) collective-permute-start(bf16[5,192,128]{2,1,0:T(8,128)(2,1)S(1)} %pad_maximum_fusion.2), channel_id=1, source_target_pairs={{0,8},{8,16},{16,24},{1,9},{9,17},{17,25},{2,10},{10,18},{18,26},{... | collective-permute-start | bytes 737288 | tf_op jit(solution)/shard_map/ppermute | solution.py:376
  145.7 1.5 collective-permute-start.11
  147.9 19.4 %block.3 = (bf16[32,192,128]{2,1,0:T(8,128)(2,1)}, bf16[2,192,128]{2,1,0:T(8,128)(2,1)}) custom-call(bf16[40,192,128]{2,1,0:T(8,128)(2,1)} %get-tuple-element.16.refs_0_, bf16[3,192,128]{2,1,0:T(8,128)(2,1)} %copy-done.6, bf16[3,192,128]{2,1,0:T(8,128)(2,1)} %copy-done.5, bf16[24,192,128]{2,1,0:T(8,128)(2,1)} %get-tuple-element.21.refs_3_, ...), custom_call_target="tpu_custom_call" | custom-call | flops 2944401408 | bytes 15728640 | tf_op jit(solution)/shard_map/block/pallas_call | solution.py:260
  169.5 1.1 broadcast_in_dim.93.refs_8_.refs_9_
  170.6 1.2 broadcast_in_dim.91.refs_7_.refs_8_
  171.8 1.2 broadcast_in_dim.89.refs_6_.refs_7_
  173.0 13.7 %block_head.2.refs_17_ = f32[128,64,128]{2,1,0:T(8,128)} custom-call(bf16[32,192,128]{2,1,0:T(8,128)(2,1)} %get-tuple-element.18.refs_0_, bf16[2,192,128]{2,1,0:T(8,128)(2,1)} %copy-done.3, bf16[2,192,128]{2,1,0:T(8,128)(2,1)} %copy-done.2, bf16[5,192,128]{2,1,0:T(8,128)(2,1)} %copy-done.7, bf16[5,192,128]{2,1,0:T(8,128)(2,1)} %copy-done.8, ...), custom_call_target="tpu_custom_call" | custom-call | flops 1384120320 | bytes 7864320 | tf_op jit(solution)/shard_map/block_head/pallas_call | solution.py:281
  187.3 27.4 %block_head.3 = f32[128,64,128]{2,1,0:T(8,128)} custom-call(bf16[32,192,128]{2,1,0:T(8,128)(2,1)} %get-tuple-element.18.refs_0_, bf16[2,192,128]{2,1,0:T(8,128)(2,1)} %copy-done.3, bf16[2,192,128]{2,1,0:T(8,128)(2,1)} %copy-done.2, bf16[32,192,128]{2,1,0:T(8,128)(2,1)} %get-tuple-element.23.refs_3_, ...), custom_call_target="tpu_custom_call", output_to_operand_aliasing={{}: (17, {})} | custom-call | flops 4680843264 | bytes 23592960 | tf_op jit(solution)/shard_map/block_head/pallas_call | solution.py:281
  (106 shorter events, 16.3 us)
Async XLA Ops:
  5.7 7.3 %copy-start.15 = (f32[2,768]{1,0:T(2,128)S(1)}, f32[2,768]{1,0:T(2,128)}, u32[]{:S(2)}) copy-start(f32[2,768]{1,0:T(2,128)} %param.25) | copy-start | bytes 18436
  5.7 7.8 %copy-start.4 = (bf16[2,192,768]{2,1,0:T(8,128)(2,1)S(1)}, bf16[2,192,768]{2,1,0:T(8,128)(2,1)}, u32[]{:S(2)}) copy-start(bf16[2,192,768]{2,1,0:T(8,128)(2,1)} %param.24) | copy-start | bytes 1769476
  5.7 40.5 %all-to-all-start = ((bf16[32,4,40,128]{3,2,1,0:T(8,128)(2,1)}), bf16[32,4,40,128]{3,2,1,0:T(8,128)(2,1)S(1)}, u32[]{:S(2)}, u32[]{:S(2)}) async-start(bf16[32,4,40,128]{3,2,1,0:T(8,128)(2,1)} %bitcast.72), calls=%async_computation | async-start | bytes 2621440 | tf_op jit(solution)/shard_map/all_to_all | solution.py:323
  13.1 1.7 copy-start.16
  13.1 1.7 copy-start.18
  13.1 1.7 copy-start.9
  14.9 34.8 %copy-start.21 = (f32[192]{0:T(256)S(1)}, f32[192]{0:T(256)}, u32[]{:S(2)}) copy-start(f32[192]{0:T(256)} %param.19) | copy-start | bytes 2308
  46.2 4.3 %copy-start = (bf16[32,4,40,128]{3,2,1,0:T(8,128)(2,1)}, bf16[32,4,40,128]{3,2,1,0:T(8,128)(2,1)S(1)}, u32[]{:S(2)}) copy-start(bf16[32,4,40,128]{3,2,1,0:T(8,128)(2,1)S(1)} %all-to-all-done) | copy-start | bytes 3932164
  46.2 56.4 %all-to-all-start.1 = ((bf16[32,4,24,128]{3,2,1,0:T(8,128)(2,1)}), bf16[32,4,24,128]{3,2,1,0:T(8,128)(2,1)S(1)}, u32[]{:S(2)}, u32[]{:S(2)}) async-start(bf16[32,4,24,128]{3,2,1,0:T(8,128)(2,1)} %bitcast.16), calls=%async_computation.1 | async-start | bytes 1572864 | tf_op jit(solution)/shard_map/all_to_all | solution.py:323
  54.1 11.2 %collective-permute-start.1 = (bf16[3,192,128]{2,1,0:T(8,128)(2,1)}, bf16[3,192,128]{2,1,0:T(8,128)(2,1)S(1)}, u32[]{:S(2)}, u32[]{:S(2)}) collective-permute-start(bf16[3,192,128]{2,1,0:T(8,128)(2,1)} %get-tuple-element.17), channel_id=1, source_target_pairs={{1,0},{2,1},{3,2},{4,3},{5,4},{6,5},{7,6},{0,7},{9,8},{10,9},{11,1... | collective-permute-start | bytes 442376 | tf_op jit(solution)/shard_map/ppermute | solution.py:367
  57.5 11.4 %collective-permute-start = (bf16[3,192,128]{2,1,0:T(8,128)(2,1)}, bf16[3,192,128]{2,1,0:T(8,128)(2,1)S(1)}, u32[]{:S(2)}, u32[]{:S(2)}) collective-permute-start(bf16[3,192,128]{2,1,0:T(8,128)(2,1)} %get-tuple-element.17), channel_id=1, source_target_pairs={{0,1},{1,2},{2,3},{3,4},{4,5},{5,6},{6,7},{7,0},{8,9},{9,10},{10,1... | collective-permute-start | bytes 442376 | tf_op jit(solution)/shard_map/ppermute | solution.py:366
  65.3 15.5 %copy-start.5 = (bf16[3,192,128]{2,1,0:T(8,128)(2,1)}, bf16[3,192,128]{2,1,0:T(8,128)(2,1)S(1)}, u32[]{:S(2)}) copy-start(bf16[3,192,128]{2,1,0:T(8,128)(2,1)S(1)} %collective-permute-done.1.refs_2_) | copy-start | bytes 442372
  68.9 12.0 %copy-start.6 = (bf16[3,192,128]{2,1,0:T(8,128)(2,1)}, bf16[3,192,128]{2,1,0:T(8,128)(2,1)S(1)}, u32[]{:S(2)}) copy-start(bf16[3,192,128]{2,1,0:T(8,128)(2,1)S(1)} %collective-permute-done.refs_1_) | copy-start | bytes 442372
  68.9 37.9 %collective-permute-start.2 = (bf16[5,192,128]{2,1,0:T(8,128)(2,1)S(1)}, bf16[5,192,128]{2,1,0:T(8,128)(2,1)S(1)}, u32[]{:S(2)}, u32[]{:S(2)}) collective-permute-start(bf16[5,192,128]{2,1,0:T(8,128)(2,1)S(1)} %pad_maximum_fusion), channel_id=1, source_target_pairs={{0,8},{8,16},{16,24},{1,9},{9,17},{17,25},{2,10},{10,18},{18,26},{... | collective-permute-start | bytes 737288 | tf_op jit(solution)/shard_map/ppermute | solution.py:376
  72.4 34.5 %collective-permute-start.3 = (bf16[5,192,128]{2,1,0:T(8,128)(2,1)S(1)}, bf16[5,192,128]{2,1,0:T(8,128)(2,1)S(1)}, u32[]{:S(2)}, u32[]{:S(2)}) collective-permute-start(bf16[5,192,128]{2,1,0:T(8,128)(2,1)S(1)} %pad_maximum_fusion.1), channel_id=1, source_target_pairs={{8,0},{16,8},{24,16},{9,1},{17,9},{25,17},{10,2},{18,10},{26,18},{... | collective-permute-start | bytes 737288 | tf_op jit(solution)/shard_map/ppermute | solution.py:377
  80.8 6.1 %copy-start.14 = (bf16[192,128]{1,0:T(8,128)(2,1)S(1)}, bf16[192,128]{1,0:T(8,128)(2,1)}, u32[]{:S(2)}) copy-start(bf16[192,128]{1,0:T(8,128)(2,1)} %param.29) | copy-start | bytes 147460
  93.7 8.9 %copy-start.19 = (f32[2,192]{1,0:T(2,128)S(1)}, f32[2,192]{1,0:T(2,128)}, u32[]{:S(2)}) copy-start(f32[2,192]{1,0:T(2,128)} %param.27) | copy-start | bytes 4612
  93.7 8.9 %copy-start.20 = (f32[2,192]{1,0:T(2,128)S(1)}, f32[2,192]{1,0:T(2,128)}, u32[]{:S(2)}) copy-start(f32[2,192]{1,0:T(2,128)} %param.28) | copy-start | bytes 4612
  106.3 40.9 %collective-permute-start.7 = (bf16[2,192,128]{2,1,0:T(8,128)(2,1)}, bf16[2,192,128]{2,1,0:T(8,128)(2,1)S(1)}, u32[]{:S(2)}, u32[]{:S(2)}) collective-permute-start(bf16[2,192,128]{2,1,0:T(8,128)(2,1)} %get-tuple-element.22), channel_id=1, source_target_pairs={{1,0},{2,1},{3,2},{4,3},{5,4},{6,5},{7,6},{0,7},{9,8},{10,9},{11,1... | collective-permute-start | bytes 294920 | tf_op jit(solution)/shard_map/ppermute | solution.py:367
  106.5 40.8 %collective-permute-start.6 = (bf16[2,192,128]{2,1,0:T(8,128)(2,1)}, bf16[2,192,128]{2,1,0:T(8,128)(2,1)S(1)}, u32[]{:S(2)}, u32[]{:S(2)}) collective-permute-start(bf16[2,192,128]{2,1,0:T(8,128)(2,1)} %get-tuple-element.22), channel_id=1, source_target_pairs={{0,1},{1,2},{2,3},{3,4},{4,5},{5,6},{6,7},{7,0},{8,9},{9,10},{10,1... | collective-permute-start | bytes 294920 | tf_op jit(solution)/shard_map/ppermute | solution.py:366
  106.9 5.8 %copy-start.22 = (bf16[5,192,128]{2,1,0:T(8,128)(2,1)}, bf16[5,192,128]{2,1,0:T(8,128)(2,1)S(1)}, u32[]{:S(2)}) copy-start(bf16[5,192,128]{2,1,0:T(8,128)(2,1)S(1)} %collective-permute-done.2.refs_3_) | copy-start | bytes 737284
  106.9 5.8 %copy-start.23 = (bf16[5,192,128]{2,1,0:T(8,128)(2,1)}, bf16[5,192,128]{2,1,0:T(8,128)(2,1)S(1)}, u32[]{:S(2)}) copy-start(bf16[5,192,128]{2,1,0:T(8,128)(2,1)S(1)} %collective-permute-done.3.refs_4_) | copy-start | bytes 737284
  131.8 6.6 %collective-permute-start.5 = (bf16[2,192,128]{2,1,0:T(8,128)(2,1)}, bf16[2,192,128]{2,1,0:T(8,128)(2,1)S(1)}, u32[]{:S(2)}, u32[]{:S(2)}) collective-permute-start(bf16[2,192,128]{2,1,0:T(8,128)(2,1)} %get-tuple-element.19), channel_id=1, source_target_pairs={{1,0},{2,1},{3,2},{4,3},{5,4},{6,5},{7,6},{0,7},{9,8},{10,9},{11,1... | collective-permute-start | bytes 294920 | tf_op jit(solution)/shard_map/ppermute | solution.py:367
  135.0 6.2 %collective-permute-start.4 = (bf16[2,192,128]{2,1,0:T(8,128)(2,1)}, bf16[2,192,128]{2,1,0:T(8,128)(2,1)S(1)}, u32[]{:S(2)}, u32[]{:S(2)}) collective-permute-start(bf16[2,192,128]{2,1,0:T(8,128)(2,1)} %get-tuple-element.19), channel_id=1, source_target_pairs={{0,1},{1,2},{2,3},{3,4},{4,5},{5,6},{6,7},{7,0},{8,9},{9,10},{10,1... | collective-permute-start | bytes 294920 | tf_op jit(solution)/shard_map/ppermute | solution.py:366
  138.5 28.8 %copy-start.2 = (bf16[2,192,128]{2,1,0:T(8,128)(2,1)}, bf16[2,192,128]{2,1,0:T(8,128)(2,1)S(1)}, u32[]{:S(2)}) copy-start(bf16[2,192,128]{2,1,0:T(8,128)(2,1)S(1)} %collective-permute-done.5.refs_2_) | copy-start | bytes 294916
  141.2 26.1 %copy-start.3 = (bf16[2,192,128]{2,1,0:T(8,128)(2,1)}, bf16[2,192,128]{2,1,0:T(8,128)(2,1)S(1)}, u32[]{:S(2)}) copy-start(bf16[2,192,128]{2,1,0:T(8,128)(2,1)S(1)} %collective-permute-done.4.refs_1_) | copy-start | bytes 294916
  141.2 26.7 %collective-permute-start.10 = (bf16[5,192,128]{2,1,0:T(8,128)(2,1)S(1)}, bf16[5,192,128]{2,1,0:T(8,128)(2,1)S(1)}, u32[]{:S(2)}, u32[]{:S(2)}) collective-permute-start(bf16[5,192,128]{2,1,0:T(8,128)(2,1)S(1)} %pad_maximum_fusion.2), channel_id=1, source_target_pairs={{0,8},{8,16},{16,24},{1,9},{9,17},{17,25},{2,10},{10,18},{18,26},{... | collective-permute-start | bytes 737288 | tf_op jit(solution)/shard_map/ppermute | solution.py:376
  145.7 22.3 %collective-permute-start.11 = (bf16[5,192,128]{2,1,0:T(8,128)(2,1)S(1)}, bf16[5,192,128]{2,1,0:T(8,128)(2,1)S(1)}, u32[]{:S(2)}, u32[]{:S(2)}) collective-permute-start(bf16[5,192,128]{2,1,0:T(8,128)(2,1)S(1)} %pad_maximum_fusion.3), channel_id=1, source_target_pairs={{8,0},{16,8},{24,16},{9,1},{17,9},{25,17},{10,2},{18,10},{26,18},{... | collective-permute-start | bytes 737288 | tf_op jit(solution)/shard_map/ppermute | solution.py:377
  167.3 19.4 %collective-permute-start.9 = (bf16[2,192,128]{2,1,0:T(8,128)(2,1)}, bf16[2,192,128]{2,1,0:T(8,128)(2,1)S(1)}, u32[]{:S(2)}, u32[]{:S(2)}) collective-permute-start(bf16[2,192,128]{2,1,0:T(8,128)(2,1)} %get-tuple-element.24), channel_id=1, source_target_pairs={{1,0},{2,1},{3,2},{4,3},{5,4},{6,5},{7,6},{0,7},{9,8},{10,9},{11,1... | collective-permute-start | bytes 294920 | tf_op jit(solution)/shard_map/ppermute | solution.py:367
  167.9 18.7 %collective-permute-start.8 = (bf16[2,192,128]{2,1,0:T(8,128)(2,1)}, bf16[2,192,128]{2,1,0:T(8,128)(2,1)S(1)}, u32[]{:S(2)}, u32[]{:S(2)}) collective-permute-start(bf16[2,192,128]{2,1,0:T(8,128)(2,1)} %get-tuple-element.24), channel_id=1, source_target_pairs={{0,1},{1,2},{2,3},{3,4},{4,5},{5,6},{6,7},{7,0},{8,9},{9,10},{10,1... | collective-permute-start | bytes 294920 | tf_op jit(solution)/shard_map/ppermute | solution.py:366
  167.9 5.0 %copy-start.7 = (bf16[5,192,128]{2,1,0:T(8,128)(2,1)}, bf16[5,192,128]{2,1,0:T(8,128)(2,1)S(1)}, u32[]{:S(2)}) copy-start(bf16[5,192,128]{2,1,0:T(8,128)(2,1)S(1)} %collective-permute-done.10.refs_3_) | copy-start | bytes 737284
  168.0 5.0 %copy-start.8 = (bf16[5,192,128]{2,1,0:T(8,128)(2,1)}, bf16[5,192,128]{2,1,0:T(8,128)(2,1)S(1)}, u32[]{:S(2)}) copy-start(bf16[5,192,128]{2,1,0:T(8,128)(2,1)S(1)} %collective-permute-done.11.refs_4_) | copy-start | bytes 737284
  (6 other events, 5.2 us)

commit v2 on v0

v2 whole, which is shorter than its diff:
```python
import functools

import jax
import jax.numpy as jnp
import numpy as np
from jax import lax
from jax.experimental import pallas as pl
from jax.experimental.pallas import tpu as pltpu
from jax.sharding import PartitionSpec as P

ln_eps = 1e-06
f32 = jnp.float32
bf16 = jnp.bfloat16
lanes = 128
half = lanes // 2
mib = 2**20


halo_chunk = -1


def window_of(span):
    per = span // 16
    even, odd = list(range(per)), list(range(per, 2 * per))
    order = []
    for s in range(-2, 3):
        chunks = (even if s > -2 else []) + (odd if s < 2 else []) + [halo_chunk]
        order += [(s, c) for c in chunks]
    return order


def window_tables(span):
    per = span // 16
    cols, rows = [], []
    for s, c in window_of(span):
        if c == halo_chunk:
            for phase in range(2):
                cols += [2 * s + phase] * 8
                rows += [-3, -2, -1, span, span + 1, span + 2, 10000, 10000]
        else:
            cols += [2 * s + c // per] * 16
            rows += [16 * (c % per) + q for q in range(16)]
    return np.array([cols], np.int32), np.array([rows], np.int32)


def params_for(vmem, flops=0, bytes_accessed=0):
    return dict(
        compiler_params=pltpu.CompilerParams(vmem_limit_bytes=vmem * mib),
        cost_estimate=pl.CostEstimate(
            flops=int(flops), bytes_accessed=int(bytes_accessed), transcendentals=0
        ),
    )


def lane_index(shape):
    return lax.broadcasted_iota(jnp.int32, shape, len(shape) - 1)


def row_index(shape):
    return lax.broadcasted_iota(jnp.int32, shape, 0)


def turn(x, amount):
    amount %= lanes
    return pltpu.roll(x, amount, 1) if amount else x


def prep_body(q_ref, s_ref, o_ref):
    channels, rows, cols = q_ref.shape
    tiles = cols // lanes
    span = rows // 2
    shape = (lanes, 2 * lanes)
    to = lane_index(shape)
    at = to & (lanes - 1)
    phase = (at >> 6) ^ (to >> 7)
    order = (row_index(shape) == 2 * (at & (half - 1)) + phase).astype(f32).astype(bf16)
    left = lane_index((span, lanes)) < half
    for c in range(channels):
        scale = jnp.broadcast_to(s_ref[:, c : c + 1], (rows, lanes))
        x = jnp.concatenate(
            [
                (q_ref[c, :, b * lanes : (b + 1) * lanes].astype(f32) * scale).astype(bf16)
                for b in range(tiles)
            ],
            axis=0,
        )
        y = jnp.dot(x, order, preferred_element_type=f32)
        for b in range(tiles):
            top = y[b * rows : b * rows + span]
            low = y[b * rows + span : (b + 1) * rows]
            o_ref[0, b, c, 0:span] = jnp.where(left, top[:, :lanes], low[:, lanes:]).astype(bf16)
            o_ref[0, b, c, span:rows] = jnp.where(left, top[:, lanes:], low[:, :lanes]).astype(bf16)


def prep(q_state, scales, n_lat, n_lon, rows):
    channels, n_rows, n_cols = q_state.shape
    return pl.pallas_call(
        prep_body,
        grid=(n_lat,),
        in_specs=[
            pl.BlockSpec((channels, rows, n_cols), lambda a: (0, a, 0)),
            pl.BlockSpec((rows, channels), lambda a: (a, 0)),
        ],
        out_specs=pl.BlockSpec((1, n_lon, channels, rows, lanes), lambda a: (a, 0, 0, 0, 0)),
        out_shape=jax.ShapeDtypeStruct((n_lat, n_lon, channels, rows, lanes), bf16),
        name="dequantize",
        **params_for(20, 0, 4 * q_state.size),
    )(q_state, scales.T).reshape(n_lat * n_lon, channels, rows, lanes)


def slot_of(shape):
    return ((lane_index(shape) + 2) >> 2) & 15


def pack_edges(packed, lead, slot):
    turned = turn(lead, 4 * slot)
    return jnp.where(slot_of(lead.shape) == slot, turned, packed)


def first_ends(shape):
    return ((lane_index(shape) + 2) & 3) >= 2


def messages(f_ref, e_ref, west_ref, east_ref, south_ref, north_ref):
    shape = f_ref.shape[1:]
    span = f_ref.shape[0] // 2
    first = first_ends(shape)
    for i in range(e_ref.shape[0] // 2):
        one, two = e_ref[2 * i], e_ref[2 * i + 1]
        west_ref[i] = jnp.where(first, one, turn(two, -2))
        east_ref[i] = jnp.where(first, turn(two, 2), one)
    left = lane_index(shape) < half
    for i in range(3):
        r = span - 3 + i
        south_ref[i] = jnp.where(left, turn(f_ref[r], half), f_ref[span + r])
        north_ref[i] = jnp.where(left, f_ref[i], turn(f_ref[span + i], half))


def received_ends(from_west, from_east):
    first = first_ends(from_west[0].shape)
    groups = []
    for west, east in zip(from_west, from_east):
        groups.append(jnp.where(first, east, west))
        groups.append(jnp.where(first, turn(east, 2), turn(west, -2)))
    return groups


def rows_body(west_in, east_in, south_in, north_in, south_ref, north_ref):
    count = west_in.shape[0]
    groups = received_ends([west_in[i] for i in range(count)], [east_in[i] for i in range(count)])
    slot = slot_of(groups[0].shape)
    south_ref[0:3] = south_in[...]
    north_ref[0:3] = north_in[...]
    south_ref[3] = jnp.where(slot > 11, groups[count - 1], turn(groups[2 * count - 1], -32))
    north_ref[3] = jnp.where(slot < 4, groups[0], turn(groups[count], 32))


def rows_with_ends(from_west, from_east, to_south, to_north):
    shape = jax.ShapeDtypeStruct((4, *to_south.shape[1:]), bf16)
    return pl.pallas_call(
        rows_body,
        out_shape=[shape, shape],
        name="rows",
        **params_for(20, 0, 20 * to_south.size),
    )(from_west, from_east, to_south, to_north)


def stem_body(x_ref, w_ref, wide_ref, mask_ref, f_ref, west_ref, east_ref, south_ref, north_ref, e_ref):
    bias = wide_ref[4]
    for g in range(x_ref.shape[1] // 16):
        x = jnp.swapaxes(x_ref[:, 16 * g : 16 * g + 16, :], 0, 1)
        packed = jnp.zeros(f_ref.shape[1:], bf16)
        for first in (0, 8):
            joined = jnp.concatenate([x[first + i] for i in range(8)], axis=1)
            y = jnp.dot(w_ref[...], joined, preferred_element_type=f32)
            for i in range(8):
                at = 16 * g + first + i
                value = (y[:, i * lanes : (i + 1) * lanes] + bias) * mask_ref[at : at + 1, :]
                value = value.astype(bf16)
                f_ref[at] = value
                packed = pack_edges(packed, value, first + i)
        e_ref[g] = packed
    messages(f_ref, e_ref, west_ref, east_ref, south_ref, north_ref)


def feature_shapes(leads, d):
    return [
        jax.ShapeDtypeStruct((n, d, lanes), bf16) for n in (leads, leads // 32, leads // 32, 3, 3)
    ]


def stem(state, weight_t, wide, mask):
    d = weight_t.shape[0]
    leads = state.shape[1]
    return pl.pallas_call(
        stem_body,
        out_shape=feature_shapes(leads, d),
        scratch_shapes=[pltpu.VMEM((leads // 16, d, lanes), bf16)],
        name="stem",
        **params_for(20, 2 * d * state.size, 2 * state.size + 2 * leads * d * lanes),
    )(state, weight_t, wide, mask)


def band_body(w_ref, col_ref, row_ref, o_ref):
    k = o_ref.shape[2]
    taps = w_ref.shape[1]
    at = row_index((taps, k))
    made = []
    for q in range(16):
        i = row_ref[...] - (8 * pl.program_id(0) + q % 8) + 3
        j = col_ref[...] - q // 8 + 3
        tap = jnp.where((i >= 0) & (i < 7) & (j >= 0) & (j < 7), 7 * i + j, -1)
        pick = (at == tap).astype(f32).astype(bf16)
        made.append(jnp.dot(w_ref[...], pick, preferred_element_type=f32).astype(bf16))
    o_ref[...] = jnp.swapaxes(jnp.stack(made), 0, 1)


def band(dw, span):
    d = dw.shape[0]
    cols, rows = window_tables(span)
    k = cols.shape[1]
    taps = jnp.pad(dw.reshape(d, 49), ((0, 0), (0, 15))).astype(bf16)
    return pl.pallas_call(
        band_body,
        grid=(span // 8,),
        in_specs=[
            pl.BlockSpec((d, 64), lambda u: (0, 0)),
            pl.BlockSpec((1, k), lambda u: (0, 0)),
            pl.BlockSpec((1, k), lambda u: (0, 0)),
        ],
        out_specs=pl.BlockSpec((d, 16, k), lambda u: (0, u, 0)),
        out_shape=jax.ShapeDtypeStruct((d, 2 * span, k), bf16),
        name="bands",
        **params_for(20, 0, 4 * d * span * k),
    )(taps, jnp.asarray(cols), jnp.asarray(rows))


def block_body(index, head, *refs):
    f_in, west_in, east_in, north_in, south_in, band_ref = refs[:6]
    thin_ref, wide_ref, w1_ref, w2_ref, mask_ref, edge_ref = refs[6:12]
    refs = refs[12:]
    if head:
        head_ref, out_ref, conv_ref, held_ref, band_sems, tend_ref, sems = refs
    else:
        f_ref, *sent_refs, conv_ref, held_ref, band_sems, e_ref = refs
    leads, d = f_in.shape[:2]
    span = leads // 2
    per = span // 16

    def fetch(g):
        cs = pl.ds(g * 16, 16)
        return pltpu.make_async_copy(band_ref.at[cs], held_ref.at[cs], band_sems.at[g])

    for g in range(d // 16):
        fetch(g).start()

    small = (16, lanes)
    left = lane_index(small) < half
    place = lane_index(small) & (half - 1)

    def conv_step(g, _):
        cs = pl.ds(pl.multiple_of(g * 16, 16), 16)
        fetch(g).wait()
        zero = jnp.zeros(small, bf16)

        def ends(group, slot):
            return turn(group, half - 4 * slot)

        count = leads // 32
        packs = received_ends(
            [west_in[i, cs, :] for i in range(count)], [east_in[i, cs, :] for i in range(count)]
        )
        norths = [north_in[i, cs, :] * edge_ref[0] for i in range(4)]
        souths = [south_in[i, cs, :] * edge_ref[1] for i in range(4)]
        chunks = {}
        for k in range(leads // 16):
            x = jnp.stack([f_in[16 * k + q, cs, :] for q in range(16)])
            h = jnp.stack([ends(packs[k], q) for q in range(16)])
            chunks[k] = (jnp.swapaxes(x, 0, 1), jnp.swapaxes(h, 0, 1))
        xrow, hrow = [], []
        for phase in range(2):
            for i in range(3):
                r = span - 3 + i
                own = f_in[phase * span + r, cs, :]
                got = norths[i]
                if phase == 0:
                    xrow.append(jnp.where(left, got, turn(own, half)))
                else:
                    xrow.append(turn(jnp.where(left, own, got), half))
                slot = r % 16
                mine = ends(packs[phase * per + r // 16], slot)
                theirs = ends(norths[3], slot - 8 * phase)
                hrow.append(turn(jnp.where(left, theirs, mine), half))
            for i in range(3):
                own = f_in[phase * span + i, cs, :]
                got = souths[i]
                if phase == 0:
                    xrow.append(turn(jnp.where(left, got, own), half))
                else:
                    xrow.append(jnp.where(left, turn(own, half), got))
                mine = ends(packs[phase * per], i)
                theirs = ends(souths[3], i + 8 * phase)
                hrow.append(turn(jnp.where(left, mine, theirs), half))
            xrow += [zero, zero]
            hrow += [zero, zero]
        chunks[halo_chunk] = tuple(jnp.swapaxes(jnp.stack(v), 0, 1) for v in (xrow, hrow))
        for u in range(16):
            taps = []
            for s, c in window_of(span):
                x, h = chunks[c][0][u], chunks[c][1][u]
                if s:
                    past = (place < s) if s > 0 else (place >= half + s)
                    x = turn(jnp.where(past, h, x), -s)
                taps.append(x)
            taps = jnp.concatenate(taps, axis=0)
            conv_ref[g * 16 + u] = jnp.dot(held_ref[g * 16 + u], taps, preferred_element_type=f32)
        return 0

    lax.fori_loop(0, d // 16, conv_step, 0)

    if head:
        shape = (2 * lanes, 2 * lanes)
        to, at = lane_index(shape), row_index(shape)
        col = to & (lanes - 1)
        source = (col & 1) * lanes + (to >> 7) * half + (col >> 1)
        back = (at == source).astype(f32).astype(bf16)
    ones = (row_index((16, 8 * lanes)) < 3).astype(f32).astype(bf16)
    dwb, gain, lnb = (thin_ref.at[3 * index + i] for i in range(3))
    ls, lsb = wide_ref[2 * index], wide_ref[2 * index + 1]
    held = []
    for k in range(leads // 8):
        u, phase = k // 2, k % 2
        lead = phase * span + 8 * u
        y = conv_ref[:, 8 * k : 8 * k + 8, :] + dwb[...]
        average = jnp.sum(y, axis=0, keepdims=True) * (1.0 / d)
        centered = y - average
        variance = jnp.sum(centered * centered, axis=0, keepdims=True) * (1.0 / d)
        normed = centered * lax.rsqrt(variance + ln_eps) * gain[...] + lnb[...]
        normed = jnp.swapaxes(normed, 0, 1).astype(bf16)
        joined = jnp.concatenate([normed[i] for i in range(8)], axis=1)
        joined = jnp.concatenate([joined, ones], axis=0)
        hidden = jnp.dot(w1_ref[...], joined, preferred_element_type=f32)
        hidden = (hidden + hidden * lax.erf(hidden * 0.7071067811865476)).astype(bf16)
        projected = jnp.dot(w2_ref[...], hidden, preferred_element_type=f32)
        if not head:
            packed = jnp.zeros((d, lanes), bf16) if lead % 16 == 0 else e_ref[lead // 16]
        for i in range(8):
            ocean = mask_ref[lead + i : lead + i + 1, :]
            branch = projected[:, i * lanes : (i + 1) * lanes] * ls + lsb
            value = ((f_in[lead + i].astype(f32) + branch) * ocean).astype(bf16)
            if head:
                held.append(value)
            else:
                f_ref[lead + i] = value
                packed = pack_edges(packed, value, (lead + i) % 16)
        if not head:
            e_ref[lead // 16] = packed
        elif phase == 1:
            both = [jnp.concatenate([held[i], held[8 + i]], axis=1) for i in range(8)]
            both = jnp.dot(jnp.concatenate(both, axis=0), back, preferred_element_type=f32)
            both = both.astype(bf16)
            for part in range(2):
                cut = slice(part * lanes, (part + 1) * lanes)
                joined = jnp.concatenate([both[i * d : (i + 1) * d, cut] for i in range(8)], axis=1)
                t = jnp.dot(head_ref[...], joined, preferred_element_type=f32)
                t = jnp.stack([t[:, i * lanes : (i + 1) * lanes] for i in range(8)])
                at = part * span + 8 * u
                tend_ref[:, at : at + 8, :] = jnp.swapaxes(t, 0, 1)
                cut = pl.ds(at, 8)
                pltpu.make_async_copy(
                    tend_ref.at[:, cut, :], out_ref.at[:, cut, :], sems.at[at // 8]
                ).start()
            held = []
    if head:
        for at in range(0, leads, 8):
            cut = pl.ds(at, 8)
            pltpu.make_async_copy(
                tend_ref.at[:, cut, :], out_ref.at[:, cut, :], sems.at[at // 8]
            ).wait()
    else:
        messages(f_ref, e_ref, *sent_refs)


def block(index, feats, bands, params, head=None):
    d, leads, k = bands.shape
    hid = params[2].shape[0]
    flops = 2 * leads * lanes * (2 * d * hid + d * k)
    operands = [*feats, bands, *params]
    vmem = pl.BlockSpec(memory_space=pltpu.VMEM)
    anywhere = pl.BlockSpec(memory_space=pl.ANY)
    specs = [vmem] * len(feats) + [anywhere] + [vmem] * len(params)
    scratch = [
        pltpu.VMEM((d, leads, lanes), f32),
        pltpu.VMEM(bands.shape, bf16),
        pltpu.SemaphoreType.DMA((d // 16,)),
    ]
    if head is None:
        return pl.pallas_call(
            functools.partial(block_body, index, False),
            out_shape=feature_shapes(leads, d),
            in_specs=specs,
            scratch_shapes=scratch + [pltpu.VMEM((leads // 16, d, lanes), bf16)],
            name="block",
            **params_for(44, flops, 20 * leads * d * lanes),
        )(*operands)
    c_out = head.shape[0]
    scratch += [pltpu.VMEM((c_out, leads, lanes), f32), pltpu.SemaphoreType.DMA((leads // 8,))]
    return pl.pallas_call(
        functools.partial(block_body, index, True),
        out_shape=jax.ShapeDtypeStruct((c_out, leads, lanes), f32),
        in_specs=specs + [vmem],
        out_specs=anywhere,
        scratch_shapes=scratch,
        name="block_head",
        **params_for(44, flops, 20 * leads * d * lanes),
    )(*operands, head)


def body(
    q_state,
    scales,
    land_mask,
    stem_weight,
    stem_bias,
    dw_weight,
    dw_bias,
    ln_gain,
    ln_bias,
    w_in,
    b_in,
    w_out,
    b_out,
    layer_scale,
    head_weight,
):
    n_lat = lax.axis_size("lat")
    n_lon = lax.axis_size("lon")
    rows = land_mask.shape[0]
    span = rows // 2
    axes = ("lat", "lon")

    send = prep(q_state, scales, n_lat, n_lon, rows)
    state = lax.all_to_all(send, axes, split_axis=0, concat_axis=0, tiled=True)
    state = state.reshape(-1, rows, lanes)

    mask = land_mask.astype(f32).reshape(2, span, half, 2).transpose(3, 1, 0, 2)
    mask = mask.reshape(rows, lanes)
    d = stem_weight.shape[1]
    thin = jnp.stack([dw_bias, ln_gain, ln_bias], axis=1).reshape(6, d)
    thin = jnp.broadcast_to(thin[:, :, None, None], (6, d, 1, lanes))
    wide = jnp.stack([layer_scale * 0.5, layer_scale * b_out], axis=1).reshape(4, d)
    wide = jnp.concatenate([wide, stem_bias[None]], axis=0)
    wide = jnp.broadcast_to(wide[:, :, None], (5, d, lanes))
    high = b_in.astype(bf16)
    rest = b_in - high.astype(f32)
    mid = rest.astype(bf16)
    low = (rest - mid.astype(f32)).astype(bf16)
    terms = jnp.pad(jnp.stack([high, mid, low], axis=2), ((0, 0), (0, 0), (0, 13)))
    w1 = jnp.concatenate([w_in.transpose(0, 2, 1), terms], axis=2)
    w2 = w_out.transpose(0, 2, 1)
    band_at = lax.axis_index("lat")
    edge = jnp.stack([band_at > 0, band_at < n_lat - 1]).astype(bf16)
    edge = jnp.broadcast_to(edge[:, None, None], (2, 16, lanes))
    dw_weight, ready = lax.optimization_barrier(
        (dw_weight, (thin, wide, w1, w2, stem_weight.T, mask, edge, head_weight.T))
    )
    bands = [band(dw_weight[b], span) for b in range(2)]
    state, bands, (thin, wide, w1, w2, weight_t, mask, edge, head_t) = lax.optimization_barrier(
        (state, bands, ready)
    )

    def shift(x, axis, by):
        n = lax.axis_size(axis)
        return lax.ppermute(x, axis, [(i, (i + by) % n) for i in range(n)])

    def exchange(feat, to_west, to_east, to_south, to_north):
        from_west, from_east = shift(to_east, "lon", 1), shift(to_west, "lon", -1)
        to_south, to_north = rows_with_ends(from_west, from_east, to_south, to_north)
        return feat, from_west, from_east, shift(to_south, "lat", 1), shift(to_north, "lat", -1)

    feats = stem(state, weight_t, wide, mask)
    feats = block(0, exchange(*feats), bands[0], (thin, wide, w1[0], w2[0], mask, edge))
    return block(1, exchange(*feats), bands[1], (thin, wide, w1[1], w2[1], mask, edge), head_t)


def solution(mesh):
    placed = (
        P(("lat", "lon"), None, None),
        P(("lat", "lon"), None),
        P("lat", "lon"),
        *([P()] * 12),
    )
    return jax.shard_map(
        body, mesh=mesh, in_specs=placed, out_specs=P(None, "lat", "lon"), check_vma=False
    )
```

time: 522 us -> 144 us (0.28)
  other arithmetic: 204 us -> 2.34 us
  matrix products: 136 us -> 0 us
  local copies, waits for them, and re-layouts: 85.5 us -> 16.3 us
  Pallas kernels: 0 us -> 64.6 us
  waiting for transfers between devices: 57.7 us -> 39.4 us
  loops' own time: 12.3 us -> 0 us
    add x2 -> x0, other arithmetic: 155 us -> none  [depthwise(): summed + padded[:, i:i + row_count, j:j + col_count] * kernel[:, i, j][:,...]
    dot_general x6 -> x0, matrix products: 136 us -> none  [the longest x4 129 us: mix_cells(): jnp.dot(contract.T, hidden, preferred_element_type=jnp.float32)]
    pallas_call x0 -> x8, Pallas kernels: none -> 64.6 us  [the longest x1 24.4 us: block(): pl.pallas_call(functools.partial(block_body, index, True), out_shape=jax....]
    concatenate x3 -> x2, other arithmetic: 25.1 us -> 2.16 us  [the longest x1 2.16 us: body(): w1 = jnp.concatenate([w_in.transpose(0, 2, 1), terms], axis=2)]
    all_to_all x1, waiting for transfers between devices: 44 us -> 22 us  [body(): state = lax.all_to_all(send, axes, split_axis=0, concat_axis=0, tiled=True)]
    unnamed x174 -> x41, local copies, waits for them, and re-layouts: 31.6 us -> 12.5 us
    slice x17 -> x1, local copies, waits for them, and re-layouts: 19.1 us -> 0.21 us  [body(): bands = [band(dw_weight[b], span) for b in range(2)]]
    reduce_sum x8 -> x0, other arithmetic: 17.2 us -> none  [the longest x4 8.97 us: mix_cells(): variance = jnp.mean(centered * centered, axis=0, keepdims=True)]
  transfers between devices with their start and end apart: 9 -> 9, of which waited for: 4 -> 7; matrix products, arithmetic and copies ran while one was open for 4% -> 5% of each run, Pallas kernels for 0% -> 9%
where the time goes in v2:
time: 144 us
  Pallas kernels  64.6 us (45%)
  waiting for transfers between devices  39.4 us (27%)
  starting transfers between devices  20.7 us (14%)
  local copies, waits for them, and re-layouts  16.3 us (11%)
  other arithmetic  2.34 us (2%)
    pallas_call x1, Pallas kernels, block(): pl.pallas_call(functools.partial(block_body, index, True), out_shape=jax....  24.4 us
    pallas_call x1, Pallas kernels, block(): pl.pallas_call(functools.partial(block_body, index, False), out_shape=fea...  22.7 us
    all_to_all x1, waiting for transfers between devices, body(): state = lax.all_to_all(send, axes, split_axis=0, concat_axis=0, tiled=True)  22 us
    ppermute x8, waiting for transfers between devices, shift(): return lax.ppermute(x, axis, [(i, (i + by) % n) for i in range(n)])  17.4 us
    ppermute x8, starting transfers between devices, shift(): return lax.ppermute(x, axis, [(i, (i + by) % n) for i in range(n)])  13.4 us
    pallas_call x2, Pallas kernels, band(): pl.pallas_call(band_body, grid=(span // 8,), in_specs=[pl.BlockSpec((d, 6...  13 us
    unnamed x41, local copies, waits for them, and re-layouts  12.5 us
    all_to_all x1, starting transfers between devices, body(): state = lax.all_to_all(send, axes, split_axis=0, concat_axis=0, tiled=True)  7.3 us
  transfers between devices with their start and end apart: 9, of which 7 were waited for; matrix products, arithmetic and copies ran while one was open for 5% of the time, Pallas kernels for 9%

profile of v2, /device:TPU:0, one launch (start us, length us, event | category | flops | bytes accessed | tf_op | source)
XLA Modules:
  0.0 144.0 jit_solution(1528142141929541557)
XLA Ops:
  0.0 0.8 copy.62
  0.8 1.6 %copy-done.3 = bf16[4,256,1024]{2,1,0:T(8,128)(2,1)S(1)} copy-done((bf16[4,256,1024]{2,1,0:T(8,128)(2,1)S(1)}, bf16[4,256,1024]{2,1,0:T(8,128)(2,1)}, u32[]{:S(2)}) %copy-start.3) | copy-done | bytes 2097176
  2.4 2.2 %dequantize.1 = bf16[4,8,4,64,128]{4,3,2,1,0:T(8,128)(2,1)S(1)} custom-call(bf16[4,256,1024]{2,1,0:T(8,128)(2,1)S(1)} %copy-done.3, f32[256,4]{1,0:T(8,128)S(1)} %bitcast.40), custom_call_target="tpu_custom_call" | custom-call | bytes 4194304 | tf_op jit(solution)/shard_map/dequantize/pallas_call | solution.py:97
  4.6 1.3 copy-done.2
  6.0 7.3 %all-to-all-start = ((bf16[32,4,64,128]{3,2,1,0:T(8,128)(2,1)}), bf16[32,4,64,128]{3,2,1,0:T(8,128)(2,1)S(1)}, u32[]{:S(2)}, u32[]{:S(2)}) async-start(bf16[32,4,64,128]{3,2,1,0:T(8,128)(2,1)} %bitcast.39), calls=%async_computation | async-start | bytes 4194304 | tf_op jit(solution)/shard_map/all_to_all | solution.py:443
  14.1 1.0 copy.66
  15.1 1.4 copy.65
  16.6 2.2 %fusion.1 = bf16[2,768,208]{2,1,0:T(8,128)(2,1)} fusion(bf16[2,768,3]{2,1,0:T(8,128)(2,1)} %copy.66, bf16[2,768,192]{2,1,0:T(8,128)(2,1)S(1)} %bitcast.43), kind=kLoop, calls=%fused_computation.2 | loop fusion | flops 1916928 | bytes 1238016 | tf_op jit(solution)/shard_map/concatenate | solution.py:459
  18.8 0.2 broadcast_in_dim.25.wide_ref.refs_7_
  19.0 1.4 %broadcast_in_dim.11.refs_6_ = f32[6,192,1,128]{3,2,1,0:T(1,128)S(1)} broadcast(f32[6,192]{1,0:T(8,128)S(1)} %broadcast_in_dim.10), dimensions={0,1} | broadcast | bytes 594432 | tf_op jit(solution)/shard_map/broadcast_in_dim | solution.py:450
  20.5 0.2 slice_reduce_fusion
  21.0 6.5 %bands.2.refs_5_ = bf16[192,64,336]{2,1,0:T(8,128)(2,1)S(1)} custom-call(bf16[192,64]{1,0:T(8,128)(2,1)S(1)} %pad.14.w_ref, s32[1,336]{1,0:T(1,128)S(1)} %copy-done.6, s32[1,336]{1,0:T(1,128)S(1)} %copy-done.5), custom_call_target="tpu_custom_call" | custom-call | bytes 8257536 | tf_op jit(solution)/shard_map/bands/pallas_call | solution.py:223
  27.6 3.7 %copy-done.1 = bf16[192,64,336]{2,1,0:T(8,128)(2,1)} copy-done((bf16[192,64,336]{2,1,0:T(8,128)(2,1)}, bf16[192,64,336]{2,1,0:T(8,128)(2,1)S(1)}, u32[]{:S(2)}) %copy-start.1) | copy-done | bytes 8257560
  31.2 6.5 %bands.3.refs_5_ = bf16[192,64,336]{2,1,0:T(8,128)(2,1)S(1)} custom-call(bf16[192,64]{1,0:T(8,128)(2,1)S(1)} %pad.15.w_ref, s32[1,336]{1,0:T(1,128)S(1)} %copy-done.6, s32[1,336]{1,0:T(1,128)S(1)} %copy-done.5), custom_call_target="tpu_custom_call" | custom-call | bytes 8257536 | tf_op jit(solution)/shard_map/bands/pallas_call | solution.py:223
  37.7 3.6 %copy-done = bf16[192,64,336]{2,1,0:T(8,128)(2,1)} copy-done((bf16[192,64,336]{2,1,0:T(8,128)(2,1)}, bf16[192,64,336]{2,1,0:T(8,128)(2,1)S(1)}, u32[]{:S(2)}) %copy-start) | copy-done | bytes 8257560
  41.4 22.0 %all-to-all-done = bf16[32,4,64,128]{3,2,1,0:T(8,128)(2,1)S(1)} async-done(((bf16[32,4,64,128]{3,2,1,0:T(8,128)(2,1)}), bf16[32,4,64,128]{3,2,1,0:T(8,128)(2,1)S(1)}, u32[]{:S(2)}, u32[]{:S(2)}) %all-to-all-start) | async-done | bytes 2097184 | tf_op jit(solution)/shard_map/all_to_all | solution.py:443
  63.4 2.1 %stem.1 = (bf16[64,192,128]{2,1,0:T(8,128)(2,1)S(1)}, bf16[2,192,128]{2,1,0:T(8,128)(2,1)S(1)}, bf16[2,192,128]{2,1,0:T(8,128)(2,1)S(1)}, bf16[3,192,128]{2,1,0:T(8,128)(2,1)S(1)}, bf16[3,192,128]{2,1,0:T(8,128)(2,1)S(1)}) custom-call(bf16[128,64,128]{2,1,0:T(8,128)(2,1)S(1)} %bitcast.38, bf16[192,128]{1,0:T(8,128)(2,1)S(1)} %bitcast.42, ...), custom_call_target="tpu_custom_call" | custom-call | flops 402653184 | bytes 5242880 | tf_op jit(solution)/shard_map/stem/pallas_call | solution.py:195
  65.5 3.5 %collective-permute-start.1 = (bf16[2,192,128]{2,1,0:T(8,128)(2,1)S(1)}, bf16[2,192,128]{2,1,0:T(8,128)(2,1)S(1)}, u32[]{:S(2)}, u32[]{:S(2)}) collective-permute-start(bf16[2,192,128]{2,1,0:T(8,128)(2,1)S(1)} %get-tuple-element.54), channel_id=1, source_target_pairs={{0,7},{1,0},{2,1},{3,2},{4,3},{5,4},{6,5},{7,6},{8,15},{9,8},{10,9... | collective-permute-start | bytes 294920 | tf_op jit(solution)/shard_map/ppermute | solution.py:474
  69.1 2.2 %collective-permute-done.west_in.refs_1_ = bf16[2,192,128]{2,1,0:T(8,128)(2,1)S(1)} collective-permute-done((bf16[2,192,128]{2,1,0:T(8,128)(2,1)S(1)}, bf16[2,192,128]{2,1,0:T(8,128)(2,1)S(1)}, u32[]{:S(2)}, u32[]{:S(2)}) %collective-permute-start) | collective-permute-done | bytes 98336 | tf_op jit(solution)/shard_map/ppermute | solution.py:474
  71.5 0.5 collective-permute-start.2
  72.0 2.5 %collective-permute-start.3 = (bf16[4,192,128]{2,1,0:T(8,128)(2,1)S(1)}, bf16[4,192,128]{2,1,0:T(8,128)(2,1)S(1)}, u32[]{:S(2)}, u32[]{:S(2)}) collective-permute-start(bf16[4,192,128]{2,1,0:T(8,128)(2,1)S(1)} %get-tuple-element.58), channel_id=1, source_target_pairs={{0,24},{8,0},{16,8},{24,16},{1,25},{9,1},{17,9},{25,17},{2,26},{10... | collective-permute-start | bytes 589832 | tf_op jit(solution)/shard_map/ppermute | solution.py:474
  74.6 4.8 %collective-permute-done.2.refs_3_ = bf16[4,192,128]{2,1,0:T(8,128)(2,1)S(1)} collective-permute-done((bf16[4,192,128]{2,1,0:T(8,128)(2,1)S(1)}, bf16[4,192,128]{2,1,0:T(8,128)(2,1)S(1)}, u32[]{:S(2)}, u32[]{:S(2)}) %collective-permute-start.2) | collective-permute-done | bytes 196640 | tf_op jit(solution)/shard_map/ppermute | solution.py:474
  79.3 1.9 %collective-permute-done.3.refs_4_ = bf16[4,192,128]{2,1,0:T(8,128)(2,1)S(1)} collective-permute-done((bf16[4,192,128]{2,1,0:T(8,128)(2,1)S(1)}, bf16[4,192,128]{2,1,0:T(8,128)(2,1)S(1)}, u32[]{:S(2)}, u32[]{:S(2)}) %collective-permute-start.3) | collective-permute-done | bytes 196640 | tf_op jit(solution)/shard_map/ppermute | solution.py:474
  81.3 22.7 %block.1 = (bf16[64,192,128]{2,1,0:T(8,128)(2,1)S(1)}, bf16[2,192,128]{2,1,0:T(8,128)(2,1)S(1)}, bf16[2,192,128]{2,1,0:T(8,128)(2,1)S(1)}, bf16[3,192,128]{2,1,0:T(8,128)(2,1)S(1)}, bf16[3,192,128]{2,1,0:T(8,128)(2,1)S(1)}) custom-call(bf16[64,192,128]{2,1,0:T(8,128)(2,1)S(1)} %get-tuple-element.52.refs_0_, ...), custom_call_target="tpu_custom_call" | custom-call | flops 5888802816 | bytes 31457280 | tf_op jit(solution)/shard_map/block/pallas_call | solution.py:398
  104.0 3.5 %collective-permute-start.5 = (bf16[2,192,128]{2,1,0:T(8,128)(2,1)S(1)}, bf16[2,192,128]{2,1,0:T(8,128)(2,1)S(1)}, u32[]{:S(2)}, u32[]{:S(2)}) collective-permute-start(bf16[2,192,128]{2,1,0:T(8,128)(2,1)S(1)} %get-tuple-element.66), channel_id=1, source_target_pairs={{0,7},{1,0},{2,1},{3,2},{4,3},{5,4},{6,5},{7,6},{8,15},{9,8},{10,9... | collective-permute-start | bytes 294920 | tf_op jit(solution)/shard_map/ppermute | solution.py:474
  107.5 2.3 %collective-permute-done.4.west_in.refs_1_ = bf16[2,192,128]{2,1,0:T(8,128)(2,1)S(1)} collective-permute-done((bf16[2,192,128]{2,1,0:T(8,128)(2,1)S(1)}, bf16[2,192,128]{2,1,0:T(8,128)(2,1)S(1)}, u32[]{:S(2)}, u32[]{:S(2)}) %collective-permute-start.4) | collective-permute-done | bytes 98336 | tf_op jit(solution)/shard_map/ppermute | solution.py:474
  109.8 0.2 rows.3
  110.0 1.4 collective-permute-start.6
  111.4 1.8 %collective-permute-start.7 = (bf16[4,192,128]{2,1,0:T(8,128)(2,1)S(1)}, bf16[4,192,128]{2,1,0:T(8,128)(2,1)S(1)}, u32[]{:S(2)}, u32[]{:S(2)}) collective-permute-start(bf16[4,192,128]{2,1,0:T(8,128)(2,1)S(1)} %get-tuple-element.70), channel_id=1, source_target_pairs={{0,24},{8,0},{16,8},{24,16},{1,25},{9,1},{17,9},{25,17},{2,26},{10... | collective-permute-start | bytes 589832 | tf_op jit(solution)/shard_map/ppermute | solution.py:474
  113.2 4.9 %collective-permute-done.6.refs_3_ = bf16[4,192,128]{2,1,0:T(8,128)(2,1)S(1)} collective-permute-done((bf16[4,192,128]{2,1,0:T(8,128)(2,1)S(1)}, bf16[4,192,128]{2,1,0:T(8,128)(2,1)S(1)}, u32[]{:S(2)}, u32[]{:S(2)}) %collective-permute-start.6) | collective-permute-done | bytes 196640 | tf_op jit(solution)/shard_map/ppermute | solution.py:474
  118.1 1.2 collective-permute-done.7.refs_4_
  119.4 24.4 %block_head.1 = f32[128,64,128]{2,1,0:T(8,128)} custom-call(bf16[64,192,128]{2,1,0:T(8,128)(2,1)S(1)} %get-tuple-element.64.refs_0_, bf16[2,192,128]{2,1,0:T(8,128)(2,1)S(1)} %collective-permute-done.4.west_in.refs_1_, bf16[2,192,128]{2,1,0:T(8,128)(2,1)S(1)} %collective-permute-done.5.east_in.refs_2_, ...), custom_call_target="tpu_custom_call" | custom-call | flops 5888802816 | bytes 31457280 | tf_op jit(solution)/shard_map/block_head/pallas_call | solution.py:408
  (66 shorter events, 1.6 us)
Async XLA Ops:
  0.8 1.6 %copy-start.3 = (bf16[4,256,1024]{2,1,0:T(8,128)(2,1)S(1)}, bf16[4,256,1024]{2,1,0:T(8,128)(2,1)}, u32[]{:S(2)}) copy-start(bf16[4,256,1024]{2,1,0:T(8,128)(2,1)} %q_ref.1) | copy-start | bytes 6291460
  4.6 1.3 copy-start.2
  5.9 7.4 %copy-start.13 = (f32[2,192]{1,0:T(2,128)S(1)}, f32[2,192]{1,0:T(2,128)}, u32[]{:S(2)}) copy-start(f32[2,192]{1,0:T(2,128)} %param.32) | copy-start | bytes 4612
  5.9 7.4 %copy-start.14 = (f32[2,192]{1,0:T(2,128)S(1)}, f32[2,192]{1,0:T(2,128)}, u32[]{:S(2)}) copy-start(f32[2,192]{1,0:T(2,128)} %param.31) | copy-start | bytes 4612
  5.9 7.5 %copy-start.15 = (f32[2,192]{1,0:T(2,128)S(1)}, f32[2,192]{1,0:T(2,128)}, u32[]{:S(2)}) copy-start(f32[2,192]{1,0:T(2,128)} %param.27) | copy-start | bytes 4612
  5.9 7.5 %copy-start.16 = (f32[2,192]{1,0:T(2,128)S(1)}, f32[2,192]{1,0:T(2,128)}, u32[]{:S(2)}) copy-start(f32[2,192]{1,0:T(2,128)} %param.26) | copy-start | bytes 4612
  5.9 7.5 %copy-start.17 = (f32[2,192]{1,0:T(2,128)S(1)}, f32[2,192]{1,0:T(2,128)}, u32[]{:S(2)}) copy-start(f32[2,192]{1,0:T(2,128)} %param.25) | copy-start | bytes 4612
  5.9 7.5 %copy-start.11 = (s32[64,128]{1,0:T(8,128)S(1)}, s32[64,128]{1,0:T(8,128)}, u32[]{:S(2)}) copy-start(s32[64,128]{1,0:T(8,128)} %param.21) | copy-start | bytes 98308
  5.9 8.0 %copy-start.10 = (bf16[192,128]{1,0:T(8,128)(2,1)S(1)}, bf16[192,128]{1,0:T(8,128)(2,1)}, u32[]{:S(2)}) copy-start(bf16[192,128]{1,0:T(8,128)(2,1)} %param.33) | copy-start | bytes 147460
  5.9 8.1 %copy-start.12 = (f32[2,768]{1,0:T(2,128)S(1)}, f32[2,768]{1,0:T(2,128)}, u32[]{:S(2)}) copy-start(f32[2,768]{1,0:T(2,128)} %param.29) | copy-start | bytes 18436
  6.0 57.4 %all-to-all-start = ((bf16[32,4,64,128]{3,2,1,0:T(8,128)(2,1)}), bf16[32,4,64,128]{3,2,1,0:T(8,128)(2,1)S(1)}, u32[]{:S(2)}, u32[]{:S(2)}) async-start(bf16[32,4,64,128]{3,2,1,0:T(8,128)(2,1)} %bitcast.39), calls=%async_computation | async-start | bytes 4194304 | tf_op jit(solution)/shard_map/all_to_all | solution.py:443
  13.3 3.3 %copy-start.18 = (f32[192]{0:T(256)S(1)}, f32[192]{0:T(256)}, u32[]{:S(2)}) copy-start(f32[192]{0:T(256)} %param.23) | copy-start | bytes 2308
  15.1 5.4 %copy-start.9 = (f32[2,192,7,7]{1,0,3,2:T(2,128)S(1)}, f32[2,192,7,7]{1,0,3,2:T(2,128)}, u32[]{:S(2)}) copy-start(f32[2,192,7,7]{1,0,3,2:T(2,128)} %param.24) | copy-start | bytes 225796
  16.4 4.6 %copy-start.5 = (s32[1,336]{1,0:T(1,128)S(1)}, s32[1,336]{1,0:T(1,128)}, u32[]{:S(2)}) copy-start(s32[1,336]{1,0:T(1,128)} %constant.20.clone.row_ref) | copy-start | bytes 4036
  16.4 4.6 %copy-start.6 = (s32[1,336]{1,0:T(1,128)S(1)}, s32[1,336]{1,0:T(1,128)}, u32[]{:S(2)}) copy-start(s32[1,336]{1,0:T(1,128)} %constant.19.clone.col_ref) | copy-start | bytes 4036
  27.6 3.7 %copy-start.1 = (bf16[192,64,336]{2,1,0:T(8,128)(2,1)}, bf16[192,64,336]{2,1,0:T(8,128)(2,1)S(1)}, u32[]{:S(2)}) copy-start(bf16[192,64,336]{2,1,0:T(8,128)(2,1)S(1)} %bands.2.refs_5_) | copy-start | bytes 24772612
  31.2 32.1 %copy-start.4 = (bf16[128,192]{0,1:T(8,128)(2,1)S(1)}, bf16[128,192]{0,1:T(8,128)(2,1)}, u32[]{:S(2)}) copy-start(bf16[128,192]{0,1:T(8,128)(2,1)} %param.22) | copy-start | bytes 147460
  37.7 3.6 %copy-start = (bf16[192,64,336]{2,1,0:T(8,128)(2,1)}, bf16[192,64,336]{2,1,0:T(8,128)(2,1)S(1)}, u32[]{:S(2)}) copy-start(bf16[192,64,336]{2,1,0:T(8,128)(2,1)S(1)} %bands.3.refs_5_) | copy-start | bytes 24772612
  63.4 5.7 %copy-start.7 = (bf16[2,768,208]{2,1,0:T(8,128)(2,1)S(1)}, bf16[2,768,208]{2,1,0:T(8,128)(2,1)}, u32[]{:S(2)}) copy-start(bf16[2,768,208]{2,1,0:T(8,128)(2,1)} %fusion.1) | copy-start | bytes 1916932
  63.4 11.1 %copy-start.8 = (bf16[2,768,192]{1,2,0:T(8,128)(2,1)S(1)}, bf16[2,768,192]{1,2,0:T(8,128)(2,1)}, u32[]{:S(2)}) copy-start(bf16[2,768,192]{1,2,0:T(8,128)(2,1)} %param.30) | copy-start | bytes 1769476
  65.5 5.9 %collective-permute-start = (bf16[2,192,128]{2,1,0:T(8,128)(2,1)S(1)}, bf16[2,192,128]{2,1,0:T(8,128)(2,1)S(1)}, u32[]{:S(2)}, u32[]{:S(2)}) collective-permute-start(bf16[2,192,128]{2,1,0:T(8,128)(2,1)S(1)} %get-tuple-element.53), channel_id=1, source_target_pairs={{0,1},{1,2},{2,3},{3,4},{4,5},{5,6},{6,7},{7,0},{8,9},{9,10},{10,1... | collective-permute-start | bytes 294920 | tf_op jit(solution)/shard_map/ppermute | solution.py:474
  65.5 5.8 %collective-permute-start.1 = (bf16[2,192,128]{2,1,0:T(8,128)(2,1)S(1)}, bf16[2,192,128]{2,1,0:T(8,128)(2,1)S(1)}, u32[]{:S(2)}, u32[]{:S(2)}) collective-permute-start(bf16[2,192,128]{2,1,0:T(8,128)(2,1)S(1)} %get-tuple-element.54), channel_id=1, source_target_pairs={{0,7},{1,0},{2,1},{3,2},{4,3},{5,4},{6,5},{7,6},{8,15},{9,8},{10,9... | collective-permute-start | bytes 294920 | tf_op jit(solution)/shard_map/ppermute | solution.py:474
  71.5 7.8 %collective-permute-start.2 = (bf16[4,192,128]{2,1,0:T(8,128)(2,1)S(1)}, bf16[4,192,128]{2,1,0:T(8,128)(2,1)S(1)}, u32[]{:S(2)}, u32[]{:S(2)}) collective-permute-start(bf16[4,192,128]{2,1,0:T(8,128)(2,1)S(1)} %get-tuple-element.57), channel_id=1, source_target_pairs={{0,8},{8,16},{16,24},{24,0},{1,9},{9,17},{17,25},{25,1},{2,10},{10... | collective-permute-start | bytes 589832 | tf_op jit(solution)/shard_map/ppermute | solution.py:474
  72.0 9.3 %collective-permute-start.3 = (bf16[4,192,128]{2,1,0:T(8,128)(2,1)S(1)}, bf16[4,192,128]{2,1,0:T(8,128)(2,1)S(1)}, u32[]{:S(2)}, u32[]{:S(2)}) collective-permute-start(bf16[4,192,128]{2,1,0:T(8,128)(2,1)S(1)} %get-tuple-element.58), channel_id=1, source_target_pairs={{0,24},{8,0},{16,8},{24,16},{1,25},{9,1},{17,9},{25,17},{2,26},{10... | collective-permute-start | bytes 589832 | tf_op jit(solution)/shard_map/ppermute | solution.py:474
  104.0 5.9 %collective-permute-start.4 = (bf16[2,192,128]{2,1,0:T(8,128)(2,1)S(1)}, bf16[2,192,128]{2,1,0:T(8,128)(2,1)S(1)}, u32[]{:S(2)}, u32[]{:S(2)}) collective-permute-start(bf16[2,192,128]{2,1,0:T(8,128)(2,1)S(1)} %get-tuple-element.65), channel_id=1, source_target_pairs={{0,1},{1,2},{2,3},{3,4},{4,5},{5,6},{6,7},{7,0},{8,9},{9,10},{10,1... | collective-permute-start | bytes 294920 | tf_op jit(solution)/shard_map/ppermute | solution.py:474
  104.0 5.8 %collective-permute-start.5 = (bf16[2,192,128]{2,1,0:T(8,128)(2,1)S(1)}, bf16[2,192,128]{2,1,0:T(8,128)(2,1)S(1)}, u32[]{:S(2)}, u32[]{:S(2)}) collective-permute-start(bf16[2,192,128]{2,1,0:T(8,128)(2,1)S(1)} %get-tuple-element.66), channel_id=1, source_target_pairs={{0,7},{1,0},{2,1},{3,2},{4,3},{5,4},{6,5},{7,6},{8,15},{9,8},{10,9... | collective-permute-start | bytes 294920 | tf_op jit(solution)/shard_map/ppermute | solution.py:474
  110.0 8.1 %collective-permute-start.6 = (bf16[4,192,128]{2,1,0:T(8,128)(2,1)S(1)}, bf16[4,192,128]{2,1,0:T(8,128)(2,1)S(1)}, u32[]{:S(2)}, u32[]{:S(2)}) collective-permute-start(bf16[4,192,128]{2,1,0:T(8,128)(2,1)S(1)} %get-tuple-element.69), channel_id=1, source_target_pairs={{0,8},{8,16},{16,24},{24,0},{1,9},{9,17},{17,25},{25,1},{2,10},{10... | collective-permute-start | bytes 589832 | tf_op jit(solution)/shard_map/ppermute | solution.py:474
  111.4 8.0 %collective-permute-start.7 = (bf16[4,192,128]{2,1,0:T(8,128)(2,1)S(1)}, bf16[4,192,128]{2,1,0:T(8,128)(2,1)S(1)}, u32[]{:S(2)}, u32[]{:S(2)}) collective-permute-start(bf16[4,192,128]{2,1,0:T(8,128)(2,1)S(1)} %get-tuple-element.70), channel_id=1, source_target_pairs={{0,24},{8,0},{16,8},{24,16},{1,25},{9,1},{17,9},{25,17},{2,26},{10... | collective-permute-start | bytes 589832 | tf_op jit(solution)/shard_map/ppermute | solution.py:474

commit v3 on v2

--- a/solution.py
+++ b/solution.py
@@ -75,8 +75,10 @@
     phase = (at >> 6) ^ (to >> 7)
     order = (row_index(shape) == 2 * (at & (half - 1)) + phase).astype(f32).astype(bf16)
     left = lane_index((span, lanes)) < half
+    every = (rows, s_ref.shape[1])
     for c in range(channels):
-        scale = jnp.broadcast_to(s_ref[:, c : c + 1], (rows, lanes))
+        own = lane_index(every) == row_index(every) + pl.program_id(0) * rows
+        scale = jnp.sum(jnp.where(own, s_ref[c : c + 1, :], 0.0), axis=1, keepdims=True)
         x = jnp.concatenate(
             [
                 (q_ref[c, :, b * lanes : (b + 1) * lanes].astype(f32) * scale).astype(bf16)
@@ -99,13 +101,13 @@
         grid=(n_lat,),
         in_specs=[
             pl.BlockSpec((channels, rows, n_cols), lambda a: (0, a, 0)),
-            pl.BlockSpec((rows, channels), lambda a: (a, 0)),
+            pl.BlockSpec((channels, n_rows), lambda a: (0, 0)),
         ],
         out_specs=pl.BlockSpec((1, n_lon, channels, rows, lanes), lambda a: (a, 0, 0, 0, 0)),
         out_shape=jax.ShapeDtypeStruct((n_lat, n_lon, channels, rows, lanes), bf16),
         name="dequantize",
-        **params_for(20, 0, 4 * q_state.size),
-    )(q_state, scales.T).reshape(n_lat * n_lon, channels, rows, lanes)
+        **params_for(60, 0, 4 * q_state.size),
+    )(q_state, scales).reshape(n_lat * n_lon, channels, rows, lanes)
 
 
 def slot_of(shape):
@@ -240,9 +242,9 @@
     thin_ref, wide_ref, w1_ref, w2_ref, mask_ref, edge_ref = refs[6:12]
     refs = refs[12:]
     if head:
-        head_ref, out_ref, conv_ref, held_ref, band_sems, tend_ref, sems = refs
+        head_ref, out_ref, conv_ref, held_ref, band_sems, sum_ref, tend_ref, sems = refs
     else:
-        f_ref, *sent_refs, conv_ref, held_ref, band_sems, e_ref = refs
+        f_ref, *sent_refs, conv_ref, held_ref, band_sems, sum_ref, e_ref = refs
     leads, d = f_in.shape[:2]
     span = leads // 2
     per = span // 16
@@ -304,6 +306,7 @@
             xrow += [zero, zero]
             hrow += [zero, zero]
         chunks[halo_chunk] = tuple(jnp.swapaxes(jnp.stack(v), 0, 1) for v in (xrow, hrow))
+        total = squares = 0.0
         for u in range(16):
             taps = []
             for s, c in window_of(span):
@@ -313,8 +316,20 @@
                     x = turn(jnp.where(past, h, x), -s)
                 taps.append(x)
             taps = jnp.concatenate(taps, axis=0)
-            conv_ref[g * 16 + u] = jnp.dot(held_ref[g * 16 + u], taps, preferred_element_type=f32)
+            y = jnp.dot(held_ref[g * 16 + u], taps, preferred_element_type=f32)
+            y = y + dwb[g * 16 + u]
+            conv_ref[g * 16 + u] = y
+            if u == 0:
+                origin = conv_ref[0]
+            y = y - origin
+            total = total + y
+            squares = squares + y * y
+        sum_ref[0] += total
+        sum_ref[1] += squares
         return 0
+
+    dwb, gain, lnb = (thin_ref.at[3 * index + i] for i in range(3))
+    sum_ref[...] = jnp.zeros_like(sum_ref)
 
     lax.fori_loop(0, d // 16, conv_step, 0)
 
@@ -325,18 +340,20 @@
         source = (col & 1) * lanes + (to >> 7) * half + (col >> 1)
         back = (at == source).astype(f32).astype(bf16)
     ones = (row_index((16, 8 * lanes)) < 3).astype(f32).astype(bf16)
-    dwb, gain, lnb = (thin_ref.at[3 * index + i] for i in range(3))
     ls, lsb = wide_ref[2 * index], wide_ref[2 * index + 1]
     held = []
     for k in range(leads // 8):
         u, phase = k // 2, k % 2
         lead = phase * span + 8 * u
-        y = conv_ref[:, 8 * k : 8 * k + 8, :] + dwb[...]
-        average = jnp.sum(y, axis=0, keepdims=True) * (1.0 / d)
-        centered = y - average
-        variance = jnp.sum(centered * centered, axis=0, keepdims=True) * (1.0 / d)
-        normed = centered * lax.rsqrt(variance + ln_eps) * gain[...] + lnb[...]
-        normed = jnp.swapaxes(normed, 0, 1).astype(bf16)
+        if phase == 0:
+            cut = slice(8 * k, 8 * k + 16)
+            average = sum_ref[0, cut, :] * (1.0 / d)
+            variance = sum_ref[1, cut, :] * (1.0 / d) - average * average
+            scale = lax.rsqrt(jnp.maximum(variance, 0.0) + ln_eps)
+            centered = conv_ref[:, cut, :] - (conv_ref[0, cut, :] + average)
+            both_normed = (centered * scale * gain[...] + lnb[...]).astype(bf16)
+            both_normed = jnp.swapaxes(both_normed, 0, 1)
+        normed = both_normed[8 * phase : 8 * phase + 8]
         joined = jnp.concatenate([normed[i] for i in range(8)], axis=1)
         joined = jnp.concatenate([joined, ones], axis=0)
         hidden = jnp.dot(w1_ref[...], joined, preferred_element_type=f32)
@@ -393,6 +410,7 @@
         pltpu.VMEM((d, leads, lanes), f32),
         pltpu.VMEM(bands.shape, bf16),
         pltpu.SemaphoreType.DMA((d // 16,)),
+        pltpu.VMEM((2, leads, lanes), f32),
     ]
     if head is None:
         return pl.pallas_call(

time: 144 us -> 137 us (0.951)
  Pallas kernels: 64.6 us -> 60.8 us
  local copies, waits for them, and re-layouts: 16.3 us -> 12.6 us
    unnamed x41 -> x36, local copies, waits for them, and re-layouts: 12.5 us -> 8.8 us
    pallas_call x1, Pallas kernels: 22.7 us -> 18.9 us  [block(): pl.pallas_call(functools.partial(block_body, index, False), out_shape=fea...]
    pallas_call x1, Pallas kernels: 24.4 us -> 21.7 us  [block(): pl.pallas_call(functools.partial(block_body, index, True), out_shape=jax....]
    pallas_call x1, Pallas kernels: 2.15 us -> 4.72 us  [prep(): pl.pallas_call(prep_body, grid=(n_lat,), in_specs=[pl.BlockSpec((channels...]
  transfers between devices with their start and end apart: 9 -> 9, of which waited for: 7 -> 7; matrix products, arithmetic and copies ran while one was open for 5% -> 6% of each run, Pallas kernels for 9% -> 10%
where the time goes in v3:
time: 137 us; the launch traced here: 136 us
  Pallas kernels  60.8 us (44%)
  waiting for transfers between devices  39.4 us (29%)
  starting transfers between devices  20.4 us (15%)
  local copies, waits for them, and re-layouts  12.6 us (9%)
  other arithmetic  2.35 us (2%)
    all_to_all x1, waiting for transfers between devices, body(): state = lax.all_to_all(send, axes, split_axis=0, concat_axis=0, tiled=True)  22 us
    pallas_call x1, Pallas kernels, block(): pl.pallas_call(functools.partial(block_body, index, True), out_shape=jax....  21.7 us
    pallas_call x1, Pallas kernels, block(): pl.pallas_call(functools.partial(block_body, index, False), out_shape=fea...  18.9 us
    ppermute x8, waiting for transfers between devices, shift(): return lax.ppermute(x, axis, [(i, (i + by) % n) for i in range(n)])  17.4 us
    ppermute x8, starting transfers between devices, shift(): return lax.ppermute(x, axis, [(i, (i + by) % n) for i in range(n)])  13.1 us
    pallas_call x2, Pallas kernels, band(): pl.pallas_call(band_body, grid=(span // 8,), in_specs=[pl.BlockSpec((d, 6...  13 us
    unnamed x36, local copies, waits for them, and re-layouts  8.8 us
    all_to_all x1, starting transfers between devices, body(): state = lax.all_to_all(send, axes, split_axis=0, concat_axis=0, tiled=True)  7.3 us
  transfers between devices with their start and end apart: 9, of which 7 were waited for; matrix products, arithmetic and copies ran while one was open for 6% of the time, Pallas kernels for 10%

profile of v3, /device:TPU:0, one launch (start us, length us, event | category | flops | bytes accessed | tf_op | source)
XLA Modules:
  0.0 136.2 jit_solution(18318344644326293694)
XLA Ops:
  0.0 4.7 %dequantize.1 = bf16[4,8,4,64,128]{4,3,2,1,0:T(8,128)(2,1)} custom-call(bf16[4,256,1024]{2,1,0:T(8,128)(2,1)} %q_ref.1, f32[4,256]{1,0:T(4,128)} %s_ref.1), custom_call_target="tpu_custom_call" | custom-call | bytes 4194304 | tf_op jit(solution)/shard_map/dequantize/pallas_call | solution.py:99
  4.8 7.3 %all-to-all-start = ((bf16[32,4,64,128]{3,2,1,0:T(8,128)(2,1)}), bf16[32,4,64,128]{3,2,1,0:T(8,128)(2,1)S(1)}, u32[]{:S(2)}, u32[]{:S(2)}) async-start(bf16[32,4,64,128]{3,2,1,0:T(8,128)(2,1)} %bitcast.40), calls=%async_computation | async-start | bytes 4194304 | tf_op jit(solution)/shard_map/all_to_all | solution.py:461
  12.4 0.1 reshape.39
  12.9 1.0 copy.61
  13.9 1.4 %copy.60 = bf16[2,192,768]{1,2,0:T(8,128)(2,1)S(1)} copy(bf16[2,192,768]{2,1,0:T(8,128)(2,1)} %param.28) | data formatting | bytes 1179648 | tf_op args[9]
  15.4 2.2 %fusion.1 = bf16[2,768,208]{2,1,0:T(8,128)(2,1)} fusion(bf16[2,768,3]{2,1,0:T(8,128)(2,1)} %copy.61, bf16[2,768,192]{2,1,0:T(8,128)(2,1)S(1)} %bitcast.41), kind=kLoop, calls=%fused_computation.2 | loop fusion | flops 1916928 | bytes 1238016 | tf_op jit(solution)/shard_map/concatenate | solution.py:477
  17.6 0.2 broadcast_in_dim.25.wide_ref.refs_7_
  17.8 1.4 %broadcast_in_dim.11.refs_6_ = f32[6,192,1,128]{3,2,1,0:T(1,128)S(1)} broadcast(f32[6,192]{1,0:T(8,128)S(1)} %broadcast_in_dim.10), dimensions={0,1} | broadcast | bytes 594432 | tf_op jit(solution)/shard_map/broadcast_in_dim | solution.py:468
  19.3 0.2 slice_reduce_fusion
  19.6 0.1 copy.66
  19.9 6.5 %bands.2.refs_5_ = bf16[192,64,336]{2,1,0:T(8,128)(2,1)S(1)} custom-call(bf16[192,64]{1,0:T(8,128)(2,1)S(1)} %pad.14.w_ref, s32[1,336]{1,0:T(1,128)S(1)} %copy-done.4, s32[1,336]{1,0:T(1,128)S(1)} %copy-done.3), custom_call_target="tpu_custom_call" | custom-call | bytes 8257536 | tf_op jit(solution)/shard_map/bands/pallas_call | solution.py:225
  26.4 3.6 %copy-done.1 = bf16[192,64,336]{2,1,0:T(8,128)(2,1)} copy-done((bf16[192,64,336]{2,1,0:T(8,128)(2,1)}, bf16[192,64,336]{2,1,0:T(8,128)(2,1)S(1)}, u32[]{:S(2)}) %copy-start.1) | copy-done | bytes 8257560
  30.1 6.5 %bands.3.refs_5_ = bf16[192,64,336]{2,1,0:T(8,128)(2,1)S(1)} custom-call(bf16[192,64]{1,0:T(8,128)(2,1)S(1)} %pad.15.w_ref, s32[1,336]{1,0:T(1,128)S(1)} %copy-done.4, s32[1,336]{1,0:T(1,128)S(1)} %copy-done.3), custom_call_target="tpu_custom_call" | custom-call | bytes 8257536 | tf_op jit(solution)/shard_map/bands/pallas_call | solution.py:225
  36.6 3.6 %copy-done = bf16[192,64,336]{2,1,0:T(8,128)(2,1)} copy-done((bf16[192,64,336]{2,1,0:T(8,128)(2,1)}, bf16[192,64,336]{2,1,0:T(8,128)(2,1)S(1)}, u32[]{:S(2)}) %copy-start) | copy-done | bytes 8257560
  40.2 22.0 %all-to-all-done = bf16[32,4,64,128]{3,2,1,0:T(8,128)(2,1)S(1)} async-done(((bf16[32,4,64,128]{3,2,1,0:T(8,128)(2,1)}), bf16[32,4,64,128]{3,2,1,0:T(8,128)(2,1)S(1)}, u32[]{:S(2)}, u32[]{:S(2)}) %all-to-all-start) | async-done | bytes 2097184 | tf_op jit(solution)/shard_map/all_to_all | solution.py:461
  62.2 2.1 %stem.1 = (bf16[64,192,128]{2,1,0:T(8,128)(2,1)S(1)}, bf16[2,192,128]{2,1,0:T(8,128)(2,1)S(1)}, bf16[2,192,128]{2,1,0:T(8,128)(2,1)S(1)}, bf16[3,192,128]{2,1,0:T(8,128)(2,1)S(1)}, bf16[3,192,128]{2,1,0:T(8,128)(2,1)S(1)}) custom-call(bf16[128,64,128]{2,1,0:T(8,128)(2,1)S(1)} %bitcast.37, bf16[192,128]{1,0:T(8,128)(2,1)S(1)} %bitcast.39, ...), custom_call_target="tpu_custom_call" | custom-call | flops 402653184 | bytes 5242880 | tf_op jit(solution)/shard_map/stem/pallas_call | solution.py:197
  64.4 3.5 %collective-permute-start.1 = (bf16[2,192,128]{2,1,0:T(8,128)(2,1)S(1)}, bf16[2,192,128]{2,1,0:T(8,128)(2,1)S(1)}, u32[]{:S(2)}, u32[]{:S(2)}) collective-permute-start(bf16[2,192,128]{2,1,0:T(8,128)(2,1)S(1)} %get-tuple-element.54), channel_id=1, source_target_pairs={{0,7},{1,0},{2,1},{3,2},{4,3},{5,4},{6,5},{7,6},{8,15},{9,8},{10,9... | collective-permute-start | bytes 294920 | tf_op jit(solution)/shard_map/ppermute | solution.py:492
  68.0 2.2 %collective-permute-done.west_in.refs_1_ = bf16[2,192,128]{2,1,0:T(8,128)(2,1)S(1)} collective-permute-done((bf16[2,192,128]{2,1,0:T(8,128)(2,1)S(1)}, bf16[2,192,128]{2,1,0:T(8,128)(2,1)S(1)}, u32[]{:S(2)}, u32[]{:S(2)}) %collective-permute-start) | collective-permute-done | bytes 98336 | tf_op jit(solution)/shard_map/ppermute | solution.py:492
  70.2 0.2 rows.2
  70.4 0.5 collective-permute-start.2
  70.8 2.5 %collective-permute-start.3 = (bf16[4,192,128]{2,1,0:T(8,128)(2,1)S(1)}, bf16[4,192,128]{2,1,0:T(8,128)(2,1)S(1)}, u32[]{:S(2)}, u32[]{:S(2)}) collective-permute-start(bf16[4,192,128]{2,1,0:T(8,128)(2,1)S(1)} %get-tuple-element.58), channel_id=1, source_target_pairs={{0,24},{8,0},{16,8},{24,16},{1,25},{9,1},{17,9},{25,17},{2,26},{10... | collective-permute-start | bytes 589832 | tf_op jit(solution)/shard_map/ppermute | solution.py:492
  73.4 4.8 %collective-permute-done.2.refs_3_ = bf16[4,192,128]{2,1,0:T(8,128)(2,1)S(1)} collective-permute-done((bf16[4,192,128]{2,1,0:T(8,128)(2,1)S(1)}, bf16[4,192,128]{2,1,0:T(8,128)(2,1)S(1)}, u32[]{:S(2)}, u32[]{:S(2)}) %collective-permute-start.2) | collective-permute-done | bytes 196640 | tf_op jit(solution)/shard_map/ppermute | solution.py:492
  78.2 1.9 %collective-permute-done.3.refs_4_ = bf16[4,192,128]{2,1,0:T(8,128)(2,1)S(1)} collective-permute-done((bf16[4,192,128]{2,1,0:T(8,128)(2,1)S(1)}, bf16[4,192,128]{2,1,0:T(8,128)(2,1)S(1)}, u32[]{:S(2)}, u32[]{:S(2)}) %collective-permute-start.3) | collective-permute-done | bytes 196640 | tf_op jit(solution)/shard_map/ppermute | solution.py:492
  80.1 18.9 %block.1 = (bf16[64,192,128]{2,1,0:T(8,128)(2,1)S(1)}, bf16[2,192,128]{2,1,0:T(8,128)(2,1)S(1)}, bf16[2,192,128]{2,1,0:T(8,128)(2,1)S(1)}, bf16[3,192,128]{2,1,0:T(8,128)(2,1)S(1)}, bf16[3,192,128]{2,1,0:T(8,128)(2,1)S(1)}) custom-call(bf16[64,192,128]{2,1,0:T(8,128)(2,1)S(1)} %get-tuple-element.52.refs_0_, ...), custom_call_target="tpu_custom_call" | custom-call | flops 5888802816 | bytes 31457280 | tf_op jit(solution)/shard_map/block/pallas_call | solution.py:416
  99.1 3.5 %collective-permute-start.5 = (bf16[2,192,128]{2,1,0:T(8,128)(2,1)S(1)}, bf16[2,192,128]{2,1,0:T(8,128)(2,1)S(1)}, u32[]{:S(2)}, u32[]{:S(2)}) collective-permute-start(bf16[2,192,128]{2,1,0:T(8,128)(2,1)S(1)} %get-tuple-element.66), channel_id=1, source_target_pairs={{0,7},{1,0},{2,1},{3,2},{4,3},{5,4},{6,5},{7,6},{8,15},{9,8},{10,9... | collective-permute-start | bytes 294920 | tf_op jit(solution)/shard_map/ppermute | solution.py:492
  102.6 2.3 %collective-permute-done.4.west_in.refs_1_ = bf16[2,192,128]{2,1,0:T(8,128)(2,1)S(1)} collective-permute-done((bf16[2,192,128]{2,1,0:T(8,128)(2,1)S(1)}, bf16[2,192,128]{2,1,0:T(8,128)(2,1)S(1)}, u32[]{:S(2)}, u32[]{:S(2)}) %collective-permute-start.4) | collective-permute-done | bytes 98336 | tf_op jit(solution)/shard_map/ppermute | solution.py:492
  104.9 0.2 rows.3
  105.1 1.2 collective-permute-start.6
  106.3 1.8 %collective-permute-start.7 = (bf16[4,192,128]{2,1,0:T(8,128)(2,1)S(1)}, bf16[4,192,128]{2,1,0:T(8,128)(2,1)S(1)}, u32[]{:S(2)}, u32[]{:S(2)}) collective-permute-start(bf16[4,192,128]{2,1,0:T(8,128)(2,1)S(1)} %get-tuple-element.70), channel_id=1, source_target_pairs={{0,24},{8,0},{16,8},{24,16},{1,25},{9,1},{17,9},{25,17},{2,26},{10... | collective-permute-start | bytes 589832 | tf_op jit(solution)/shard_map/ppermute | solution.py:492
  108.1 4.9 %collective-permute-done.6.refs_3_ = bf16[4,192,128]{2,1,0:T(8,128)(2,1)S(1)} collective-permute-done((bf16[4,192,128]{2,1,0:T(8,128)(2,1)S(1)}, bf16[4,192,128]{2,1,0:T(8,128)(2,1)S(1)}, u32[]{:S(2)}, u32[]{:S(2)}) %collective-permute-start.6) | collective-permute-done | bytes 196640 | tf_op jit(solution)/shard_map/ppermute | solution.py:492
  113.0 1.2 collective-permute-done.7.refs_4_
  114.3 21.7 %block_head.1 = f32[128,64,128]{2,1,0:T(8,128)} custom-call(bf16[64,192,128]{2,1,0:T(8,128)(2,1)S(1)} %get-tuple-element.64.refs_0_, bf16[2,192,128]{2,1,0:T(8,128)(2,1)S(1)} %collective-permute-done.4.west_in.refs_1_, bf16[2,192,128]{2,1,0:T(8,128)(2,1)S(1)} %collective-permute-done.5.east_in.refs_2_, ...), custom_call_target="tpu_custom_call" | custom-call | flops 5888802816 | bytes 31457280 | tf_op jit(solution)/shard_map/block_head/pallas_call | solution.py:426
  (61 shorter events, 1.2 us)
Async XLA Ops:
  4.7 7.4 %copy-start.11 = (f32[2,192]{1,0:T(2,128)S(1)}, f32[2,192]{1,0:T(2,128)}, u32[]{:S(2)}) copy-start(f32[2,192]{1,0:T(2,128)} %param.32) | copy-start | bytes 4612
  4.7 7.4 %copy-start.12 = (f32[2,192]{1,0:T(2,128)S(1)}, f32[2,192]{1,0:T(2,128)}, u32[]{:S(2)}) copy-start(f32[2,192]{1,0:T(2,128)} %param.31) | copy-start | bytes 4612
  4.7 7.5 %copy-start.13 = (f32[2,192]{1,0:T(2,128)S(1)}, f32[2,192]{1,0:T(2,128)}, u32[]{:S(2)}) copy-start(f32[2,192]{1,0:T(2,128)} %param.27) | copy-start | bytes 4612
  4.7 7.5 %copy-start.14 = (f32[2,192]{1,0:T(2,128)S(1)}, f32[2,192]{1,0:T(2,128)}, u32[]{:S(2)}) copy-start(f32[2,192]{1,0:T(2,128)} %param.26) | copy-start | bytes 4612
  4.7 7.5 %copy-start.15 = (f32[2,192]{1,0:T(2,128)S(1)}, f32[2,192]{1,0:T(2,128)}, u32[]{:S(2)}) copy-start(f32[2,192]{1,0:T(2,128)} %param.25) | copy-start | bytes 4612
  4.8 7.5 %copy-start.9 = (s32[64,128]{1,0:T(8,128)S(1)}, s32[64,128]{1,0:T(8,128)}, u32[]{:S(2)}) copy-start(s32[64,128]{1,0:T(8,128)} %param.21) | copy-start | bytes 98308
  4.8 8.0 %copy-start.8 = (bf16[192,128]{1,0:T(8,128)(2,1)S(1)}, bf16[192,128]{1,0:T(8,128)(2,1)}, u32[]{:S(2)}) copy-start(bf16[192,128]{1,0:T(8,128)(2,1)} %param.33) | copy-start | bytes 147460
  4.8 8.1 %copy-start.10 = (f32[2,768]{1,0:T(2,128)S(1)}, f32[2,768]{1,0:T(2,128)}, u32[]{:S(2)}) copy-start(f32[2,768]{1,0:T(2,128)} %param.29) | copy-start | bytes 18436
  4.8 57.4 %all-to-all-start = ((bf16[32,4,64,128]{3,2,1,0:T(8,128)(2,1)}), bf16[32,4,64,128]{3,2,1,0:T(8,128)(2,1)S(1)}, u32[]{:S(2)}, u32[]{:S(2)}) async-start(bf16[32,4,64,128]{3,2,1,0:T(8,128)(2,1)} %bitcast.40), calls=%async_computation | async-start | bytes 4194304 | tf_op jit(solution)/shard_map/all_to_all | solution.py:461
  12.1 3.3 %copy-start.16 = (f32[192]{0:T(256)S(1)}, f32[192]{0:T(256)}, u32[]{:S(2)}) copy-start(f32[192]{0:T(256)} %param.23) | copy-start | bytes 2308
  13.9 5.4 %copy-start.7 = (f32[2,192,7,7]{1,0,3,2:T(2,128)S(1)}, f32[2,192,7,7]{1,0,3,2:T(2,128)}, u32[]{:S(2)}) copy-start(f32[2,192,7,7]{1,0,3,2:T(2,128)} %param.24) | copy-start | bytes 225796
  15.3 4.6 %copy-start.3 = (s32[1,336]{1,0:T(1,128)S(1)}, s32[1,336]{1,0:T(1,128)}, u32[]{:S(2)}) copy-start(s32[1,336]{1,0:T(1,128)} %constant.20.clone.row_ref) | copy-start | bytes 4036
  15.3 4.6 %copy-start.4 = (s32[1,336]{1,0:T(1,128)S(1)}, s32[1,336]{1,0:T(1,128)}, u32[]{:S(2)}) copy-start(s32[1,336]{1,0:T(1,128)} %constant.19.clone.col_ref) | copy-start | bytes 4036
  26.4 3.7 %copy-start.1 = (bf16[192,64,336]{2,1,0:T(8,128)(2,1)}, bf16[192,64,336]{2,1,0:T(8,128)(2,1)S(1)}, u32[]{:S(2)}) copy-start(bf16[192,64,336]{2,1,0:T(8,128)(2,1)S(1)} %bands.2.refs_5_) | copy-start | bytes 24772612
  30.1 32.1 %copy-start.2 = (bf16[128,192]{0,1:T(8,128)(2,1)S(1)}, bf16[128,192]{0,1:T(8,128)(2,1)}, u32[]{:S(2)}) copy-start(bf16[128,192]{0,1:T(8,128)(2,1)} %param.22) | copy-start | bytes 147460
  36.6 3.6 %copy-start = (bf16[192,64,336]{2,1,0:T(8,128)(2,1)}, bf16[192,64,336]{2,1,0:T(8,128)(2,1)S(1)}, u32[]{:S(2)}) copy-start(bf16[192,64,336]{2,1,0:T(8,128)(2,1)S(1)} %bands.3.refs_5_) | copy-start | bytes 24772612
  62.2 5.7 %copy-start.5 = (bf16[2,768,208]{2,1,0:T(8,128)(2,1)S(1)}, bf16[2,768,208]{2,1,0:T(8,128)(2,1)}, u32[]{:S(2)}) copy-start(bf16[2,768,208]{2,1,0:T(8,128)(2,1)} %fusion.1) | copy-start | bytes 1916932
  62.2 11.1 %copy-start.6 = (bf16[2,768,192]{1,2,0:T(8,128)(2,1)S(1)}, bf16[2,768,192]{1,2,0:T(8,128)(2,1)}, u32[]{:S(2)}) copy-start(bf16[2,768,192]{1,2,0:T(8,128)(2,1)} %param.30) | copy-start | bytes 1769476
  64.3 5.9 %collective-permute-start = (bf16[2,192,128]{2,1,0:T(8,128)(2,1)S(1)}, bf16[2,192,128]{2,1,0:T(8,128)(2,1)S(1)}, u32[]{:S(2)}, u32[]{:S(2)}) collective-permute-start(bf16[2,192,128]{2,1,0:T(8,128)(2,1)S(1)} %get-tuple-element.53), channel_id=1, source_target_pairs={{0,1},{1,2},{2,3},{3,4},{4,5},{5,6},{6,7},{7,0},{8,9},{9,10},{10,1... | collective-permute-start | bytes 294920 | tf_op jit(solution)/shard_map/ppermute | solution.py:492
  64.4 5.8 %collective-permute-start.1 = (bf16[2,192,128]{2,1,0:T(8,128)(2,1)S(1)}, bf16[2,192,128]{2,1,0:T(8,128)(2,1)S(1)}, u32[]{:S(2)}, u32[]{:S(2)}) collective-permute-start(bf16[2,192,128]{2,1,0:T(8,128)(2,1)S(1)} %get-tuple-element.54), channel_id=1, source_target_pairs={{0,7},{1,0},{2,1},{3,2},{4,3},{5,4},{6,5},{7,6},{8,15},{9,8},{10,9... | collective-permute-start | bytes 294920 | tf_op jit(solution)/shard_map/ppermute | solution.py:492
  70.4 7.8 %collective-permute-start.2 = (bf16[4,192,128]{2,1,0:T(8,128)(2,1)S(1)}, bf16[4,192,128]{2,1,0:T(8,128)(2,1)S(1)}, u32[]{:S(2)}, u32[]{:S(2)}) collective-permute-start(bf16[4,192,128]{2,1,0:T(8,128)(2,1)S(1)} %get-tuple-element.57), channel_id=1, source_target_pairs={{0,8},{8,16},{16,24},{24,0},{1,9},{9,17},{17,25},{25,1},{2,10},{10... | collective-permute-start | bytes 589832 | tf_op jit(solution)/shard_map/ppermute | solution.py:492
  70.8 9.3 %collective-permute-start.3 = (bf16[4,192,128]{2,1,0:T(8,128)(2,1)S(1)}, bf16[4,192,128]{2,1,0:T(8,128)(2,1)S(1)}, u32[]{:S(2)}, u32[]{:S(2)}) collective-permute-start(bf16[4,192,128]{2,1,0:T(8,128)(2,1)S(1)} %get-tuple-element.58), channel_id=1, source_target_pairs={{0,24},{8,0},{16,8},{24,16},{1,25},{9,1},{17,9},{25,17},{2,26},{10... | collective-permute-start | bytes 589832 | tf_op jit(solution)/shard_map/ppermute | solution.py:492
  99.0 5.9 %collective-permute-start.4 = (bf16[2,192,128]{2,1,0:T(8,128)(2,1)S(1)}, bf16[2,192,128]{2,1,0:T(8,128)(2,1)S(1)}, u32[]{:S(2)}, u32[]{:S(2)}) collective-permute-start(bf16[2,192,128]{2,1,0:T(8,128)(2,1)S(1)} %get-tuple-element.65), channel_id=1, source_target_pairs={{0,1},{1,2},{2,3},{3,4},{4,5},{5,6},{6,7},{7,0},{8,9},{9,10},{10,1... | collective-permute-start | bytes 294920 | tf_op jit(solution)/shard_map/ppermute | solution.py:492
  99.1 5.8 %collective-permute-start.5 = (bf16[2,192,128]{2,1,0:T(8,128)(2,1)S(1)}, bf16[2,192,128]{2,1,0:T(8,128)(2,1)S(1)}, u32[]{:S(2)}, u32[]{:S(2)}) collective-permute-start(bf16[2,192,128]{2,1,0:T(8,128)(2,1)S(1)} %get-tuple-element.66), channel_id=1, source_target_pairs={{0,7},{1,0},{2,1},{3,2},{4,3},{5,4},{6,5},{7,6},{8,15},{9,8},{10,9... | collective-permute-start | bytes 294920 | tf_op jit(solution)/shard_map/ppermute | solution.py:492
  105.1 7.9 %collective-permute-start.6 = (bf16[4,192,128]{2,1,0:T(8,128)(2,1)S(1)}, bf16[4,192,128]{2,1,0:T(8,128)(2,1)S(1)}, u32[]{:S(2)}, u32[]{:S(2)}) collective-permute-start(bf16[4,192,128]{2,1,0:T(8,128)(2,1)S(1)} %get-tuple-element.69), channel_id=1, source_target_pairs={{0,8},{8,16},{16,24},{24,0},{1,9},{9,17},{17,25},{25,1},{2,10},{10... | collective-permute-start | bytes 589832 | tf_op jit(solution)/shard_map/ppermute | solution.py:492
  106.3 8.0 %collective-permute-start.7 = (bf16[4,192,128]{2,1,0:T(8,128)(2,1)S(1)}, bf16[4,192,128]{2,1,0:T(8,128)(2,1)S(1)}, u32[]{:S(2)}, u32[]{:S(2)}) collective-permute-start(bf16[4,192,128]{2,1,0:T(8,128)(2,1)S(1)} %get-tuple-element.70), channel_id=1, source_target_pairs={{0,24},{8,0},{16,8},{24,16},{1,25},{9,1},{17,9},{25,17},{2,26},{10... | collective-permute-start | bytes 589832 | tf_op jit(solution)/shard_map/ppermute | solution.py:492

commit v4 on v3

--- a/solution.py
+++ b/solution.py
@@ -65,7 +65,7 @@
     return pltpu.roll(x, amount, 1) if amount else x
 
 
-def prep_body(q_ref, s_ref, o_ref):
+def prep_body(q_ref, before_ref, after_ref, s_ref, o_ref):
     channels, rows, cols = q_ref.shape
     tiles = cols // lanes
     span = rows // 2
@@ -75,39 +75,56 @@
     phase = (at >> 6) ^ (to >> 7)
     order = (row_index(shape) == 2 * (at & (half - 1)) + phase).astype(f32).astype(bf16)
     left = lane_index((span, lanes)) < half
-    every = (rows, s_ref.shape[1])
+    first = pl.program_id(0) * rows
+
+    def scale_of(c, start, count):
+        every = (count, s_ref.shape[1])
+        own = lane_index(every) == row_index(every) + start
+        return jnp.sum(jnp.where(own, s_ref[c : c + 1, :], 0.0), axis=1, keepdims=True)
+
+    beyond = [[] for _ in range(tiles)]
     for c in range(channels):
-        own = lane_index(every) == row_index(every) + pl.program_id(0) * rows
-        scale = jnp.sum(jnp.where(own, s_ref[c : c + 1, :], 0.0), axis=1, keepdims=True)
-        x = jnp.concatenate(
-            [
-                (q_ref[c, :, b * lanes : (b + 1) * lanes].astype(f32) * scale).astype(bf16)
-                for b in range(tiles)
-            ],
-            axis=0,
-        )
-        y = jnp.dot(x, order, preferred_element_type=f32)
+        scale = scale_of(c, first, rows)
+        scale_before = scale_of(c, first - 16, 16)
+        scale_after = scale_of(c, first + rows, 16)
+        parts = []
+        for ref, own in ((q_ref, scale), (before_ref, scale_before), (after_ref, scale_after)):
+            for b in range(tiles):
+                cut = slice(b * lanes, (b + 1) * lanes)
+                parts.append((ref[c, :, cut].astype(f32) * own).astype(bf16))
+        y = jnp.dot(jnp.concatenate(parts, axis=0), order, preferred_element_type=f32)
         for b in range(tiles):
             top = y[b * rows : b * rows + span]
             low = y[b * rows + span : (b + 1) * rows]
-            o_ref[0, b, c, 0:span] = jnp.where(left, top[:, :lanes], low[:, lanes:]).astype(bf16)
-            o_ref[0, b, c, span:rows] = jnp.where(left, top[:, lanes:], low[:, :lanes]).astype(bf16)
+            even = jnp.where(left, top[:, :lanes], low[:, lanes:])
+            odd = jnp.where(left, top[:, lanes:], low[:, :lanes])
+            o_ref[0, b, c * rows : c * rows + span] = even.astype(bf16)
+            o_ref[0, b, c * rows + span : (c + 1) * rows] = odd.astype(bf16)
+            before = tiles * rows + 16 * b
+            after = before + 16 * tiles
+            beyond[b] += [y[before + 13 : before + 16, :lanes], y[after : after + 3, :lanes]]
+    for b in range(tiles):
+        o_ref[0, b, channels * rows :] = jnp.concatenate(beyond[b], axis=0).astype(bf16)
 
 
 def prep(q_state, scales, n_lat, n_lon, rows):
     channels, n_rows, n_cols = q_state.shape
+    count = channels * (rows + 6)
+    step, last = rows // 16, n_rows // 16 - 1
     return pl.pallas_call(
         prep_body,
         grid=(n_lat,),
         in_specs=[
             pl.BlockSpec((channels, rows, n_cols), lambda a: (0, a, 0)),
+            pl.BlockSpec((channels, 16, n_cols), lambda a: (0, jnp.maximum(a * step - 1, 0), 0)),
+            pl.BlockSpec((channels, 16, n_cols), lambda a: (0, jnp.minimum(a * step + step, last), 0)),
             pl.BlockSpec((channels, n_rows), lambda a: (0, 0)),
         ],
-        out_specs=pl.BlockSpec((1, n_lon, channels, rows, lanes), lambda a: (a, 0, 0, 0, 0)),
-        out_shape=jax.ShapeDtypeStruct((n_lat, n_lon, channels, rows, lanes), bf16),
+        out_specs=pl.BlockSpec((1, n_lon, count, lanes), lambda a: (a, 0, 0, 0)),
+        out_shape=jax.ShapeDtypeStruct((n_lat, n_lon, count, lanes), bf16),
         name="dequantize",
         **params_for(60, 0, 4 * q_state.size),
-    )(q_state, scales).reshape(n_lat * n_lon, channels, rows, lanes)
+    )(q_state, q_state, q_state, scales).reshape(n_lat * n_lon, count, lanes)
 
 
 def slot_of(shape):
@@ -123,14 +140,18 @@
     return ((lane_index(shape) + 2) & 3) >= 2
 
 
-def messages(f_ref, e_ref, west_ref, east_ref, south_ref, north_ref):
-    shape = f_ref.shape[1:]
-    span = f_ref.shape[0] // 2
-    first = first_ends(shape)
+def ends_messages(e_ref, west_ref, east_ref):
+    first = first_ends(e_ref.shape[1:])
     for i in range(e_ref.shape[0] // 2):
         one, two = e_ref[2 * i], e_ref[2 * i + 1]
         west_ref[i] = jnp.where(first, one, turn(two, -2))
         east_ref[i] = jnp.where(first, turn(two, 2), one)
+
+
+def messages(f_ref, e_ref, west_ref, east_ref, south_ref, north_ref):
+    shape = f_ref.shape[1:]
+    span = f_ref.shape[0] // 2
+    ends_messages(e_ref, west_ref, east_ref)
     left = lane_index(shape) < half
     for i in range(3):
         r = span - 3 + i
@@ -147,59 +168,83 @@
     return groups
 
 
-def rows_body(west_in, east_in, south_in, north_in, south_ref, north_ref):
+def pack_beyond(north, south):
+    packed = jnp.zeros(north[0].shape, bf16)
+    for i, value in enumerate([*north, *south]):
+        packed = pack_edges(packed, value, i)
+    return packed
+
+
+def rows_body(west_in, east_in, north_in, south_in, west_ref, east_ref):
     count = west_in.shape[0]
-    groups = received_ends([west_in[i] for i in range(count)], [east_in[i] for i in range(count)])
-    slot = slot_of(groups[0].shape)
-    south_ref[0:3] = south_in[...]
-    north_ref[0:3] = north_in[...]
-    south_ref[3] = jnp.where(slot > 11, groups[count - 1], turn(groups[2 * count - 1], -32))
-    north_ref[3] = jnp.where(slot < 4, groups[0], turn(groups[count], 32))
-
-
-def rows_with_ends(from_west, from_east, to_south, to_north):
-    shape = jax.ShapeDtypeStruct((4, *to_south.shape[1:]), bf16)
+    packed = pack_beyond([north_in[i] for i in range(3)], [south_in[i] for i in range(3)])
+    west_ref[0:count] = west_in[...]
+    east_ref[0:count] = east_in[...]
+    west_ref[count] = packed
+    east_ref[count] = packed
+
+
+def with_rows(to_west, to_east, from_north, from_south):
+    shape = jax.ShapeDtypeStruct((to_west.shape[0] + 1, *to_west.shape[1:]), bf16)
     return pl.pallas_call(
         rows_body,
         out_shape=[shape, shape],
         name="rows",
-        **params_for(20, 0, 20 * to_south.size),
-    )(from_west, from_east, to_south, to_north)
-
-
-def stem_body(x_ref, w_ref, wide_ref, mask_ref, f_ref, west_ref, east_ref, south_ref, north_ref, e_ref):
+        **params_for(20, 0, 20 * to_west.size),
+    )(to_west, to_east, from_north, from_south)
+
+
+def stem_body(x_ref, w_ref, wide_ref, mask_ref, f_ref, west_ref, east_ref, north_ref, south_ref, e_ref):
     bias = wide_ref[4]
-    for g in range(x_ref.shape[1] // 16):
-        x = jnp.swapaxes(x_ref[:, 16 * g : 16 * g + 16, :], 0, 1)
+    senders, count = x_ref.shape[:2]
+    leads = f_ref.shape[0]
+    channels = count // (leads + 6)
+
+    def features(x, first, n):
+        x = jnp.swapaxes(x, 0, 1)
+        joined = jnp.concatenate([x[i] for i in range(n)], axis=1).astype(bf16)
+        y = jnp.dot(w_ref[...], joined, preferred_element_type=f32)
+        for i in range(n):
+            value = (y[:, i * lanes : (i + 1) * lanes] + bias) * mask_ref[first + i : first + i + 1, :]
+            yield i, value.astype(bf16)
+
+    for g in range(leads // 16):
         packed = jnp.zeros(f_ref.shape[1:], bf16)
-        for first in (0, 8):
-            joined = jnp.concatenate([x[first + i] for i in range(8)], axis=1)
-            y = jnp.dot(w_ref[...], joined, preferred_element_type=f32)
-            for i in range(8):
-                at = 16 * g + first + i
-                value = (y[:, i * lanes : (i + 1) * lanes] + bias) * mask_ref[at : at + 1, :]
-                value = value.astype(bf16)
-                f_ref[at] = value
-                packed = pack_edges(packed, value, first + i)
+        x = jnp.stack(
+            [x_ref[:, c * leads + 16 * g : c * leads + 16 * g + 16, :] for c in range(channels)], axis=1
+        )
+        for i, value in features(x.reshape(senders * channels, 16, lanes), 16 * g, 16):
+            f_ref[16 * g + i] = value
+            packed = pack_edges(packed, value, i)
         e_ref[g] = packed
-    messages(f_ref, e_ref, west_ref, east_ref, south_ref, north_ref)
-
-
-def feature_shapes(leads, d):
+    ends_messages(e_ref, west_ref, east_ref)
+    beyond = x_ref[:, channels * leads :, :].astype(f32)
+    x = jnp.stack([beyond[:, 6 * c : 6 * c + 6, :] for c in range(channels)], axis=1)
+    x = jnp.concatenate([x, jnp.zeros((senders, channels, 2, lanes), f32)], axis=2)
+    values = [v for _, v in features(x.reshape(senders * channels, 8, lanes), leads, 6)]
+    for i in range(3):
+        north_ref[i] = values[i]
+        south_ref[i] = values[3 + i]
+    packed = pack_beyond(values[:3], values[3:])
+    west_ref[leads // 32] = packed
+    east_ref[leads // 32] = packed
+
+
+def feature_shapes(leads, d, more=0):
     return [
-        jax.ShapeDtypeStruct((n, d, lanes), bf16) for n in (leads, leads // 32, leads // 32, 3, 3)
+        jax.ShapeDtypeStruct((n, d, lanes), bf16)
+        for n in (leads, leads // 32 + more, leads // 32 + more, 3, 3)
     ]
 
 
-def stem(state, weight_t, wide, mask):
+def stem(state, weight_t, wide, mask, leads):
     d = weight_t.shape[0]
-    leads = state.shape[1]
     return pl.pallas_call(
         stem_body,
-        out_shape=feature_shapes(leads, d),
+        out_shape=feature_shapes(leads, d, 1),
         scratch_shapes=[pltpu.VMEM((leads // 16, d, lanes), bf16)],
         name="stem",
-        **params_for(20, 2 * d * state.size, 2 * state.size + 2 * leads * d * lanes),
+        **params_for(24, 2 * d * state.size, 2 * state.size + 2 * leads * d * lanes),
     )(state, weight_t, wide, mask)
 
 
@@ -259,6 +304,7 @@
     small = (16, lanes)
     left = lane_index(small) < half
     place = lane_index(small) & (half - 1)
+    first = first_ends(small)
 
     def conv_step(g, _):
         cs = pl.ds(pl.multiple_of(g * 16, 16), 16)
@@ -272,8 +318,11 @@
         packs = received_ends(
             [west_in[i, cs, :] for i in range(count)], [east_in[i, cs, :] for i in range(count)]
         )
-        norths = [north_in[i, cs, :] * edge_ref[0] for i in range(4)]
-        souths = [south_in[i, cs, :] * edge_ref[1] for i in range(4)]
+        norths = [north_in[i, cs, :] * edge_ref[0] for i in range(3)]
+        souths = [south_in[i, cs, :] * edge_ref[1] for i in range(3)]
+        both = jnp.where(first, east_in[count, cs, :], west_in[count, cs, :])
+        before = [ends(both, i) * edge_ref[0] for i in range(3)]
+        after = [ends(both, 3 + i) * edge_ref[1] for i in range(3)]
         chunks = {}
         for k in range(leads // 16):
             x = jnp.stack([f_in[16 * k + q, cs, :] for q in range(16)])
@@ -291,7 +340,7 @@
                     xrow.append(turn(jnp.where(left, own, got), half))
                 slot = r % 16
                 mine = ends(packs[phase * per + r // 16], slot)
-                theirs = ends(norths[3], slot - 8 * phase)
+                theirs = turn(before[i], half if phase == 0 else 0)
                 hrow.append(turn(jnp.where(left, theirs, mine), half))
             for i in range(3):
                 own = f_in[phase * span + i, cs, :]
@@ -301,7 +350,7 @@
                 else:
                     xrow.append(jnp.where(left, turn(own, half), got))
                 mine = ends(packs[phase * per], i)
-                theirs = ends(souths[3], i + 8 * phase)
+                theirs = turn(after[i], 0 if phase == 0 else half)
                 hrow.append(turn(jnp.where(left, mine, theirs), half))
             xrow += [zero, zero]
             hrow += [zero, zero]
@@ -328,7 +377,7 @@
         sum_ref[1] += squares
         return 0
 
-    dwb, gain, lnb = (thin_ref.at[3 * index + i] for i in range(3))
+    dwb = thin_ref.at[index]
     sum_ref[...] = jnp.zeros_like(sum_ref)
 
     lax.fori_loop(0, d // 16, conv_step, 0)
@@ -351,13 +400,15 @@
             variance = sum_ref[1, cut, :] * (1.0 / d) - average * average
             scale = lax.rsqrt(jnp.maximum(variance, 0.0) + ln_eps)
             centered = conv_ref[:, cut, :] - (conv_ref[0, cut, :] + average)
-            both_normed = (centered * scale * gain[...] + lnb[...]).astype(bf16)
+            both_normed = (centered * scale).astype(bf16)
             both_normed = jnp.swapaxes(both_normed, 0, 1)
         normed = both_normed[8 * phase : 8 * phase + 8]
         joined = jnp.concatenate([normed[i] for i in range(8)], axis=1)
         joined = jnp.concatenate([joined, ones], axis=0)
         hidden = jnp.dot(w1_ref[...], joined, preferred_element_type=f32)
-        hidden = (hidden + hidden * lax.erf(hidden * 0.7071067811865476)).astype(bf16)
+        factor = lax.erf(hidden * 0.7071067811865476).astype(bf16)
+        hidden = hidden.astype(bf16)
+        hidden = hidden + hidden * factor
         projected = jnp.dot(w2_ref[...], hidden, preferred_element_type=f32)
         if not head:
             packed = jnp.zeros((d, lanes), bf16) if lead % 16 == 0 else e_ref[lead // 16]
@@ -459,46 +510,56 @@
 
     send = prep(q_state, scales, n_lat, n_lon, rows)
     state = lax.all_to_all(send, axes, split_axis=0, concat_axis=0, tiled=True)
-    state = state.reshape(-1, rows, lanes)
-
-    mask = land_mask.astype(f32).reshape(2, span, half, 2).transpose(3, 1, 0, 2)
-    mask = mask.reshape(rows, lanes)
+
+    def shift(x, axis, by):
+        n = lax.axis_size(axis)
+        return lax.ppermute(x, axis, [(i, (i + by) % n) for i in range(n)])
+
+    ocean = land_mask.astype(f32)
+    mask = ocean.reshape(2, span, half, 2).transpose(3, 1, 0, 2).reshape(rows, lanes)
+    beyond = jnp.concatenate(
+        [shift(ocean[rows - 3 :], "lat", 1), shift(ocean[:3], "lat", -1), ocean[:2]], axis=0
+    )
+    beyond = beyond.reshape(8, half, 2).transpose(0, 2, 1).reshape(8, lanes)
+    mask = jnp.concatenate([mask, beyond], axis=0)
     d = stem_weight.shape[1]
-    thin = jnp.stack([dw_bias, ln_gain, ln_bias], axis=1).reshape(6, d)
-    thin = jnp.broadcast_to(thin[:, :, None, None], (6, d, 1, lanes))
+    thin = jnp.broadcast_to(dw_bias[:, :, None, None], (2, d, 1, lanes))
     wide = jnp.stack([layer_scale * 0.5, layer_scale * b_out], axis=1).reshape(4, d)
     wide = jnp.concatenate([wide, stem_bias[None]], axis=0)
     wide = jnp.broadcast_to(wide[:, :, None], (5, d, lanes))
-    high = b_in.astype(bf16)
-    rest = b_in - high.astype(f32)
+    w_wide = w_in.astype(f32)
+    bias = b_in + jnp.sum(w_wide * ln_bias[:, :, None], axis=1)
+    w_scaled = (w_wide * ln_gain[:, :, None]).astype(bf16)
+    high = bias.astype(bf16)
+    rest = bias - high.astype(f32)
     mid = rest.astype(bf16)
     low = (rest - mid.astype(f32)).astype(bf16)
     terms = jnp.pad(jnp.stack([high, mid, low], axis=2), ((0, 0), (0, 0), (0, 13)))
-    w1 = jnp.concatenate([w_in.transpose(0, 2, 1), terms], axis=2)
+    w1 = jnp.concatenate([w_scaled.transpose(0, 2, 1), terms], axis=2)
     w2 = w_out.transpose(0, 2, 1)
+    mlp = [(w1[b], w2[b]) for b in range(2)]
     band_at = lax.axis_index("lat")
     edge = jnp.stack([band_at > 0, band_at < n_lat - 1]).astype(bf16)
     edge = jnp.broadcast_to(edge[:, None, None], (2, 16, lanes))
     dw_weight, ready = lax.optimization_barrier(
-        (dw_weight, (thin, wide, w1, w2, stem_weight.T, mask, edge, head_weight.T))
+        (dw_weight, (thin, wide, mlp, stem_weight.T, mask, edge, head_weight.T))
     )
     bands = [band(dw_weight[b], span) for b in range(2)]
-    state, bands, (thin, wide, w1, w2, weight_t, mask, edge, head_t) = lax.optimization_barrier(
+    state, bands, (thin, wide, mlp, weight_t, mask, edge, head_t) = lax.optimization_barrier(
         (state, bands, ready)
     )
 
-    def shift(x, axis, by):
-        n = lax.axis_size(axis)
-        return lax.ppermute(x, axis, [(i, (i + by) % n) for i in range(n)])
+    def columns(feat, to_west, to_east, north, south):
+        return feat, shift(to_east, "lon", 1), shift(to_west, "lon", -1), north, south
 
     def exchange(feat, to_west, to_east, to_south, to_north):
-        from_west, from_east = shift(to_east, "lon", 1), shift(to_west, "lon", -1)
-        to_south, to_north = rows_with_ends(from_west, from_east, to_south, to_north)
-        return feat, from_west, from_east, shift(to_south, "lat", 1), shift(to_north, "lat", -1)
-
-    feats = stem(state, weight_t, wide, mask)
-    feats = block(0, exchange(*feats), bands[0], (thin, wide, w1[0], w2[0], mask, edge))
-    return block(1, exchange(*feats), bands[1], (thin, wide, w1[1], w2[1], mask, edge), head_t)
+        north, south = shift(to_south, "lat", 1), shift(to_north, "lat", -1)
+        to_west, to_east = with_rows(to_west, to_east, north, south)
+        return columns(feat, to_west, to_east, north, south)
+
+    feats = columns(*stem(state, weight_t, wide, mask, rows))
+    feats = block(0, feats, bands[0], (thin, wide, *mlp[0], mask, edge))
+    return block(1, exchange(*feats), bands[1], (thin, wide, *mlp[1], mask, edge), head_t)
 
 
 def solution(mesh):

time: 137 us -> 132 us (0.964)
  waiting for transfers between devices: 39.4 us -> 23 us
  local copies, waits for them, and re-layouts: 12.6 us -> 22.5 us
  other arithmetic: 2.35 us -> 4.78 us
    all_to_all x1, waiting for transfers between devices: 22 us -> 8.83 us  [body(): state = lax.all_to_all(send, axes, split_axis=0, concat_axis=0, tiled=True)]
    another operation x4, local copies, waits for them, and re-layouts: 0.29 us -> 4.95 us  [band(): taps = jnp.pad(dw.reshape(d, 49), ((0, 0), (0, 15))).astype(bf16)]
    ppermute x8, waiting for transfers between devices: 17.4 us -> 14.2 us  [shift(): return lax.ppermute(x, axis, [(i, (i + by) % n) for i in range(n)])]
    squeeze x2, local copies, waits for them, and re-layouts: 0.09 us -> 2.63 us  [body(): mlp = [(w1[b], w2[b]) for b in range(2)]]
    transpose x0 -> x1, other arithmetic: none -> 2.29 us  [body(): w1 = jnp.concatenate([w_scaled.transpose(0, 2, 1), terms], axis=2)]
    pad x2, local copies, waits for them, and re-layouts: 0.03 us -> 1.62 us  [band(): taps = jnp.pad(dw.reshape(d, 49), ((0, 0), (0, 15))).astype(bf16)]
    unnamed x36 -> x40, local copies, waits for them, and re-layouts: 8.8 us -> 10.1 us
  transfers between devices with their start and end apart: 9 -> 9, of which waited for: 7 -> 6; matrix products, arithmetic and copies ran while one was open for 6% -> 15% of each run, Pallas kernels for 10% -> 10%
where the time goes in v4:
time: 132 us; the launch traced here: 131 us
  Pallas kernels  59.7 us (45%)
  waiting for transfers between devices  23 us (17%)
  local copies, waits for them, and re-layouts  22.5 us (17%)
  starting transfers between devices  20.4 us (15%)
  other arithmetic  4.78 us (4%)
    pallas_call x1, Pallas kernels, block(): pl.pallas_call(functools.partial(block_body, index, True), out_shape=jax....  21.2 us
    pallas_call x1, Pallas kernels, block(): pl.pallas_call(functools.partial(block_body, index, False), out_shape=fea...  18.1 us
    ppermute x8, waiting for transfers between devices, shift(): return lax.ppermute(x, axis, [(i, (i + by) % n) for i in range(n)])  14.2 us
    ppermute x8, starting transfers between devices, shift(): return lax.ppermute(x, axis, [(i, (i + by) % n) for i in range(n)])  13.1 us
    pallas_call x2, Pallas kernels, band(): pl.pallas_call(band_body, grid=(span // 8,), in_specs=[pl.BlockSpec((d, 6...  13 us
    unnamed x40, local copies, waits for them, and re-layouts  10.1 us
    all_to_all x1, waiting for transfers between devices, body(): state = lax.all_to_all(send, axes, split_axis=0, concat_axis=0, tiled=True)  8.83 us
    all_to_all x1, starting transfers between devices, body(): state = lax.all_to_all(send, axes, split_axis=0, concat_axis=0, tiled=True)  7.3 us
  transfers between devices with their start and end apart: 9, of which 6 were waited for; matrix products, arithmetic and copies ran while one was open for 15% of the time, Pallas kernels for 10%

profile of v4, /device:TPU:0, one launch (start us, length us, event | category | flops | bytes accessed | tf_op | source)
XLA Modules:
  0.0 131.0 jit_solution(4062397148220014535)
XLA Ops:
  0.0 5.3 %dequantize.1 = bf16[4,8,280,128]{3,2,1,0:T(8,128)(2,1)} custom-call(bf16[4,256,1024]{2,1,0:T(8,128)(2,1)} %after_ref.1, bf16[4,256,1024]{2,1,0:T(8,128)(2,1)} %after_ref.1, bf16[4,256,1024]{2,1,0:T(8,128)(2,1)} %after_ref.1, f32[4,256]{1,0:T(4,128)} %s_ref.1), custom_call_target="tpu_custom_call" | custom-call | bytes 4194304 | tf_op jit(solution)/shard_map/dequantize/pallas_call | solution.py:114
  5.3 7.3 %all-to-all-start = ((bf16[32,280,128]{2,1,0:T(8,128)(2,1)}), bf16[32,280,128]{2,1,0:T(8,128)(2,1)S(1)}, u32[]{:S(2)}, u32[]{:S(2)}) async-start(bf16[32,280,128]{2,1,0:T(8,128)(2,1)} %bitcast.39), calls=%async_computation | async-start | bytes 4587520 | tf_op jit(solution)/shard_map/all_to_all | solution.py:512
  12.7 1.8 %collective-permute-start = (f32[3,128]{1,0:T(4,128)S(1)}, f32[3,128]{1,0:T(4,128)S(1)}, u32[]{:S(2)}, u32[]{:S(2)}) collective-permute-start(f32[3,128]{1,0:T(4,128)S(1)} %get-tuple-element.85), channel_id=1, source_target_pairs={{0,8},{8,16},{16,24},{24,0},{1,9},{9,17},{17,25},{25,1},{2,10},{10... | collective-permute-start | bytes 4616 | tf_op jit(solution)/shard_map/ppermute | solution.py:516
  14.5 1.2 collective-permute-start.1
  15.7 1.2 copy.63
  16.9 2.3 %fusion.4 = (bf16[2,768,192]{2,1,0:T(8,128)(2,1)}, f32[2,768]{1,0:T(2,128)S(1)}) fusion(bf16[2,192,768]{1,2,0:T(8,128)(2,1)} %copy.63, f32[2,192]{1,0:T(2,128)S(1)} %copy-done.13, f32[2,192]{1,0:T(2,128)S(1)} %copy-done.14), kind=kLoop, calls=%fused_computation.7 | loop fusion | flops 1473024 | bytes 1188864 | tf_op jit(solution)/shard_map/transpose | solution.py:538
  19.6 1.4 %fusion.3 = bf16[2,768,208]{2,1,0:T(8,128)(2,1)S(1)} fusion(bf16[2,768,3]{2,1,0:T(8,128)(2,1)S(1)} %copy.64, bf16[2,768,192]{2,1,0:T(8,128)(2,1)} %get-tuple-element.81), kind=kLoop, calls=%fused_computation.6 | loop fusion | flops 1916928 | bytes 1238016 | tf_op jit(solution)/shard_map/concatenate | solution.py:538
  21.0 1.8 %slice_bitcast_fusion.2 = (bf16[192,768]{1,0:T(8,128)(2,1)S(1)}, bf16[192,768]{1,0:T(8,128)(2,1)}) fusion(bf16[2,192,768]{2,1,0:T(8,128)(2,1)} %bitcast.40), kind=kLoop, calls=%fused_computation.10 | loop fusion | bytes 1179648 | tf_op jit(solution)/shard_map/squeeze | solution.py:540
  24.9 2.9 %collective-permute-done = f32[3,128]{1,0:T(4,128)S(1)} collective-permute-done((f32[3,128]{1,0:T(4,128)S(1)}, f32[3,128]{1,0:T(4,128)S(1)}, u32[]{:S(2)}, u32[]{:S(2)}) %collective-permute-start) | collective-permute-done | bytes 1568 | tf_op jit(solution)/shard_map/ppermute | solution.py:516
  28.2 1.2 broadcast_in_dim.8.refs_6_
  29.6 0.9 convert.10
  31.3 1.4 %reshape_squeeze.9 = bf16[192,49]{0,1:T(8,128)(2,1)} reshape(bf16[192,7,7]{0,2,1:T(8,128)(2,1)} %get-tuple-element.77) | data formatting | bytes 37632 | tf_op jit(solution)/shard_map/reshape;squeeze | solution.py:269
  32.7 1.5 %copy.71 = bf16[192,49]{1,0:T(8,128)(2,1)} copy(bf16[192,49]{0,1:T(8,128)(2,1)} %reshape_squeeze.9) | data formatting | bytes 37632 | tf_op jit(solution)/shard_map/reshape;squeeze | solution.py:269
  34.8 1.5 %copy.70 = bf16[192,49]{1,0:T(8,128)(2,1)} copy(bf16[192,49]{0,1:T(8,128)(2,1)} %reshape_squeeze.8) | data formatting | bytes 37632 | tf_op jit(solution)/shard_map/reshape;squeeze | solution.py:269
  36.3 0.8 pad.15.w_ref
  37.1 0.8 pad.14.w_ref
  37.9 6.5 %bands.2.refs_5_ = bf16[192,64,336]{2,1,0:T(8,128)(2,1)S(1)} custom-call(bf16[192,64]{1,0:T(8,128)(2,1)S(1)} %pad.14.w_ref, s32[1,336]{1,0:T(1,128)S(1)} %copy-done.8, s32[1,336]{1,0:T(1,128)S(1)} %copy-done.7), custom_call_target="tpu_custom_call" | custom-call | bytes 8257536 | tf_op jit(solution)/shard_map/bands/pallas_call | solution.py:270
  44.5 3.6 %copy-done.1 = bf16[192,64,336]{2,1,0:T(8,128)(2,1)} copy-done((bf16[192,64,336]{2,1,0:T(8,128)(2,1)}, bf16[192,64,336]{2,1,0:T(8,128)(2,1)S(1)}, u32[]{:S(2)}) %copy-start.1) | copy-done | bytes 8257560
  48.1 6.5 %bands.3.refs_5_ = bf16[192,64,336]{2,1,0:T(8,128)(2,1)S(1)} custom-call(bf16[192,64]{1,0:T(8,128)(2,1)S(1)} %pad.15.w_ref, s32[1,336]{1,0:T(1,128)S(1)} %copy-done.8, s32[1,336]{1,0:T(1,128)S(1)} %copy-done.7), custom_call_target="tpu_custom_call" | custom-call | bytes 8257536 | tf_op jit(solution)/shard_map/bands/pallas_call | solution.py:270
  54.6 3.6 %copy-done = bf16[192,64,336]{2,1,0:T(8,128)(2,1)} copy-done((bf16[192,64,336]{2,1,0:T(8,128)(2,1)}, bf16[192,64,336]{2,1,0:T(8,128)(2,1)S(1)}, u32[]{:S(2)}) %copy-start) | copy-done | bytes 8257560
  58.2 8.8 %all-to-all-done.x_ref = bf16[32,280,128]{2,1,0:T(8,128)(2,1)S(1)} async-done(((bf16[32,280,128]{2,1,0:T(8,128)(2,1)}), bf16[32,280,128]{2,1,0:T(8,128)(2,1)S(1)}, u32[]{:S(2)}, u32[]{:S(2)}) %all-to-all-start) | async-done | bytes 2293792 | tf_op jit(solution)/shard_map/all_to_all | solution.py:512
  67.9 2.1 %stem.1 = (bf16[64,192,128]{2,1,0:T(8,128)(2,1)S(1)}, bf16[3,192,128]{2,1,0:T(8,128)(2,1)S(1)}, bf16[3,192,128]{2,1,0:T(8,128)(2,1)S(1)}, bf16[3,192,128]{2,1,0:T(8,128)(2,1)S(1)}, bf16[3,192,128]{2,1,0:T(8,128)(2,1)S(1)}) custom-call(bf16[32,280,128]{2,1,0:T(8,128)(2,1)S(1)} %all-to-all-done.x_ref, bf16[192,128]{1,0:T(8,128)(2,1)S(1)} %bitcast.38, ...), custom_call_target="tpu_custom_call" | custom-call | flops 440401920 | bytes 5439488 | tf_op jit(solution)/shard_map/stem/pallas_call | solution.py:242
  70.0 3.5 %collective-permute-start.3 = (bf16[3,192,128]{2,1,0:T(8,128)(2,1)S(1)}, bf16[3,192,128]{2,1,0:T(8,128)(2,1)S(1)}, u32[]{:S(2)}, u32[]{:S(2)}) collective-permute-start(bf16[3,192,128]{2,1,0:T(8,128)(2,1)S(1)} %get-tuple-element.58), channel_id=1, source_target_pairs={{0,7},{1,0},{2,1},{3,2},{4,3},{5,4},{6,5},{7,6},{8,15},{9,8},{10,9... | collective-permute-start | bytes 442376 | tf_op jit(solution)/shard_map/ppermute | solution.py:516
  73.5 2.8 %collective-permute-done.2.refs_1_ = bf16[3,192,128]{2,1,0:T(8,128)(2,1)S(1)} collective-permute-done((bf16[3,192,128]{2,1,0:T(8,128)(2,1)S(1)}, bf16[3,192,128]{2,1,0:T(8,128)(2,1)S(1)}, u32[]{:S(2)}, u32[]{:S(2)}) %collective-permute-start.2) | collective-permute-done | bytes 147488 | tf_op jit(solution)/shard_map/ppermute | solution.py:516
  76.4 18.1 %block.1 = (bf16[64,192,128]{2,1,0:T(8,128)(2,1)S(1)}, bf16[2,192,128]{2,1,0:T(8,128)(2,1)S(1)}, bf16[2,192,128]{2,1,0:T(8,128)(2,1)S(1)}, bf16[3,192,128]{2,1,0:T(8,128)(2,1)S(1)}, bf16[3,192,128]{2,1,0:T(8,128)(2,1)S(1)}) custom-call(bf16[64,192,128]{2,1,0:T(8,128)(2,1)S(1)} %get-tuple-element.56.refs_0_, ...), custom_call_target="tpu_custom_call" | custom-call | flops 5888802816 | bytes 31457280 | tf_op jit(solution)/shard_map/block/pallas_call | solution.py:467
  94.5 1.2 collective-permute-start.4
  95.7 1.8 %collective-permute-start.5 = (bf16[3,192,128]{2,1,0:T(8,128)(2,1)S(1)}, bf16[3,192,128]{2,1,0:T(8,128)(2,1)S(1)}, u32[]{:S(2)}, u32[]{:S(2)}) collective-permute-start(bf16[3,192,128]{2,1,0:T(8,128)(2,1)S(1)} %get-tuple-element.70), channel_id=1, source_target_pairs={{0,24},{8,0},{16,8},{24,16},{1,25},{9,1},{17,9},{25,17},{2,26},{10... | collective-permute-start | bytes 442376 | tf_op jit(solution)/shard_map/ppermute | solution.py:516
  97.4 3.4 %collective-permute-done.4.north_in.refs_3_ = bf16[3,192,128]{2,1,0:T(8,128)(2,1)S(1)} collective-permute-done((bf16[3,192,128]{2,1,0:T(8,128)(2,1)S(1)}, bf16[3,192,128]{2,1,0:T(8,128)(2,1)S(1)}, u32[]{:S(2)}, u32[]{:S(2)}) %collective-permute-start.4) | collective-permute-done | bytes 147488 | tf_op jit(solution)/shard_map/ppermute | solution.py:516
  100.9 2.2 %collective-permute-done.5.south_in.refs_4_ = bf16[3,192,128]{2,1,0:T(8,128)(2,1)S(1)} collective-permute-done((bf16[3,192,128]{2,1,0:T(8,128)(2,1)S(1)}, bf16[3,192,128]{2,1,0:T(8,128)(2,1)S(1)}, u32[]{:S(2)}, u32[]{:S(2)}) %collective-permute-start.5) | collective-permute-done | bytes 147488 | tf_op jit(solution)/shard_map/ppermute | solution.py:516
  103.3 3.5 %collective-permute-start.7 = (bf16[3,192,128]{2,1,0:T(8,128)(2,1)S(1)}, bf16[3,192,128]{2,1,0:T(8,128)(2,1)S(1)}, u32[]{:S(2)}, u32[]{:S(2)}) collective-permute-start(bf16[3,192,128]{2,1,0:T(8,128)(2,1)S(1)} %get-tuple-element.72), channel_id=1, source_target_pairs={{0,7},{1,0},{2,1},{3,2},{4,3},{5,4},{6,5},{7,6},{8,15},{9,8},{10,9... | collective-permute-start | bytes 442376 | tf_op jit(solution)/shard_map/ppermute | solution.py:516
  106.8 2.8 %collective-permute-done.6.refs_1_ = bf16[3,192,128]{2,1,0:T(8,128)(2,1)S(1)} collective-permute-done((bf16[3,192,128]{2,1,0:T(8,128)(2,1)S(1)}, bf16[3,192,128]{2,1,0:T(8,128)(2,1)S(1)}, u32[]{:S(2)}, u32[]{:S(2)}) %collective-permute-start.6) | collective-permute-done | bytes 147488 | tf_op jit(solution)/shard_map/ppermute | solution.py:516
  109.6 21.2 %block_head.1 = f32[128,64,128]{2,1,0:T(8,128)} custom-call(bf16[64,192,128]{2,1,0:T(8,128)(2,1)S(1)} %get-tuple-element.66.refs_0_, bf16[3,192,128]{2,1,0:T(8,128)(2,1)S(1)} %collective-permute-done.6.refs_1_, bf16[3,192,128]{2,1,0:T(8,128)(2,1)S(1)} %collective-permute-done.7.refs_2_, bf16[3,192,128]{2,1,0:T(8,128)(2,1)S(1)} %collective-permute-done.4.north_in.refs_3_, ...), custom_call_target="tpu_custom_call" | custom-call | flops 5888802816 | bytes 31457280 | tf_op jit(solution)/shard_map/block_head/pallas_call | solution.py:477
  (69 shorter events, 5.5 us)
Async XLA Ops:
  5.3 7.4 %copy-start.11 = (s32[64,128]{1,0:T(8,128)S(1)}, s32[64,128]{1,0:T(8,128)}, u32[]{:S(2)}) copy-start(s32[64,128]{1,0:T(8,128)} %param.21) | copy-start | bytes 98308
  5.3 10.4 %copy-start.16 = (f32[2,192]{1,0:T(2,128)S(1)}, f32[2,192]{1,0:T(2,128)}, u32[]{:S(2)}) copy-start(f32[2,192]{1,0:T(2,128)} %param.32) | copy-start | bytes 4612
  5.3 10.4 %copy-start.17 = (f32[2,192]{1,0:T(2,128)S(1)}, f32[2,192]{1,0:T(2,128)}, u32[]{:S(2)}) copy-start(f32[2,192]{1,0:T(2,128)} %param.31) | copy-start | bytes 4612
  5.3 10.4 %copy-start.9 = (bf16[2,192,768]{2,1,0:T(8,128)(2,1)S(1)}, bf16[2,192,768]{2,1,0:T(8,128)(2,1)}, u32[]{:S(2)}) copy-start(bf16[2,192,768]{2,1,0:T(8,128)(2,1)} %param.28) | copy-start | bytes 1769476
  5.3 11.6 %copy-start.13 = (f32[2,192]{1,0:T(2,128)S(1)}, f32[2,192]{1,0:T(2,128)}, u32[]{:S(2)}) copy-start(f32[2,192]{1,0:T(2,128)} %param.26) | copy-start | bytes 4612
  5.3 11.6 %copy-start.14 = (f32[2,192]{1,0:T(2,128)S(1)}, f32[2,192]{1,0:T(2,128)}, u32[]{:S(2)}) copy-start(f32[2,192]{1,0:T(2,128)} %param.27) | copy-start | bytes 4612
  5.3 61.7 %all-to-all-start = ((bf16[32,280,128]{2,1,0:T(8,128)(2,1)}), bf16[32,280,128]{2,1,0:T(8,128)(2,1)S(1)}, u32[]{:S(2)}, u32[]{:S(2)}) async-start(bf16[32,280,128]{2,1,0:T(8,128)(2,1)} %bitcast.39), calls=%async_computation | async-start | bytes 4587520 | tf_op jit(solution)/shard_map/all_to_all | solution.py:512
  12.7 6.6 %copy-start.12 = (f32[2,768]{1,0:T(2,128)S(1)}, f32[2,768]{1,0:T(2,128)}, u32[]{:S(2)}) copy-start(f32[2,768]{1,0:T(2,128)} %param.29) | copy-start | bytes 18436
  12.7 15.2 %collective-permute-start = (f32[3,128]{1,0:T(4,128)S(1)}, f32[3,128]{1,0:T(4,128)S(1)}, u32[]{:S(2)}, u32[]{:S(2)}) collective-permute-start(f32[3,128]{1,0:T(4,128)S(1)} %get-tuple-element.85), channel_id=1, source_target_pairs={{0,8},{8,16},{16,24},{24,0},{1,9},{9,17},{17,25},{25,1},{2,10},{10... | collective-permute-start | bytes 4616 | tf_op jit(solution)/shard_map/ppermute | solution.py:516
  14.5 13.4 %collective-permute-start.1 = (f32[3,128]{1,0:T(4,128)S(1)}, f32[3,128]{1,0:T(4,128)S(1)}, u32[]{:S(2)}, u32[]{:S(2)}) collective-permute-start(f32[3,128]{1,0:T(4,128)S(1)} %get-tuple-element.86), channel_id=1, source_target_pairs={{0,24},{8,0},{16,8},{24,16},{1,25},{9,1},{17,9},{25,17},{2,26},{10... | collective-permute-start | bytes 4616 | tf_op jit(solution)/shard_map/ppermute | solution.py:516
  15.7 3.8 %copy-start.18 = (f32[192]{0:T(256)S(1)}, f32[192]{0:T(256)}, u32[]{:S(2)}) copy-start(f32[192]{0:T(256)} %param.23) | copy-start | bytes 2308
  21.0 3.2 %copy-start.10 = (bf16[192,128]{1,0:T(8,128)(2,1)S(1)}, bf16[192,128]{1,0:T(8,128)(2,1)}, u32[]{:S(2)}) copy-start(bf16[192,128]{1,0:T(8,128)(2,1)} %param.33) | copy-start | bytes 147460
  21.0 7.2 %copy-start.15 = (f32[2,192]{1,0:T(2,128)S(1)}, f32[2,192]{1,0:T(2,128)}, u32[]{:S(2)}) copy-start(f32[2,192]{1,0:T(2,128)} %param.25) | copy-start | bytes 4612
  23.7 14.3 %copy-start.7 = (s32[1,336]{1,0:T(1,128)S(1)}, s32[1,336]{1,0:T(1,128)}, u32[]{:S(2)}) copy-start(s32[1,336]{1,0:T(1,128)} %constant.22.clone.row_ref) | copy-start | bytes 4036
  23.7 14.3 %copy-start.8 = (s32[1,336]{1,0:T(1,128)S(1)}, s32[1,336]{1,0:T(1,128)}, u32[]{:S(2)}) copy-start(s32[1,336]{1,0:T(1,128)} %constant.21.clone.col_ref) | copy-start | bytes 4036
  44.5 3.6 %copy-start.1 = (bf16[192,64,336]{2,1,0:T(8,128)(2,1)}, bf16[192,64,336]{2,1,0:T(8,128)(2,1)S(1)}, u32[]{:S(2)}) copy-start(bf16[192,64,336]{2,1,0:T(8,128)(2,1)S(1)} %bands.2.refs_5_) | copy-start | bytes 24772612
  54.6 3.7 %copy-start = (bf16[192,64,336]{2,1,0:T(8,128)(2,1)}, bf16[192,64,336]{2,1,0:T(8,128)(2,1)S(1)}, u32[]{:S(2)}) copy-start(bf16[192,64,336]{2,1,0:T(8,128)(2,1)S(1)} %bands.3.refs_5_) | copy-start | bytes 24772612
  67.0 0.8 copy-start.6
  67.8 8.5 %copy-start.2 = (bf16[768,208]{1,0:T(8,128)(2,1)S(1)}, bf16[768,208]{1,0:T(8,128)(2,1)}, u32[]{:S(2)}) copy-start(bf16[768,208]{1,0:T(8,128)(2,1)} %get-tuple-element.63.refs_8_) | copy-start | bytes 958468
  67.8 8.5 %copy-start.3 = (bf16[192,768]{1,0:T(8,128)(2,1)S(1)}, bf16[192,768]{1,0:T(8,128)(2,1)}, u32[]{:S(2)}) copy-start(bf16[192,768]{1,0:T(8,128)(2,1)} %get-tuple-element.64.refs_9_) | copy-start | bytes 884740
  67.9 8.5 %copy-start.4 = (f32[2,192,1,128]{3,2,1,0:T(1,128)S(1)}, f32[2,192,1,128]{3,2,1,0:T(1,128)}, u32[]{:S(2)}) copy-start(f32[2,192,1,128]{3,2,1,0:T(1,128)} %broadcast_in_dim.8.refs_6_) | copy-start | bytes 589828
  69.9 6.4 %collective-permute-start.2 = (bf16[3,192,128]{2,1,0:T(8,128)(2,1)S(1)}, bf16[3,192,128]{2,1,0:T(8,128)(2,1)S(1)}, u32[]{:S(2)}, u32[]{:S(2)}) collective-permute-start(bf16[3,192,128]{2,1,0:T(8,128)(2,1)S(1)} %get-tuple-element.57), channel_id=1, source_target_pairs={{0,1},{1,2},{2,3},{3,4},{4,5},{5,6},{6,7},{7,0},{8,9},{9,10},{10,1... | collective-permute-start | bytes 442376 | tf_op jit(solution)/shard_map/ppermute | solution.py:516
  70.0 6.4 %collective-permute-start.3 = (bf16[3,192,128]{2,1,0:T(8,128)(2,1)S(1)}, bf16[3,192,128]{2,1,0:T(8,128)(2,1)S(1)}, u32[]{:S(2)}, u32[]{:S(2)}) collective-permute-start(bf16[3,192,128]{2,1,0:T(8,128)(2,1)S(1)} %get-tuple-element.58), channel_id=1, source_target_pairs={{0,7},{1,0},{2,1},{3,2},{4,3},{5,4},{6,5},{7,6},{8,15},{9,8},{10,9... | collective-permute-start | bytes 442376 | tf_op jit(solution)/shard_map/ppermute | solution.py:516
  76.4 33.2 %copy-start.5 = (bf16[192,128]{0,1:T(8,128)(2,1)S(1)}, bf16[192,128]{0,1:T(8,128)(2,1)}, u32[]{:S(2)}) copy-start(bf16[192,128]{0,1:T(8,128)(2,1)} %copy.69) | copy-start | bytes 147460
  94.5 6.4 %collective-permute-start.4 = (bf16[3,192,128]{2,1,0:T(8,128)(2,1)S(1)}, bf16[3,192,128]{2,1,0:T(8,128)(2,1)S(1)}, u32[]{:S(2)}, u32[]{:S(2)}) collective-permute-start(bf16[3,192,128]{2,1,0:T(8,128)(2,1)S(1)} %get-tuple-element.69), channel_id=1, source_target_pairs={{0,8},{8,16},{16,24},{24,0},{1,9},{9,17},{17,25},{25,1},{2,10},{10... | collective-permute-start | bytes 442376 | tf_op jit(solution)/shard_map/ppermute | solution.py:516
  95.7 7.4 %collective-permute-start.5 = (bf16[3,192,128]{2,1,0:T(8,128)(2,1)S(1)}, bf16[3,192,128]{2,1,0:T(8,128)(2,1)S(1)}, u32[]{:S(2)}, u32[]{:S(2)}) collective-permute-start(bf16[3,192,128]{2,1,0:T(8,128)(2,1)S(1)} %get-tuple-element.70), channel_id=1, source_target_pairs={{0,24},{8,0},{16,8},{24,16},{1,25},{9,1},{17,9},{25,17},{2,26},{10... | collective-permute-start | bytes 442376 | tf_op jit(solution)/shard_map/ppermute | solution.py:516
  103.2 6.4 %collective-permute-start.6 = (bf16[3,192,128]{2,1,0:T(8,128)(2,1)S(1)}, bf16[3,192,128]{2,1,0:T(8,128)(2,1)S(1)}, u32[]{:S(2)}, u32[]{:S(2)}) collective-permute-start(bf16[3,192,128]{2,1,0:T(8,128)(2,1)S(1)} %get-tuple-element.71), channel_id=1, source_target_pairs={{0,1},{1,2},{2,3},{3,4},{4,5},{5,6},{6,7},{7,0},{8,9},{9,10},{10,1... | collective-permute-start | bytes 442376 | tf_op jit(solution)/shard_map/ppermute | solution.py:516
  103.3 6.4 %collective-permute-start.7 = (bf16[3,192,128]{2,1,0:T(8,128)(2,1)S(1)}, bf16[3,192,128]{2,1,0:T(8,128)(2,1)S(1)}, u32[]{:S(2)}, u32[]{:S(2)}) collective-permute-start(bf16[3,192,128]{2,1,0:T(8,128)(2,1)S(1)} %get-tuple-element.72), channel_id=1, source_target_pairs={{0,7},{1,0},{2,1},{3,2},{4,3},{5,4},{6,5},{7,6},{8,15},{9,8},{10,9... | collective-permute-start | bytes 442376 | tf_op jit(solution)/shard_map/ppermute | solution.py:516

commit v5 on v4

--- a/solution.py
+++ b/solution.py
@@ -377,7 +377,7 @@
         sum_ref[1] += squares
         return 0
 
-    dwb = thin_ref.at[index]
+    dwb, gain, lnb = (thin_ref.at[3 * index + i] for i in range(3))
     sum_ref[...] = jnp.zeros_like(sum_ref)
 
     lax.fori_loop(0, d // 16, conv_step, 0)
@@ -400,15 +400,13 @@
             variance = sum_ref[1, cut, :] * (1.0 / d) - average * average
             scale = lax.rsqrt(jnp.maximum(variance, 0.0) + ln_eps)
             centered = conv_ref[:, cut, :] - (conv_ref[0, cut, :] + average)
-            both_normed = (centered * scale).astype(bf16)
+            both_normed = (centered * scale * gain[...] + lnb[...]).astype(bf16)
             both_normed = jnp.swapaxes(both_normed, 0, 1)
         normed = both_normed[8 * phase : 8 * phase + 8]
         joined = jnp.concatenate([normed[i] for i in range(8)], axis=1)
         joined = jnp.concatenate([joined, ones], axis=0)
         hidden = jnp.dot(w1_ref[...], joined, preferred_element_type=f32)
-        factor = lax.erf(hidden * 0.7071067811865476).astype(bf16)
-        hidden = hidden.astype(bf16)
-        hidden = hidden + hidden * factor
+        hidden = (hidden + hidden * lax.erf(hidden * 0.7071067811865476)).astype(bf16)
         projected = jnp.dot(w2_ref[...], hidden, preferred_element_type=f32)
         if not head:
             packed = jnp.zeros((d, lanes), bf16) if lead % 16 == 0 else e_ref[lead // 16]
@@ -523,19 +521,18 @@
     beyond = beyond.reshape(8, half, 2).transpose(0, 2, 1).reshape(8, lanes)
     mask = jnp.concatenate([mask, beyond], axis=0)
     d = stem_weight.shape[1]
-    thin = jnp.broadcast_to(dw_bias[:, :, None, None], (2, d, 1, lanes))
+    thin = jnp.stack([dw_bias, ln_gain, ln_bias], axis=1).reshape(6, d)
+    thin = jnp.broadcast_to(thin[:, :, None, None], (6, d, 1, lanes))
     wide = jnp.stack([layer_scale * 0.5, layer_scale * b_out], axis=1).reshape(4, d)
     wide = jnp.concatenate([wide, stem_bias[None]], axis=0)
     wide = jnp.broadcast_to(wide[:, :, None], (5, d, lanes))
-    w_wide = w_in.astype(f32)
-    bias = b_in + jnp.sum(w_wide * ln_bias[:, :, None], axis=1)
-    w_scaled = (w_wide * ln_gain[:, :, None]).astype(bf16)
-    high = bias.astype(bf16)
-    rest = bias - high.astype(f32)
-    mid = rest.astype(bf16)
-    low = (rest - mid.astype(f32)).astype(bf16)
-    terms = jnp.pad(jnp.stack([high, mid, low], axis=2), ((0, 0), (0, 0), (0, 13)))
-    w1 = jnp.concatenate([w_scaled.transpose(0, 2, 1), terms], axis=2)
+    bias = b_in
+    high = lax.reduce_precision(bias, 8, 7)
+    mid = lax.reduce_precision(bias - high, 8, 7)
+    low = bias - high - mid
+    terms = jnp.stack([high, mid, low], axis=2).astype(bf16)
+    terms = jnp.pad(terms, ((0, 0), (0, 0), (0, 13)))
+    w1 = jnp.concatenate([w_in.transpose(0, 2, 1), terms], axis=2)
     w2 = w_out.transpose(0, 2, 1)
     mlp = [(w1[b], w2[b]) for b in range(2)]
     band_at = lax.axis_index("lat")

time: 132 us -> 133 us (level)
  Pallas kernels: 59.7 us -> 61.7 us
  waiting for transfers between devices: 23 us -> 24.9 us
  other arithmetic: 4.78 us -> 3.22 us
    ppermute x8, waiting for transfers between devices: 14.2 us -> 16.7 us  [shift(): return lax.ppermute(x, axis, [(i, (i + by) % n) for i in range(n)])]
    transpose x1 -> x0, other arithmetic: 2.29 us -> none  [body(): w1 = jnp.concatenate([w_scaled.transpose(0, 2, 1), terms], axis=2)]
    broadcast_in_dim x1 -> x2, local copies, waits for them, and re-layouts: 1.16 us -> 2.94 us  [body(): thin = jnp.broadcast_to(thin[:, :, None, None], (6, d, 1, lanes))]
    unnamed x40 -> x44, local copies, waits for them, and re-layouts: 10.1 us -> 8.79 us
  transfers between devices with their start and end apart: 9 -> 9, of which waited for: 6 -> 6; matrix products, arithmetic and copies ran while one was open for 15% -> 13% of each run, Pallas kernels for 10% -> 10%
where the time goes in v5:
time: 133 us; the launch traced here: 132 us
  Pallas kernels  61.7 us (46%)
  waiting for transfers between devices  24.9 us (19%)
  local copies, waits for them, and re-layouts  21.4 us (16%)
  starting transfers between devices  20.4 us (15%)
  other arithmetic  3.22 us (2%)
    pallas_call x1, Pallas kernels, block(): pl.pallas_call(functools.partial(block_body, index, True), out_shape=jax....  22 us
    pallas_call x1, Pallas kernels, block(): pl.pallas_call(functools.partial(block_body, index, False), out_shape=fea...  19.2 us
    ppermute x8, waiting for transfers between devices, shift(): return lax.ppermute(x, axis, [(i, (i + by) % n) for i in range(n)])  16.7 us
    ppermute x8, starting transfers between devices, shift(): return lax.ppermute(x, axis, [(i, (i + by) % n) for i in range(n)])  13.1 us
    pallas_call x2, Pallas kernels, band(): pl.pallas_call(band_body, grid=(span // 8,), in_specs=[pl.BlockSpec((d, 6...  13 us
    unnamed x44, local copies, waits for them, and re-layouts  8.79 us
    all_to_all x1, waiting for transfers between devices, body(): state = lax.all_to_all(send, axes, split_axis=0, concat_axis=0, tiled=True)  8.22 us
    all_to_all x1, starting transfers between devices, body(): state = lax.all_to_all(send, axes, split_axis=0, concat_axis=0, tiled=True)  7.3 us
  transfers between devices with their start and end apart: 9, of which 6 were waited for; matrix products, arithmetic and copies ran while one was open for 13% of the time, Pallas kernels for 10%

profile of v5, /device:TPU:0, one launch (start us, length us, event | category | flops | bytes accessed | tf_op | source)
XLA Modules:
  0.0 132.2 jit_solution(11932186874136764103)
XLA Ops:
  0.0 5.3 %dequantize.1 = bf16[4,8,280,128]{3,2,1,0:T(8,128)(2,1)} custom-call(bf16[4,256,1024]{2,1,0:T(8,128)(2,1)} %after_ref.1, bf16[4,256,1024]{2,1,0:T(8,128)(2,1)} %after_ref.1, bf16[4,256,1024]{2,1,0:T(8,128)(2,1)} %after_ref.1, f32[4,256]{1,0:T(4,128)} %s_ref.1), custom_call_target="tpu_custom_call" | custom-call | bytes 4194304 | tf_op jit(solution)/shard_map/dequantize/pallas_call | solution.py:114
  5.4 7.3 %all-to-all-start = ((bf16[32,280,128]{2,1,0:T(8,128)(2,1)}), bf16[32,280,128]{2,1,0:T(8,128)(2,1)S(1)}, u32[]{:S(2)}, u32[]{:S(2)}) async-start(bf16[32,280,128]{2,1,0:T(8,128)(2,1)} %bitcast.41), calls=%async_computation | async-start | bytes 4587520 | tf_op jit(solution)/shard_map/all_to_all | solution.py:510
  13.3 1.8 %collective-permute-start = (f32[3,128]{1,0:T(4,128)}, f32[3,128]{1,0:T(4,128)}, u32[]{:S(2)}, u32[]{:S(2)}) collective-permute-start(f32[3,128]{1,0:T(4,128)} %get-tuple-element.83), channel_id=1, source_target_pairs={{0,8},{8,16},{16,24},{24,0},{1,9},{9,17},{17,25},{25,1},{2,10},{10... | collective-permute-start | bytes 4616 | tf_op jit(solution)/shard_map/ppermute | solution.py:514
  15.1 1.2 collective-permute-start.1
  16.6 1.3 %copy.67 = bf16[2,192,768]{1,2,0:T(8,128)(2,1)S(1)} copy(bf16[2,192,768]{2,1,0:T(8,128)(2,1)} %param.28) | data formatting | bytes 1179648 | tf_op args[9]
  19.5 0.9 slice_bitcast_fusion.2
  20.4 0.9 slice_bitcast_fusion
  22.6 5.4 %collective-permute-done = f32[3,128]{1,0:T(4,128)} collective-permute-done((f32[3,128]{1,0:T(4,128)}, f32[3,128]{1,0:T(4,128)}, u32[]{:S(2)}, u32[]{:S(2)}) %collective-permute-start) | collective-permute-done | bytes 1568 | tf_op jit(solution)/shard_map/ppermute | solution.py:514
  28.0 0.7 pad_maximum_fusion.5
  29.2 2.3 %broadcast_in_dim.11.refs_6_ = f32[6,192,1,128]{3,2,1,0:T(1,128)S(1)} broadcast(f32[6,192]{1,0:T(8,128)} %broadcast_in_dim.10), dimensions={0,1} | broadcast | bytes 594432 | tf_op jit(solution)/shard_map/broadcast_in_dim | solution.py:525
  31.6 0.9 convert.25
  32.5 0.8 slice_reduce_fusion
  34.0 0.9 copy.75
  34.9 1.4 %reshape_squeeze.8 = bf16[192,49]{0,1:T(8,128)(2,1)} reshape(bf16[192,7,7]{0,2,1:T(8,128)(2,1)} %get-tuple-element.78) | data formatting | bytes 37632 | tf_op jit(solution)/shard_map/reshape;squeeze | solution.py:269
  36.2 1.5 %copy.74 = bf16[192,49]{1,0:T(8,128)(2,1)} copy(bf16[192,49]{0,1:T(8,128)(2,1)} %reshape_squeeze.8) | data formatting | bytes 37632 | tf_op jit(solution)/shard_map/reshape;squeeze | solution.py:269
  37.7 0.8 pad.14.w_ref
  38.6 6.5 %bands.2.refs_5_ = bf16[192,64,336]{2,1,0:T(8,128)(2,1)S(1)} custom-call(bf16[192,64]{1,0:T(8,128)(2,1)S(1)} %pad.14.w_ref, s32[1,336]{1,0:T(1,128)S(1)} %copy-done.8, s32[1,336]{1,0:T(1,128)S(1)} %copy-done.7), custom_call_target="tpu_custom_call" | custom-call | bytes 8257536 | tf_op jit(solution)/shard_map/bands/pallas_call | solution.py:270
  45.1 3.6 %copy-done.1 = bf16[192,64,336]{2,1,0:T(8,128)(2,1)} copy-done((bf16[192,64,336]{2,1,0:T(8,128)(2,1)}, bf16[192,64,336]{2,1,0:T(8,128)(2,1)S(1)}, u32[]{:S(2)}) %copy-start.1) | copy-done | bytes 8257560
  48.7 6.5 %bands.3.refs_5_ = bf16[192,64,336]{2,1,0:T(8,128)(2,1)S(1)} custom-call(bf16[192,64]{1,0:T(8,128)(2,1)S(1)} %pad.15.w_ref, s32[1,336]{1,0:T(1,128)S(1)} %copy-done.8, s32[1,336]{1,0:T(1,128)S(1)} %copy-done.7), custom_call_target="tpu_custom_call" | custom-call | bytes 8257536 | tf_op jit(solution)/shard_map/bands/pallas_call | solution.py:270
  55.2 3.6 %copy-done = bf16[192,64,336]{2,1,0:T(8,128)(2,1)} copy-done((bf16[192,64,336]{2,1,0:T(8,128)(2,1)}, bf16[192,64,336]{2,1,0:T(8,128)(2,1)S(1)}, u32[]{:S(2)}) %copy-start) | copy-done | bytes 8257560
  58.8 8.2 %all-to-all-done.x_ref = bf16[32,280,128]{2,1,0:T(8,128)(2,1)S(1)} async-done(((bf16[32,280,128]{2,1,0:T(8,128)(2,1)}), bf16[32,280,128]{2,1,0:T(8,128)(2,1)S(1)}, u32[]{:S(2)}, u32[]{:S(2)}) %all-to-all-start) | async-done | bytes 2293792 | tf_op jit(solution)/shard_map/all_to_all | solution.py:510
  67.1 2.1 %stem.1 = (bf16[64,192,128]{2,1,0:T(8,128)(2,1)S(1)}, bf16[3,192,128]{2,1,0:T(8,128)(2,1)S(1)}, bf16[3,192,128]{2,1,0:T(8,128)(2,1)S(1)}, bf16[3,192,128]{2,1,0:T(8,128)(2,1)S(1)}, bf16[3,192,128]{2,1,0:T(8,128)(2,1)S(1)}) custom-call(bf16[32,280,128]{2,1,0:T(8,128)(2,1)S(1)} %all-to-all-done.x_ref, bf16[192,128]{1,0:T(8,128)(2,1)S(1)} %bitcast.40, ...), custom_call_target="tpu_custom_call" | custom-call | flops 440401920 | bytes 5439488 | tf_op jit(solution)/shard_map/stem/pallas_call | solution.py:242
  69.2 3.5 %collective-permute-start.3 = (bf16[3,192,128]{2,1,0:T(8,128)(2,1)S(1)}, bf16[3,192,128]{2,1,0:T(8,128)(2,1)S(1)}, u32[]{:S(2)}, u32[]{:S(2)}) collective-permute-start(bf16[3,192,128]{2,1,0:T(8,128)(2,1)S(1)} %get-tuple-element.58), channel_id=1, source_target_pairs={{0,7},{1,0},{2,1},{3,2},{4,3},{5,4},{6,5},{7,6},{8,15},{9,8},{10,9... | collective-permute-start | bytes 442376 | tf_op jit(solution)/shard_map/ppermute | solution.py:514
  72.8 2.8 %collective-permute-done.2.refs_1_ = bf16[3,192,128]{2,1,0:T(8,128)(2,1)S(1)} collective-permute-done((bf16[3,192,128]{2,1,0:T(8,128)(2,1)S(1)}, bf16[3,192,128]{2,1,0:T(8,128)(2,1)S(1)}, u32[]{:S(2)}, u32[]{:S(2)}) %collective-permute-start.2) | collective-permute-done | bytes 147488 | tf_op jit(solution)/shard_map/ppermute | solution.py:514
  75.6 19.2 %block.1 = (bf16[64,192,128]{2,1,0:T(8,128)(2,1)S(1)}, bf16[2,192,128]{2,1,0:T(8,128)(2,1)S(1)}, bf16[2,192,128]{2,1,0:T(8,128)(2,1)S(1)}, bf16[3,192,128]{2,1,0:T(8,128)(2,1)S(1)}, bf16[3,192,128]{2,1,0:T(8,128)(2,1)S(1)}) custom-call(bf16[64,192,128]{2,1,0:T(8,128)(2,1)S(1)} %get-tuple-element.56.refs_0_, ...), custom_call_target="tpu_custom_call" | custom-call | flops 5888802816 | bytes 31457280 | tf_op jit(solution)/shard_map/block/pallas_call | solution.py:465
  94.9 1.2 collective-permute-start.4
  96.1 1.8 %collective-permute-start.5 = (bf16[3,192,128]{2,1,0:T(8,128)(2,1)S(1)}, bf16[3,192,128]{2,1,0:T(8,128)(2,1)S(1)}, u32[]{:S(2)}, u32[]{:S(2)}) collective-permute-start(bf16[3,192,128]{2,1,0:T(8,128)(2,1)S(1)} %get-tuple-element.70), channel_id=1, source_target_pairs={{0,24},{8,0},{16,8},{24,16},{1,25},{9,1},{17,9},{25,17},{2,26},{10... | collective-permute-start | bytes 442376 | tf_op jit(solution)/shard_map/ppermute | solution.py:514
  97.8 3.4 %collective-permute-done.4.north_in.refs_3_ = bf16[3,192,128]{2,1,0:T(8,128)(2,1)S(1)} collective-permute-done((bf16[3,192,128]{2,1,0:T(8,128)(2,1)S(1)}, bf16[3,192,128]{2,1,0:T(8,128)(2,1)S(1)}, u32[]{:S(2)}, u32[]{:S(2)}) %collective-permute-start.4) | collective-permute-done | bytes 147488 | tf_op jit(solution)/shard_map/ppermute | solution.py:514
  101.2 2.2 %collective-permute-done.5.south_in.refs_4_ = bf16[3,192,128]{2,1,0:T(8,128)(2,1)S(1)} collective-permute-done((bf16[3,192,128]{2,1,0:T(8,128)(2,1)S(1)}, bf16[3,192,128]{2,1,0:T(8,128)(2,1)S(1)}, u32[]{:S(2)}, u32[]{:S(2)}) %collective-permute-start.5) | collective-permute-done | bytes 147488 | tf_op jit(solution)/shard_map/ppermute | solution.py:514
  103.6 3.5 %collective-permute-start.7 = (bf16[3,192,128]{2,1,0:T(8,128)(2,1)S(1)}, bf16[3,192,128]{2,1,0:T(8,128)(2,1)S(1)}, u32[]{:S(2)}, u32[]{:S(2)}) collective-permute-start(bf16[3,192,128]{2,1,0:T(8,128)(2,1)S(1)} %get-tuple-element.72), channel_id=1, source_target_pairs={{0,7},{1,0},{2,1},{3,2},{4,3},{5,4},{6,5},{7,6},{8,15},{9,8},{10,9... | collective-permute-start | bytes 442376 | tf_op jit(solution)/shard_map/ppermute | solution.py:514
  107.2 2.8 %collective-permute-done.6.refs_1_ = bf16[3,192,128]{2,1,0:T(8,128)(2,1)S(1)} collective-permute-done((bf16[3,192,128]{2,1,0:T(8,128)(2,1)S(1)}, bf16[3,192,128]{2,1,0:T(8,128)(2,1)S(1)}, u32[]{:S(2)}, u32[]{:S(2)}) %collective-permute-start.6) | collective-permute-done | bytes 147488 | tf_op jit(solution)/shard_map/ppermute | solution.py:514
  110.0 22.0 %block_head.1 = f32[128,64,128]{2,1,0:T(8,128)} custom-call(bf16[64,192,128]{2,1,0:T(8,128)(2,1)S(1)} %get-tuple-element.66.refs_0_, bf16[3,192,128]{2,1,0:T(8,128)(2,1)S(1)} %collective-permute-done.6.refs_1_, bf16[3,192,128]{2,1,0:T(8,128)(2,1)S(1)} %collective-permute-done.7.refs_2_, bf16[3,192,128]{2,1,0:T(8,128)(2,1)S(1)} %collective-permute-done.4.north_in.refs_3_, ...), custom_call_target="tpu_custom_call" | custom-call | flops 5888802816 | bytes 31457280 | tf_op jit(solution)/shard_map/block_head/pallas_call | solution.py:475
  (75 shorter events, 5.2 us)
Async XLA Ops:
  5.3 7.4 %copy-start.12 = (s32[64,128]{1,0:T(8,128)S(1)}, s32[64,128]{1,0:T(8,128)}, u32[]{:S(2)}) copy-start(s32[64,128]{1,0:T(8,128)} %param.21) | copy-start | bytes 98308
  5.3 10.9 %copy-start.15 = (f32[2,192]{1,0:T(2,128)S(1)}, f32[2,192]{1,0:T(2,128)}, u32[]{:S(2)}) copy-start(f32[2,192]{1,0:T(2,128)} %param.32) | copy-start | bytes 4612
  5.3 10.9 %copy-start.16 = (f32[2,192]{1,0:T(2,128)S(1)}, f32[2,192]{1,0:T(2,128)}, u32[]{:S(2)}) copy-start(f32[2,192]{1,0:T(2,128)} %param.31) | copy-start | bytes 4612
  5.3 11.0 %copy-start.14 = (f32[2,768]{1,0:T(2,128)S(1)}, f32[2,768]{1,0:T(2,128)}, u32[]{:S(2)}) copy-start(f32[2,768]{1,0:T(2,128)} %param.29) | copy-start | bytes 18436
  5.3 12.7 %copy-start.17 = (f32[2,192]{1,0:T(2,128)S(1)}, f32[2,192]{1,0:T(2,128)}, u32[]{:S(2)}) copy-start(f32[2,192]{1,0:T(2,128)} %param.27) | copy-start | bytes 4612
  5.3 12.7 %copy-start.18 = (f32[2,192]{1,0:T(2,128)S(1)}, f32[2,192]{1,0:T(2,128)}, u32[]{:S(2)}) copy-start(f32[2,192]{1,0:T(2,128)} %param.26) | copy-start | bytes 4612
  5.3 12.7 %copy-start.19 = (f32[2,192]{1,0:T(2,128)S(1)}, f32[2,192]{1,0:T(2,128)}, u32[]{:S(2)}) copy-start(f32[2,192]{1,0:T(2,128)} %param.25) | copy-start | bytes 4612
  5.3 13.3 %copy-start.20 = (f32[192]{0:T(256)S(1)}, f32[192]{0:T(256)}, u32[]{:S(2)}) copy-start(f32[192]{0:T(256)} %param.23) | copy-start | bytes 2308
  5.4 61.7 %all-to-all-start = ((bf16[32,280,128]{2,1,0:T(8,128)(2,1)}), bf16[32,280,128]{2,1,0:T(8,128)(2,1)S(1)}, u32[]{:S(2)}, u32[]{:S(2)}) async-start(bf16[32,280,128]{2,1,0:T(8,128)(2,1)} %bitcast.41), calls=%async_computation | async-start | bytes 4587520 | tf_op jit(solution)/shard_map/all_to_all | solution.py:510
  13.3 14.7 %collective-permute-start = (f32[3,128]{1,0:T(4,128)}, f32[3,128]{1,0:T(4,128)}, u32[]{:S(2)}, u32[]{:S(2)}) collective-permute-start(f32[3,128]{1,0:T(4,128)} %get-tuple-element.83), channel_id=1, source_target_pairs={{0,8},{8,16},{16,24},{24,0},{1,9},{9,17},{17,25},{25,1},{2,10},{10... | collective-permute-start | bytes 4616 | tf_op jit(solution)/shard_map/ppermute | solution.py:514
  15.1 13.0 %collective-permute-start.1 = (f32[3,128]{1,0:T(4,128)}, f32[3,128]{1,0:T(4,128)}, u32[]{:S(2)}, u32[]{:S(2)}) collective-permute-start(f32[3,128]{1,0:T(4,128)} %get-tuple-element.84), channel_id=1, source_target_pairs={{0,24},{8,0},{16,8},{24,16},{1,25},{9,1},{17,9},{25,17},{2,26},{10... | collective-permute-start | bytes 4616 | tf_op jit(solution)/shard_map/ppermute | solution.py:514
  18.0 1.5 %copy-start.9 = (bf16[2,768,192]{1,2,0:T(8,128)(2,1)S(1)}, bf16[2,768,192]{1,2,0:T(8,128)(2,1)}, u32[]{:S(2)}) copy-start(bf16[2,768,192]{1,2,0:T(8,128)(2,1)} %param.30) | copy-start | bytes 1769476
  19.2 3.2 %copy-start.10 = (bf16[192,128]{1,0:T(8,128)(2,1)S(1)}, bf16[192,128]{1,0:T(8,128)(2,1)}, u32[]{:S(2)}) copy-start(bf16[192,128]{1,0:T(8,128)(2,1)} %param.33) | copy-start | bytes 147460
  19.5 2.0 %copy-start.13 = (f32[2,3,192]{2,0,1:T(2,128)S(1)}, f32[2,3,192]{2,0,1:T(2,128)}, u32[]{:S(2)}) copy-start(f32[2,3,192]{2,0,1:T(2,128)} %pad_maximum_fusion.3) | copy-start | bytes 13828
  19.5 9.6 %copy-start.11 = (f32[5,192]{1,0:T(8,128)S(1)}, f32[5,192]{1,0:T(8,128)}, u32[]{:S(2)}) copy-start(f32[5,192]{1,0:T(8,128)} %pad_maximum_fusion.2) | copy-start | bytes 11524
  20.4 18.2 %copy-start.7 = (s32[1,336]{1,0:T(1,128)S(1)}, s32[1,336]{1,0:T(1,128)}, u32[]{:S(2)}) copy-start(s32[1,336]{1,0:T(1,128)} %constant.20.clone.row_ref) | copy-start | bytes 4036
  20.4 18.2 %copy-start.8 = (s32[1,336]{1,0:T(1,128)S(1)}, s32[1,336]{1,0:T(1,128)}, u32[]{:S(2)}) copy-start(s32[1,336]{1,0:T(1,128)} %constant.19.clone.col_ref) | copy-start | bytes 4036
  45.1 3.6 %copy-start.1 = (bf16[192,64,336]{2,1,0:T(8,128)(2,1)}, bf16[192,64,336]{2,1,0:T(8,128)(2,1)S(1)}, u32[]{:S(2)}) copy-start(bf16[192,64,336]{2,1,0:T(8,128)(2,1)S(1)} %bands.2.refs_5_) | copy-start | bytes 24772612
  48.7 18.4 %copy-start.6 = (bf16[128,192]{0,1:T(8,128)(2,1)S(1)}, bf16[128,192]{0,1:T(8,128)(2,1)}, u32[]{:S(2)}) copy-start(bf16[128,192]{0,1:T(8,128)(2,1)} %param.22) | copy-start | bytes 147460
  55.2 3.7 %copy-start = (bf16[192,64,336]{2,1,0:T(8,128)(2,1)}, bf16[192,64,336]{2,1,0:T(8,128)(2,1)S(1)}, u32[]{:S(2)}) copy-start(bf16[192,64,336]{2,1,0:T(8,128)(2,1)S(1)} %bands.3.refs_5_) | copy-start | bytes 24772612
  67.1 8.5 %copy-start.3 = (bf16[768,208]{1,0:T(8,128)(2,1)S(1)}, bf16[768,208]{1,0:T(8,128)(2,1)}, u32[]{:S(2)}) copy-start(bf16[768,208]{1,0:T(8,128)(2,1)} %get-tuple-element.63.refs_8_) | copy-start | bytes 958468
  67.1 8.5 %copy-start.5 = (bf16[192,768]{1,0:T(8,128)(2,1)S(1)}, bf16[192,768]{1,0:T(8,128)(2,1)}, u32[]{:S(2)}) copy-start(bf16[192,768]{1,0:T(8,128)(2,1)} %get-tuple-element.64.refs_9_) | copy-start | bytes 884740
  69.2 6.4 %collective-permute-start.2 = (bf16[3,192,128]{2,1,0:T(8,128)(2,1)S(1)}, bf16[3,192,128]{2,1,0:T(8,128)(2,1)S(1)}, u32[]{:S(2)}, u32[]{:S(2)}) collective-permute-start(bf16[3,192,128]{2,1,0:T(8,128)(2,1)S(1)} %get-tuple-element.57), channel_id=1, source_target_pairs={{0,1},{1,2},{2,3},{3,4},{4,5},{5,6},{6,7},{7,0},{8,9},{9,10},{10,1... | collective-permute-start | bytes 442376 | tf_op jit(solution)/shard_map/ppermute | solution.py:514
  69.2 6.4 %collective-permute-start.3 = (bf16[3,192,128]{2,1,0:T(8,128)(2,1)S(1)}, bf16[3,192,128]{2,1,0:T(8,128)(2,1)S(1)}, u32[]{:S(2)}, u32[]{:S(2)}) collective-permute-start(bf16[3,192,128]{2,1,0:T(8,128)(2,1)S(1)} %get-tuple-element.58), channel_id=1, source_target_pairs={{0,7},{1,0},{2,1},{3,2},{4,3},{5,4},{6,5},{7,6},{8,15},{9,8},{10,9... | collective-permute-start | bytes 442376 | tf_op jit(solution)/shard_map/ppermute | solution.py:514
  75.6 34.4 %copy-start.2 = (bf16[768,208]{1,0:T(8,128)(2,1)S(1)}, bf16[768,208]{1,0:T(8,128)(2,1)}, u32[]{:S(2)}) copy-start(bf16[768,208]{1,0:T(8,128)(2,1)} %get-tuple-element.74.refs_8_) | copy-start | bytes 958468
  75.6 34.4 %copy-start.4 = (bf16[192,768]{1,0:T(8,128)(2,1)S(1)}, bf16[192,768]{1,0:T(8,128)(2,1)}, u32[]{:S(2)}) copy-start(bf16[192,768]{1,0:T(8,128)(2,1)} %get-tuple-element.75.refs_9_) | copy-start | bytes 884740
  94.9 6.4 %collective-permute-start.4 = (bf16[3,192,128]{2,1,0:T(8,128)(2,1)S(1)}, bf16[3,192,128]{2,1,0:T(8,128)(2,1)S(1)}, u32[]{:S(2)}, u32[]{:S(2)}) collective-permute-start(bf16[3,192,128]{2,1,0:T(8,128)(2,1)S(1)} %get-tuple-element.69), channel_id=1, source_target_pairs={{0,8},{8,16},{16,24},{24,0},{1,9},{9,17},{17,25},{25,1},{2,10},{10... | collective-permute-start | bytes 442376 | tf_op jit(solution)/shard_map/ppermute | solution.py:514
  96.1 7.4 %collective-permute-start.5 = (bf16[3,192,128]{2,1,0:T(8,128)(2,1)S(1)}, bf16[3,192,128]{2,1,0:T(8,128)(2,1)S(1)}, u32[]{:S(2)}, u32[]{:S(2)}) collective-permute-start(bf16[3,192,128]{2,1,0:T(8,128)(2,1)S(1)} %get-tuple-element.70), channel_id=1, source_target_pairs={{0,24},{8,0},{16,8},{24,16},{1,25},{9,1},{17,9},{25,17},{2,26},{10... | collective-permute-start | bytes 442376 | tf_op jit(solution)/shard_map/ppermute | solution.py:514
  103.6 6.4 %collective-permute-start.6 = (bf16[3,192,128]{2,1,0:T(8,128)(2,1)S(1)}, bf16[3,192,128]{2,1,0:T(8,128)(2,1)S(1)}, u32[]{:S(2)}, u32[]{:S(2)}) collective-permute-start(bf16[3,192,128]{2,1,0:T(8,128)(2,1)S(1)} %get-tuple-element.71), channel_id=1, source_target_pairs={{0,1},{1,2},{2,3},{3,4},{4,5},{5,6},{6,7},{7,0},{8,9},{9,10},{10,1... | collective-permute-start | bytes 442376 | tf_op jit(solution)/shard_map/ppermute | solution.py:514
  103.6 6.4 %collective-permute-start.7 = (bf16[3,192,128]{2,1,0:T(8,128)(2,1)S(1)}, bf16[3,192,128]{2,1,0:T(8,128)(2,1)S(1)}, u32[]{:S(2)}, u32[]{:S(2)}) collective-permute-start(bf16[3,192,128]{2,1,0:T(8,128)(2,1)S(1)} %get-tuple-element.72), channel_id=1, source_target_pairs={{0,7},{1,0},{2,1},{3,2},{4,3},{5,4},{6,5},{7,6},{8,15},{9,8},{10,9... | collective-permute-start | bytes 442376 | tf_op jit(solution)/shard_map/ppermute | solution.py:514
